TPU v7x, 512 devices: a whole 4x8x8 slice. The times are simulated.
512 devices in a mesh: lat: 16 (over y_hi, z), lon: 32 (over y_lo, x, core).
Axes of the slice: x: 4, y: 8 (y_hi: 2, y_lo: 4; y = y_hi * 4 + y_lo), z: 8, core: 2. Of those that a mesh axis runs over, the one named last changes fastest.
Arguments:
- state: bfloat16 [1, 512, 2048, 128], P(None, 'lat', 'lon'), may hold values from -6 to 6
- obs_members: bfloat16 [16, 32, 512, 128], P('lat', 'lon'), may hold values from -6 to 6
- obs_values: float32 [16, 32, 512], P('lat', 'lon'), may hold values from -6 to 6
- obs_precision: float32 [16, 32, 512], P('lat', 'lon'), may hold values from 0.5 to 500
- obs_cells: int32 [16, 32, 512], P('lat', 'lon'), may hold values from 0 to 2047
- obs_counts: int32 [16, 32], P('lat', 'lon'), may hold values from 85 to 512, as said below
Outputs:
- analysis: bfloat16 [1, 512, 2048, 128], P(None, 'lat', 'lon')
Inputs may be any that keep to these rules, and one draw needn't show every extreme that they name: `obs_counts`: exactly one tile uses all 512 slots; every other tile uses between 85 and 256 slots, and some other tile uses exactly 256.
All inputs are finite; a program needn't handle non-finite values.
Results may differ from a plain program's by a relative error of at most 0.0087.
Values may be sent and summed in bfloat16 or wider, within the bound.
No kernel may reach another device: no remote copies, remote signals or barrier semaphores. Data moves between devices by JAX's collectives and lax.ppermute only.
A program may use at most 64 MiB of HBM per device.

v0:
```python
import jax
import jax.numpy as jnp
from jax import lax
from jax.sharding import PartitionSpec as P

PATCH = 16
NS_STEPS = 12
RAD = 24


def with_halo(cells, sides, width):
    for axis, dim in sides:
        count = lax.axis_size(axis)
        head = lax.slice_in_dim(cells, 0, width, axis=dim)
        tail = lax.slice_in_dim(cells, cells.shape[dim] - width, cells.shape[dim], axis=dim)
        cells = jnp.concatenate(
            [
                lax.ppermute(tail, axis, [(i, (i + 1) % count) for i in range(count)]),
                cells,
                lax.ppermute(head, axis, [((i + 1) % count, i) for i in range(count)]),
            ],
            axis=dim,
        )
    return cells


def local_solve(members_near, scalars_near, tile_state, lat_here, lat_total):
    ensemble = members_near.shape[-1]
    levels, tile_rows, tile_cols, _ = tile_state.shape
    offsets = jnp.arange(3, dtype=jnp.int32) - 1
    lat_ok = ((lat_here + offsets >= 0) & (lat_here + offsets < lat_total)).astype(jnp.float32)
    values = scalars_near[:, :, 0, :].reshape(-1)
    weight = (scalars_near[:, :, 1, :] * lat_ok[:, None, None]).reshape(-1)
    obs_cells = scalars_near[:, :, 2, :].astype(jnp.int32)
    obs_rows = offsets[:, None, None] * tile_rows + obs_cells // tile_cols
    obs_cols = offsets[None, :, None] * tile_cols + obs_cells % tile_cols
    rows_twice = (2 * obs_rows + 1).reshape(-1)
    cols_twice = (2 * obs_cols + 1).reshape(-1)
    flattened = members_near.reshape(-1, ensemble)
    obs_mean = jnp.sum(flattened, axis=1, dtype=jnp.float32) / ensemble
    spread = (flattened.astype(jnp.float32) - obs_mean[:, None]).astype(jnp.bfloat16)
    innovation = values - obs_mean
    patch_cols = tile_cols // PATCH

    def patch_terms(patch_index):
        patch_row = patch_index // patch_cols
        patch_col = patch_index % patch_cols
        row_gap = rows_twice - (2 * patch_row * PATCH + PATCH)
        col_gap = cols_twice - (2 * patch_col * PATCH + PATCH)
        distance = row_gap * row_gap + col_gap * col_gap
        tapering = jnp.where(
            distance < 4 * RAD * RAD,
            jnp.exp(-distance.astype(jnp.float32) / (2.0 * RAD * RAD)),
            0.0,
        )
        local_weight = weight * tapering
        weighted = (local_weight[:, None] * spread.astype(jnp.float32)).astype(jnp.bfloat16)
        gram_part = lax.dot_general(
            weighted, spread, (((0,), (0,)), ((), ())), preferred_element_type=jnp.float32
        )
        pull_term = jnp.dot(
            innovation, weighted.astype(jnp.float32), precision=lax.Precision.HIGHEST
        )
        return (gram_part, pull_term)

    patches = tile_rows // PATCH * patch_cols
    grams, pulls = lax.map(patch_terms, jnp.arange(patches, dtype=jnp.int32))
    identity = jnp.eye(ensemble, dtype=jnp.float32)
    system = grams + (ensemble - 1.0) * identity
    trace_sum = jnp.trace(system, axis1=1, axis2=2)
    iterate = system / trace_sum[:, None, None]
    inverse_root = jnp.broadcast_to(identity, system.shape)
    for sweep_index in range(NS_STEPS):
        factor = 1.5 * identity - 0.5 * jnp.matmul(
            inverse_root, iterate, precision=lax.Precision.HIGHEST
        )
        iterate = jnp.matmul(iterate, factor, precision=lax.Precision.HIGHEST)
        inverse_root = jnp.matmul(factor, inverse_root, precision=lax.Precision.HIGHEST)
    spread_scale = jnp.sqrt((ensemble - 1.0) / trace_sum)
    inner = jnp.matmul(inverse_root, pulls[:, :, None], precision=lax.Precision.HIGHEST)
    mean_weights = (
        jnp.matmul(inverse_root, inner, precision=lax.Precision.HIGHEST)[:, :, 0]
        / trace_sum[:, None]
    )
    transform = (inverse_root * spread_scale[:, None, None] + mean_weights[:, :, None]).astype(
        jnp.bfloat16
    )
    state_mean = jnp.sum(tile_state, axis=-1, dtype=jnp.float32) / ensemble
    perturbation = (tile_state.astype(jnp.float32) - state_mean[..., None]).astype(jnp.bfloat16)
    blocks = perturbation.reshape(levels, tile_rows // PATCH, PATCH, patch_cols, PATCH, ensemble)
    matrices = transform.reshape(tile_rows // PATCH, patch_cols, ensemble, ensemble)
    updated = jnp.einsum(
        "lapbqk,abkj->lapbqj", blocks, matrices, preferred_element_type=jnp.float32
    )
    return (updated.reshape(levels, tile_rows, tile_cols, ensemble) + state_mean[..., None]).astype(
        jnp.bfloat16
    )


def spread_observations(members, scalars):
    members_near = with_halo(members, (("lat", 0), ("lon", 1)), 1)
    scalars_near = with_halo(scalars, (("lat", 0), ("lon", 1)), 1)
    return (members_near, scalars_near)


def body(state, obs_members, obs_values, obs_precision, obs_cells, obs_counts):
    capacity = obs_members.shape[2]
    slot_index = jnp.arange(capacity, dtype=jnp.int32)
    valid = (slot_index[None, None, :] < obs_counts[:, :, None]).astype(jnp.float32)
    scalars = jnp.stack([obs_values, obs_precision * valid, obs_cells.astype(jnp.float32)], axis=2)
    lat_here = lax.axis_index("lat")
    members_near, scalars_near = spread_observations(obs_members, scalars)
    return local_solve(members_near, scalars_near, state, lat_here, lax.axis_size("lat"))


def solution(mesh):
    in_specs = (
        P(None, "lat", "lon", None),
        P("lat", "lon", None, None),
        P("lat", "lon", None),
        P("lat", "lon", None),
        P("lat", "lon", None),
        P("lat", "lon"),
    )
    out_specs = P(None, "lat", "lon", None)
    return jax.shard_map(body, mesh=mesh, in_specs=in_specs, out_specs=out_specs, check_vma=False)
```

profile of v0, /device:TPU:31, one launch (start us, length us, event | category | flops | bytes accessed | tf_op | source)
XLA Modules:
  0.0 135.5 jit_solution(223347580811019223)
XLA Ops:
  2.8 4.0 %collective-permute-start = (f32[1,1,3,512]{3,2,1,0:T(4,128)S(1)}, f32[1,1,3,512]{3,2,1,0:T(4,128)S(1)}, u32[]{:S(2)}, u32[]{:S(2)}) collective-permute-start(f32[1,1,3,512]{3,2,1,0:T(4,128)S(1)} %pad_maximum_fusion.7), channel_id=1, source_target_pairs={{0,32},{32,64},{64,96},{96,128},{128,160},{160,192},{192,224},{224... | collective-permute-start | bytes 18440 | tf_op jit(solution)/shard_map/ppermute | solution.py:18
  6.8 11.2 %collective-permute-start.1 = (f32[1,1,3,512]{3,2,1,0:T(4,128)S(1)}, f32[1,1,3,512]{3,2,1,0:T(4,128)S(1)}, u32[]{:S(2)}, u32[]{:S(2)}) collective-permute-start(f32[1,1,3,512]{3,2,1,0:T(4,128)S(1)} %pad_maximum_fusion.7), channel_id=1, source_target_pairs={{32,0},{64,32},{96,64},{128,96},{160,128},{192,160},{224,192},{256... | collective-permute-start | bytes 18440 | tf_op jit(solution)/shard_map/ppermute | solution.py:20
  17.9 1.9 %collective-permute-start.4 = (bf16[1,1,512,128]{3,2,1,0:T(8,128)(2,1)}, bf16[1,1,512,128]{3,2,1,0:T(8,128)(2,1)S(1)}, u32[]{:S(2)}, u32[]{:S(2)}) collective-permute-start(bf16[1,1,512,128]{3,2,1,0:T(8,128)(2,1)} %param.9), channel_id=1, source_target_pairs={{0,32},{32,64},{64,96},{96,128},{128,160},{160,192},{192,224},{224... | collective-permute-start | bytes 393224 | tf_op jit(solution)/shard_map/ppermute | solution.py:18
  19.9 9.4 %collective-permute-start.5 = (bf16[1,1,512,128]{3,2,1,0:T(8,128)(2,1)}, bf16[1,1,512,128]{3,2,1,0:T(8,128)(2,1)S(1)}, u32[]{:S(2)}, u32[]{:S(2)}) collective-permute-start(bf16[1,1,512,128]{3,2,1,0:T(8,128)(2,1)} %param.9), channel_id=1, source_target_pairs={{32,0},{64,32},{96,64},{128,96},{160,128},{192,160},{224,192},{256... | collective-permute-start | bytes 393224 | tf_op jit(solution)/shard_map/ppermute | solution.py:20
  29.3 1.4 %convert_reduce_fusion = f32[32,64]{1,0:T(8,128)S(1)} fusion(bf16[1,32,64,128]{3,2,1,0:T(8,128)(2,1)} %param.8), kind=kLoop, calls=%fused_computation.13 | loop fusion | flops 522240 | bytes 532480 | tf_op jit(solution)/shard_map/reduce_sum | solution.py:88
  30.7 1.4 %fusion.19 = bf16[1,32,64,128]{3,2,1,0:T(8,128)(2,1)S(1)} fusion(bf16[1,32,64,128]{3,2,1,0:T(8,128)(2,1)} %param.8, f32[32,64]{1,0:T(8,128)S(1)} %broadcast_multiply_fusion.1), kind=kLoop, calls=%fused_computation.40 | loop fusion | flops 786432 | bytes 1056768 | tf_op jit(solution)/shard_map/convert_element_type | solution.py:89
  32.1 1.2 collective-permute-done.4
  34.4 6.0 %collective-permute-start.6 = (bf16[3,1,512,128]{3,2,1,0:T(8,128)(2,1)S(1)}, bf16[3,1,512,128]{3,2,1,0:T(8,128)(2,1)S(1)}, u32[]{:S(2)}, u32[]{:S(2)}) collective-permute-start(bf16[3,1,512,128]{3,2,1,0:T(8,128)(2,1)S(1)} %constant_dynamic-update-slice_fusion), channel_id=1, source_target_pairs={{0,1},{1,2},{2,3},{3,4},{4,5},{5,6},{6,7},{7,8},{8,9},{9,10},{10,1... | collective-permute-start | bytes 1179656 | tf_op jit(solution)/shard_map/ppermute | solution.py:18
  40.5 1.9 %collective-permute-start.7 = (bf16[3,1,512,128]{3,2,1,0:T(8,128)(2,1)S(1)}, bf16[3,1,512,128]{3,2,1,0:T(8,128)(2,1)S(1)}, u32[]{:S(2)}, u32[]{:S(2)}) collective-permute-start(bf16[3,1,512,128]{3,2,1,0:T(8,128)(2,1)S(1)} %constant_dynamic-update-slice_fusion), channel_id=1, source_target_pairs={{1,0},{2,1},{3,2},{4,3},{5,4},{6,5},{7,6},{8,7},{9,8},{10,9},{11,1... | collective-permute-start | bytes 1179656 | tf_op jit(solution)/shard_map/ppermute | solution.py:20
  42.4 7.5 %collective-permute-start.2 = (f32[3,1,3,512]{3,2,1,0:T(4,128)S(1)}, f32[3,1,3,512]{3,2,1,0:T(4,128)S(1)}, u32[]{:S(2)}, u32[]{:S(2)}) collective-permute-start(f32[3,1,3,512]{3,2,1,0:T(4,128)S(1)} %pad_maximum_fusion), channel_id=1, source_target_pairs={{0,1},{1,2},{2,3},{3,4},{4,5},{5,6},{6,7},{7,8},{8,9},{9,10},{10,1... | collective-permute-start | bytes 55304 | tf_op jit(solution)/shard_map/ppermute | solution.py:18
  50.0 1.9 %collective-permute-start.3 = (f32[3,1,3,512]{3,2,1,0:T(4,128)S(1)}, f32[3,1,3,512]{3,2,1,0:T(4,128)S(1)}, u32[]{:S(2)}, u32[]{:S(2)}) collective-permute-start(f32[3,1,3,512]{3,2,1,0:T(4,128)S(1)} %pad_maximum_fusion), channel_id=1, source_target_pairs={{1,0},{2,1},{3,2},{4,3},{5,4},{6,5},{7,6},{8,7},{9,8},{10,9},{11,1... | collective-permute-start | bytes 55304 | tf_op jit(solution)/shard_map/ppermute | solution.py:20
  52.2 6.8 %collective-permute-done.3 = f32[3,1,3,512]{3,2,1,0:T(4,128)S(1)} collective-permute-done((f32[3,1,3,512]{3,2,1,0:T(4,128)S(1)}, f32[3,1,3,512]{3,2,1,0:T(4,128)S(1)}, u32[]{:S(2)}, u32[]{:S(2)}) %collective-permute-start.3) | collective-permute-done | bytes 18464 | tf_op jit(solution)/shard_map/ppermute | solution.py:20
  60.0 2.0 %fusion.6 = bf16[4608,128]{1,0:T(8,128)(2,1)S(1)} fusion(f32[3,3,512,128]{3,2,1,0:T(8,128)S(1)} %maximum_convert_fusion, f32[4608]{0:T(1024)S(1)} %div.68), kind=kLoop, calls=%fused_computation.10 | loop fusion | flops 1179648 | bytes 3557376 | tf_op jit(solution)/shard_map/convert_element_type | solution.py:41
  62.0 46.3 %while.17 = (s32[]{:T(128)}, f32[8,128,128]{2,1,0:T(8,128)S(1)}, f32[8,128]{1,0:T(8,128)S(1)}, s32[8]{0:T(128)S(1)}, s32[4608]{0:T(1024)S(1)}, /*index=5*/s32[46...) while((s32[]{:T(128)}, f32[8,128,128]{2,1,0:T(8,128)S(1)}, ...), condition=%wide.wide.region_2.3_spmd.clone, body=%wide.wide.region_1.2_spmd.sunk.clone | while | flops 161662496 | bytes 3737444 | solution.py:67
  65.5 1.2 fusion.151
  66.7 1.1 fusion.152
  71.3 1.2 fusion.151
  77.1 1.2 fusion.151
  82.8 1.2 fusion.151
  88.6 1.2 fusion.151
  94.4 1.2 fusion.151
  100.1 1.2 fusion.151
  105.9 1.2 fusion.151
  134.3 1.1 add_convert_fusion
  (120 shorter events, 43.3 us)
Async XLA Ops:
  0.0 33.4 %copy-start = (bf16[1,1,512,128]{3,2,1,0:T(8,128)(2,1)S(1)}, bf16[1,1,512,128]{3,2,1,0:T(8,128)(2,1)}, u32[]{:S(2)}) copy-start(bf16[1,1,512,128]{3,2,1,0:T(8,128)(2,1)} %param.9) | copy-start | bytes 393220
  2.8 39.6 %collective-permute-start = (f32[1,1,3,512]{3,2,1,0:T(4,128)S(1)}, f32[1,1,3,512]{3,2,1,0:T(4,128)S(1)}, u32[]{:S(2)}, u32[]{:S(2)}) collective-permute-start(f32[1,1,3,512]{3,2,1,0:T(4,128)S(1)} %pad_maximum_fusion.7), channel_id=1, source_target_pairs={{0,32},{32,64},{64,96},{96,128},{128,160},{160,192},{192,224},{224... | collective-permute-start | bytes 18440 | tf_op jit(solution)/shard_map/ppermute | solution.py:18
  6.8 35.6 %collective-permute-start.1 = (f32[1,1,3,512]{3,2,1,0:T(4,128)S(1)}, f32[1,1,3,512]{3,2,1,0:T(4,128)S(1)}, u32[]{:S(2)}, u32[]{:S(2)}) collective-permute-start(f32[1,1,3,512]{3,2,1,0:T(4,128)S(1)} %pad_maximum_fusion.7), channel_id=1, source_target_pairs={{32,0},{64,32},{96,64},{128,96},{160,128},{192,160},{224,192},{256... | collective-permute-start | bytes 18440 | tf_op jit(solution)/shard_map/ppermute | solution.py:20
  17.9 15.4 %collective-permute-start.4 = (bf16[1,1,512,128]{3,2,1,0:T(8,128)(2,1)}, bf16[1,1,512,128]{3,2,1,0:T(8,128)(2,1)S(1)}, u32[]{:S(2)}, u32[]{:S(2)}) collective-permute-start(bf16[1,1,512,128]{3,2,1,0:T(8,128)(2,1)} %param.9), channel_id=1, source_target_pairs={{0,32},{32,64},{64,96},{96,128},{128,160},{160,192},{192,224},{224... | collective-permute-start | bytes 393224 | tf_op jit(solution)/shard_map/ppermute | solution.py:18
  19.9 14.6 %collective-permute-start.5 = (bf16[1,1,512,128]{3,2,1,0:T(8,128)(2,1)}, bf16[1,1,512,128]{3,2,1,0:T(8,128)(2,1)S(1)}, u32[]{:S(2)}, u32[]{:S(2)}) collective-permute-start(bf16[1,1,512,128]{3,2,1,0:T(8,128)(2,1)} %param.9), channel_id=1, source_target_pairs={{32,0},{64,32},{96,64},{128,96},{160,128},{192,160},{224,192},{256... | collective-permute-start | bytes 393224 | tf_op jit(solution)/shard_map/ppermute | solution.py:20
  29.3 13.1 %copy-start.1 = (f32[1,1,512]{2,1,0:T(1,128)S(1)}, f32[1,1,512]{2,1,0:T(1,128)}, u32[]{:S(2)}) copy-start(f32[1,1,512]{2,1,0:T(1,128)} %param.10) | copy-start | bytes 6148
  34.4 24.9 %collective-permute-start.6 = (bf16[3,1,512,128]{3,2,1,0:T(8,128)(2,1)S(1)}, bf16[3,1,512,128]{3,2,1,0:T(8,128)(2,1)S(1)}, u32[]{:S(2)}, u32[]{:S(2)}) collective-permute-start(bf16[3,1,512,128]{3,2,1,0:T(8,128)(2,1)S(1)} %constant_dynamic-update-slice_fusion), channel_id=1, source_target_pairs={{0,1},{1,2},{2,3},{3,4},{4,5},{5,6},{6,7},{7,8},{8,9},{9,10},{10,1... | collective-permute-start | bytes 1179656 | tf_op jit(solution)/shard_map/ppermute | solution.py:18
  40.5 18.9 %collective-permute-start.7 = (bf16[3,1,512,128]{3,2,1,0:T(8,128)(2,1)S(1)}, bf16[3,1,512,128]{3,2,1,0:T(8,128)(2,1)S(1)}, u32[]{:S(2)}, u32[]{:S(2)}) collective-permute-start(bf16[3,1,512,128]{3,2,1,0:T(8,128)(2,1)S(1)} %constant_dynamic-update-slice_fusion), channel_id=1, source_target_pairs={{1,0},{2,1},{3,2},{4,3},{5,4},{6,5},{7,6},{8,7},{9,8},{10,9},{11,1... | collective-permute-start | bytes 1179656 | tf_op jit(solution)/shard_map/ppermute | solution.py:20
  42.4 9.8 %collective-permute-start.2 = (f32[3,1,3,512]{3,2,1,0:T(4,128)S(1)}, f32[3,1,3,512]{3,2,1,0:T(4,128)S(1)}, u32[]{:S(2)}, u32[]{:S(2)}) collective-permute-start(f32[3,1,3,512]{3,2,1,0:T(4,128)S(1)} %pad_maximum_fusion), channel_id=1, source_target_pairs={{0,1},{1,2},{2,3},{3,4},{4,5},{5,6},{6,7},{7,8},{8,9},{9,10},{10,1... | collective-permute-start | bytes 55304 | tf_op jit(solution)/shard_map/ppermute | solution.py:18
  50.0 9.1 %collective-permute-start.3 = (f32[3,1,3,512]{3,2,1,0:T(4,128)S(1)}, f32[3,1,3,512]{3,2,1,0:T(4,128)S(1)}, u32[]{:S(2)}, u32[]{:S(2)}) collective-permute-start(f32[3,1,3,512]{3,2,1,0:T(4,128)S(1)} %pad_maximum_fusion), channel_id=1, source_target_pairs={{1,0},{2,1},{3,2},{4,3},{5,4},{6,5},{7,6},{8,7},{9,8},{10,9},{11,1... | collective-permute-start | bytes 55304 | tf_op jit(solution)/shard_map/ppermute | solution.py:20
where the time goes:
time: 136 us; the launch traced here: 135 us
  starting transfers between devices  43.9 us (32%)
  matrix products  42.9 us (32%)
  loops' own time  22.7 us (17%)
  other arithmetic  9.49 us (7%)
  waiting for transfers between devices  9.06 us (7%)
  local copies, waits for them, and re-layouts  6.16 us (5%)
    ppermute x4, starting transfers between devices, with_halo(): lax.ppermute(head, axis, [((i + 1) % count, i) for i in range(count)])  24.4 us
    another operation x1, loops' own time, local_solve(): grams, pulls = lax.map(patch_terms, jnp.arange(patches, dtype=jnp.int32))  22.7 us
    ppermute x4, starting transfers between devices, with_halo(): lax.ppermute(tail, axis, [(i, (i + 1) % count) for i in range(count)])  19.5 us
    dot_general x8, matrix products, patch_terms(): lax.dot_general(weighted, spread, (((0,), (0,)), ((), ())), preferred_ele...  9.24 us
    dot_general x8, matrix products, patch_terms(): jnp.dot(innovation, weighted.astype(jnp.float32), precision=lax.Precision...  8.61 us
    dot_general x12, matrix products, local_solve(): jnp.matmul(factor, inverse_root, precision=lax.Precision.HIGHEST)  7.92 us
    ppermute x4, waiting for transfers between devices, with_halo(): lax.ppermute(head, axis, [((i + 1) % count, i) for i in range(count)])  7.82 us
    dot_general x12, matrix products, local_solve(): jnp.matmul(inverse_root, iterate, precision=lax.Precision.HIGHEST)  7.79 us
  transfers between devices with their start and end apart: 8, of which 3 were waited for; matrix products, arithmetic and copies ran while one was open for 3% of the time, Pallas kernels for 0%

commit v1 on v0

v1 whole, which is shorter than its diff:
```python
import functools

import jax
import jax.numpy as jnp
from jax import lax
from jax.experimental import pallas as pl
from jax.experimental.pallas import tpu as pltpu
from jax.sharding import PartitionSpec as P

PATCH = 16
NS_STEPS = 12
RAD = 24
EXTRA = 16
WEIGHT, ROW, COL = 2, 5, 6
F32, BF16 = jnp.float32, jnp.bfloat16


def halves(x):
    high = x.astype(BF16)
    return high, (x - high.astype(F32)).astype(BF16)


def thirds(x):
    high = x.astype(BF16)
    return high, *halves(x - high.astype(F32))


def side_by_side(x):
    return jnp.concatenate(halves(x), axis=1)


def pack_kernel(count_ref, members_ref, values_ref, precision_ref, cells_ref, out_ref, *, tile_cols):
    capacity, ensemble = members_ref.shape
    members = members_ref[...].T.astype(F32)
    mean = jnp.sum(members, axis=0, keepdims=True) * (1.0 / ensemble)
    out_ref[:ensemble, :] = (members - mean).astype(BF16)
    slot = lax.broadcasted_iota(jnp.int32, (1, capacity), 1)
    weight = jnp.where(slot < count_ref[0, 0], precision_ref[...], 0.0)
    cells = cells_ref[...]
    rows = [
        *halves(values_ref[...] - mean),
        *thirds(weight),
        (cells // tile_cols).astype(BF16),
        (cells % tile_cols).astype(BF16),
    ]
    index = lax.broadcasted_iota(jnp.int32, (EXTRA, capacity), 0)
    extra = jnp.zeros((EXTRA, capacity), F32)
    for at, row in enumerate(rows):
        extra = jnp.where(index == at, row.astype(F32), extra)
    out_ref[ensemble:, :] = extra.astype(BF16)


def locals_of(scalars, row_shift, col_shift, centres):
    high, middle, low = (scalars[WEIGHT + at : WEIGHT + at + 1] for at in range(3))
    weight = high + (middle + low)
    rows_twice = 2.0 * (scalars[ROW : ROW + 1] + row_shift) + 1.0
    cols_twice = 2.0 * (scalars[COL : COL + 1] + col_shift) + 1.0
    count = len(centres)
    index = lax.broadcasted_iota(jnp.int32, (8, 1), 0)
    row_centre = jnp.zeros((8, 1), F32)
    col_centre = jnp.zeros((8, 1), F32)
    for at, (row, col) in enumerate(centres):
        row_centre = jnp.where(index == at, row, row_centre)
        col_centre = jnp.where(index == at, col, col_centre)
    row_gap = rows_twice - row_centre
    col_gap = cols_twice - col_centre
    distance = row_gap * row_gap + col_gap * col_gap
    taper = jnp.where(distance < 4.0 * RAD * RAD, jnp.exp(-distance / (2.0 * RAD * RAD)), 0.0)
    local = weight * taper
    return [local[at : at + 1] for at in range(count)]


def add_grams(gram_ref, payload, shifts, patches, centres, ensemble):
    scalars = payload[ensemble:].astype(F32)
    spread = payload[:ensemble].astype(F32)
    local = locals_of(scalars, *shifts, [centres[p] for p in patches])
    weighted = jnp.concatenate([(row * spread).astype(BF16) for row in local], axis=0)
    part = lax.dot_general(weighted, payload, (((1,), (1,)), ((), ())), preferred_element_type=F32)
    for at, p in enumerate(patches):
        gram_ref[p] += part[at * ensemble : (at + 1) * ensemble]


def double_dot(left, right):
    width = right.shape[1] // 2
    both = jnp.dot(left, jnp.concatenate([right, right], axis=0), preferred_element_type=F32)
    return both[:, :width] + both[:, width:]


def solve(gram_ref, half_ref, z_ref, transform_ref, patches, ensemble):
    row = lax.broadcasted_iota(jnp.int32, (ensemble, ensemble), 0)
    col = lax.broadcasted_iota(jnp.int32, (ensemble, ensemble), 1)
    diagonal = row == col
    traces = []
    for p in range(patches):
        system = gram_ref[p, :, :ensemble] + jnp.where(diagonal, ensemble - 1.0, 0.0)
        on = jnp.where(diagonal, system, 0.0)
        trace = jnp.sum(jnp.sum(on, axis=0, keepdims=True), axis=1, keepdims=True)
        traces.append(trace)
        half = system * (-0.5 / trace)
        half_ref[p] = half
        z_ref[p] = jnp.where(diagonal, 1.5, 0.0) + half

    def times(matrix, column):
        across = jnp.sum(jnp.where(diagonal, column, 0.0), axis=0, keepdims=True)
        return jnp.sum(matrix * across, axis=1, keepdims=True)

    def advance_half(p, half, right):
        middle = 1.5 * half + double_dot(right, right)
        half_ref[p] = 1.5 * middle + double_dot(side_by_side(middle), right)

    for p in range(patches):
        half = half_ref[p]
        advance_half(p, half, side_by_side(half))

    def step(_, carry):
        for p in range(patches):
            half, z = half_ref[p], z_ref[p]
            right = side_by_side(half)
            left = jnp.concatenate([right, side_by_side(z)], axis=0)
            both = double_dot(left, right)
            middle = 1.5 * half + both[:ensemble]
            z_ref[p] = 1.5 * z + both[ensemble:]
            half_ref[p] = 1.5 * middle + double_dot(side_by_side(middle), right)
        return carry

    lax.fori_loop(0, NS_STEPS - 2, step, 0)
    for p in range(patches):
        half, z = half_ref[p], z_ref[p]
        z = 1.5 * z + double_dot(side_by_side(z), side_by_side(half))
        pull = gram_ref[p, :, ensemble : ensemble + 1] + gram_ref[p, :, ensemble + 1 : ensemble + 2]
        weights = times(z, times(z, pull)) / traces[p]
        transform_ref[p] = (z * jnp.sqrt((ensemble - 1.0) / traces[p]) + weights).astype(BF16)


def analyse(cells, transform):
    ensemble = cells.shape[1]
    ones = jnp.full((ensemble, ensemble), 1.0 / ensemble, BF16)
    mean = jnp.dot(cells, ones, preferred_element_type=F32)
    perturbation = (cells.astype(F32) - mean).astype(BF16)
    return (mean + jnp.dot(perturbation, transform, preferred_element_type=F32)).astype(BF16)


def sides(parity_ref, span):
    odd = parity_ref
    near = 1 - odd
    shift = (2 * near - 1).astype(F32) * span
    return near, shift


def centre_of(index):
    return jnp.asarray(2 * PATCH * index + PATCH, F32)


def mid_kernel(parity_ref, own_ref, first_ref, second_ref, state_ref, out_ref, gram, half, z, transform):
    ensemble = own_ref.shape[0] - EXTRA
    rows, cols = state_ref.shape[0], state_ref.shape[1]
    near, shift = sides(parity_ref[0], float(rows))
    row_index = (near, 1 - near)
    gram[...] = jnp.zeros_like(gram)
    inner = (1, 2)
    centres = [(centre_of(r), centre_of(c)) for r in row_index for c in inner]
    add_grams(gram, own_ref[...], (0.0, 0.0), (0, 1, 2, 3), centres, ensemble)
    add_grams(gram, first_ref[...], (shift, 0.0), (0, 1), centres, ensemble)
    add_grams(gram, second_ref[...], (-shift, 0.0), (2, 3), centres, ensemble)
    solve(gram, half, z, transform, 4, ensemble)
    for p in range(4):
        r, c = row_index[p // 2], inner[p % 2]
        at = pl.ds(pl.multiple_of(r * PATCH, PATCH), PATCH)
        cells = state_ref[at, c * PATCH : (c + 1) * PATCH, :].reshape(PATCH * PATCH, ensemble)
        out = analyse(cells, transform[p]).reshape(PATCH, PATCH, ensemble)
        out_ref[at, (c - 1) * PATCH : c * PATCH, :] = out


def edge_kernel(
    parity_ref, own_ref, first_ref, second_ref, near_ref, far_ref, state_ref, mid_ref, out_ref, gram, half, z, transform
):
    payload = own_ref.shape[0]
    ensemble = payload - EXTRA
    rows, cols = state_ref.shape[0], state_ref.shape[1]
    row_near, row_shift = sides(parity_ref[0], float(rows))
    col_near, col_shift = sides(parity_ref[1], float(cols))
    last = cols // PATCH - 1
    row_index = (row_near, 1 - row_near)
    col_index = (last * col_near, last * (1 - col_near))
    gram[...] = jnp.zeros_like(gram)
    centres = [(centre_of(r), centre_of(c)) for r in row_index for c in col_index]
    add_grams(gram, own_ref[...], (0.0, 0.0), (0, 1, 2, 3), centres, ensemble)
    add_grams(gram, first_ref[...], (row_shift, 0.0), (0, 1), centres, ensemble)
    add_grams(gram, second_ref[...], (-row_shift, 0.0), (2, 3), centres, ensemble)
    for at, (ref, shift) in enumerate(((near_ref, col_shift), (far_ref, -col_shift))):
        add_grams(gram, ref[:payload], (0.0, shift), (at, 2 + at), centres, ensemble)
        add_grams(gram, ref[payload : 2 * payload], (row_shift, shift), (at,), centres, ensemble)
        add_grams(gram, ref[2 * payload :], (-row_shift, shift), (2 + at,), centres, ensemble)
    solve(gram, half, z, transform, 4, ensemble)
    out_ref[:, PATCH : cols - PATCH, :] = mid_ref[...]
    for p in range(4):
        r, c = row_index[p // 2], col_index[p % 2]
        at = pl.ds(pl.multiple_of(r * PATCH, PATCH), PATCH)
        across = pl.ds(pl.multiple_of(c * PATCH, PATCH), PATCH)
        cells = state_ref[at, across, :].reshape(PATCH * PATCH, ensemble)
        out = analyse(cells, transform[p]).reshape(PATCH, PATCH, ensemble)
        out_ref[at, across, :] = out


def vmem(count):
    return [pl.BlockSpec(memory_space=pltpu.VMEM)] * count


SMEM = pl.BlockSpec(memory_space=pltpu.SMEM)


def scratch(ensemble):
    return [
        pltpu.VMEM((4, ensemble, ensemble + EXTRA), F32),
        pltpu.VMEM((4, ensemble, ensemble), F32),
        pltpu.VMEM((4, ensemble, ensemble), F32),
        pltpu.VMEM((4, ensemble, ensemble), BF16),
    ]


def pack(members, values, precision, cells, counts, tile_cols):
    capacity, ensemble = members.shape
    return pl.pallas_call(
        functools.partial(pack_kernel, tile_cols=tile_cols),
        out_shape=jax.ShapeDtypeStruct((ensemble + EXTRA, capacity), BF16),
        in_specs=[SMEM] + vmem(4),
        out_specs=pl.BlockSpec(memory_space=pltpu.VMEM),
    )(counts, members, values, precision, cells)


def middle(parity, own, first, second, state):
    rows, cols, ensemble = state.shape
    return pl.pallas_call(
        mid_kernel,
        out_shape=jax.ShapeDtypeStruct((rows, cols - 2 * PATCH, ensemble), BF16),
        in_specs=[SMEM] + vmem(4),
        out_specs=pl.BlockSpec(memory_space=pltpu.VMEM),
        scratch_shapes=scratch(ensemble),
        compiler_params=pltpu.CompilerParams(vmem_limit_bytes=24 << 20),
        cost_estimate=pl.CostEstimate(flops=1 << 32, bytes_accessed=1 << 20, transcendentals=0),
    )(parity, own, first, second, state)


def edges(parity, own, first, second, near, far, state, mid):
    return pl.pallas_call(
        edge_kernel,
        out_shape=jax.ShapeDtypeStruct(state.shape, BF16),
        in_specs=[SMEM] + vmem(7),
        out_specs=pl.BlockSpec(memory_space=pltpu.VMEM),
        scratch_shapes=scratch(state.shape[-1]),
        compiler_params=pltpu.CompilerParams(vmem_limit_bytes=24 << 20),
    )(parity, own, first, second, near, far, state, mid)


def exchange(x, axis, first, wrap):
    count = lax.axis_size(axis)
    pairs = []
    for low in range(first, count, 2):
        high = (low + 1) % count
        if high > low or wrap:
            pairs += [(low, high), (high, low)]
    return lax.ppermute(x, axis, pairs)


def body(state, obs_members, obs_values, obs_precision, obs_cells, obs_counts):
    _, tile_rows, tile_cols, ensemble = state.shape
    capacity = obs_members.shape[2]
    parity = jnp.stack([lax.axis_index("lat") % 2, lax.axis_index("lon") % 2]).astype(jnp.int32)
    own = pack(
        obs_members.reshape(capacity, ensemble),
        obs_values.reshape(1, capacity),
        obs_precision.reshape(1, capacity),
        obs_cells.reshape(1, capacity),
        obs_counts,
        tile_cols,
    )
    second = exchange(own, "lat", 1, False)
    first = exchange(own, "lat", 0, False)
    column = jnp.concatenate([own, first, second], axis=0)
    far = exchange(column, "lon", 1, True)
    near = exchange(column, "lon", 0, True)
    cells = state.reshape(tile_rows, tile_cols, ensemble)
    mid = middle(parity, own, first, second, cells)
    out = edges(parity, own, first, second, near, far, cells, mid)
    return out.reshape(state.shape)


def solution(mesh):
    in_specs = (
        P(None, "lat", "lon", None),
        P("lat", "lon", None, None),
        P("lat", "lon", None),
        P("lat", "lon", None),
        P("lat", "lon", None),
        P("lat", "lon"),
    )
    out_specs = P(None, "lat", "lon", None)
    return jax.shard_map(body, mesh=mesh, in_specs=in_specs, out_specs=out_specs, check_vma=False)
```

time: 136 us -> 52.4 us (0.39)
  the two profiles are of different devices: /device:TPU:31 before, /device:TPU:57 now
where the time goes in v1:
time: 52.4 us; the launch traced here: 52.1 us
  Pallas kernels  23.3 us (44%)
  starting transfers between devices  22.5 us (43%)
  waiting for transfers between devices  4.55 us (9%)
  other arithmetic  1.02 us (2%)
  between operations  0.74 us (1%)
    ppermute x4, starting transfers between devices, exchange(): return lax.ppermute(x, axis, pairs)  22.5 us
    pallas_call x1, Pallas kernels, edges(): pl.pallas_call(edge_kernel, out_shape=jax.ShapeDtypeStruct(state.shape, B...  11.4 us
    pallas_call x1, Pallas kernels, middle(): pl.pallas_call(mid_kernel, out_shape=jax.ShapeDtypeStruct((rows, cols - 2...  10.2 us
    ppermute x4, waiting for transfers between devices, exchange(): return lax.ppermute(x, axis, pairs)  4.55 us
    pallas_call x1, Pallas kernels, pack(): pl.pallas_call(functools.partial(pack_kernel, tile_cols=tile_cols), out_s...  1.72 us
  transfers between devices with their start and end apart: 4, of which 2 were waited for; matrix products, arithmetic and copies ran while one was open for 0% of the time, Pallas kernels for 20%

profile of v1, /device:TPU:57, one launch (start us, length us, event | category | flops | bytes accessed | tf_op | source)
XLA Modules:
  0.0 52.1 jit_solution(11190188544096990565)
XLA Ops:
  0.7 1.7 %shard_map.64.own_ref = bf16[144,512]{1,0:T(8,128)(2,1)} custom-call(s32[1,1]{1,0:T(1,128)S(6)} %copy.7.count_ref, bf16[512,128]{1,0:T(8,128)(2,1)} %bitcast.10, f32[1,512]{1,0:T(1,128)} %bitcast.11, f32[1,512]{1,0:T(1,128)} %bitcast.12, s32[1,512]{1,0:T(1,128)} %bitcast.13), custom_call_target="tpu_custom_call" | custom-call | tf_op jit(solution)/shard_map/pallas_call | solution.py:223
  2.4 0.0 copy-start.1
  2.4 13.0 %collective-permute-start.1 = (bf16[144,512]{1,0:T(8,128)(2,1)}, bf16[144,512]{1,0:T(8,128)(2,1)S(1)}, u32[]{:S(2)}, u32[]{:S(2)}) collective-permute-start(bf16[144,512]{1,0:T(8,128)(2,1)} %shard_map.64.own_ref), channel_id=1, source_target_pairs={{32,64},{64,32},{96,128},{128,96},{160,192},{192,160},{224,256},{2... | collective-permute-start | bytes 442376 | tf_op jit(solution)/shard_map/ppermute | solution.py:262
  15.4 1.9 %collective-permute-start = (bf16[144,512]{1,0:T(8,128)(2,1)}, bf16[144,512]{1,0:T(8,128)(2,1)S(1)}, u32[]{:S(2)}, u32[]{:S(2)}) collective-permute-start(bf16[144,512]{1,0:T(8,128)(2,1)} %shard_map.64.own_ref), channel_id=1, source_target_pairs={{0,32},{32,0},{64,96},{96,64},{128,160},{160,128},{192,224},{224,1... | collective-permute-start | bytes 442376 | tf_op jit(solution)/shard_map/ppermute | solution.py:262
  17.4 0.0 copy-start
  17.4 1.8 %collective-permute-done.1.second_ref = bf16[144,512]{1,0:T(8,128)(2,1)S(1)} collective-permute-done((bf16[144,512]{1,0:T(8,128)(2,1)}, bf16[144,512]{1,0:T(8,128)(2,1)S(1)}, u32[]{:S(2)}, u32[]{:S(2)}) %collective-permute-start.1) | collective-permute-done | bytes 147488 | tf_op jit(solution)/shard_map/ppermute | solution.py:262
  19.2 2.7 %collective-permute-done.first_ref = bf16[144,512]{1,0:T(8,128)(2,1)S(1)} collective-permute-done((bf16[144,512]{1,0:T(8,128)(2,1)}, bf16[144,512]{1,0:T(8,128)(2,1)S(1)}, u32[]{:S(2)}, u32[]{:S(2)}) %collective-permute-start) | collective-permute-done | bytes 147488 | tf_op jit(solution)/shard_map/ppermute | solution.py:262
  21.9 0.9 %pad_maximum_fusion = bf16[432,512]{1,0:T(8,128)(2,1)S(1)} fusion(bf16[144,512]{1,0:T(8,128)(2,1)S(1)} %collective-permute-done.1.second_ref, bf16[144,512]{1,0:T(8,128)(2,1)S(1)} %collective-permute-done.first_ref, bf16[144,512]{1,0:T(8,128)(2,1)} %shard_map.64.own_ref), kind=kLoop, calls=%fused_computation | loop fusion | flops 1327104 | bytes 884736 | tf_op jit(solution)/shard_map/concatenate | solution.py:279
  22.9 4.9 %collective-permute-start.3 = (bf16[432,512]{1,0:T(8,128)(2,1)S(1)}, bf16[432,512]{1,0:T(8,128)(2,1)S(1)}, u32[]{:S(2)}, u32[]{:S(2)}) collective-permute-start(bf16[432,512]{1,0:T(8,128)(2,1)S(1)} %pad_maximum_fusion), channel_id=1, source_target_pairs={{1,2},{2,1},{3,4},{4,3},{5,6},{6,5},{7,8},{8,7},{9,10},{10,9},{11,... | collective-permute-start | bytes 1327112 | tf_op jit(solution)/shard_map/ppermute | solution.py:262
  27.7 2.7 %collective-permute-start.2 = (bf16[432,512]{1,0:T(8,128)(2,1)S(1)}, bf16[432,512]{1,0:T(8,128)(2,1)S(1)}, u32[]{:S(2)}, u32[]{:S(2)}) collective-permute-start(bf16[432,512]{1,0:T(8,128)(2,1)S(1)} %pad_maximum_fusion), channel_id=1, source_target_pairs={{0,1},{1,0},{2,3},{3,2},{4,5},{5,4},{6,7},{7,6},{8,9},{9,8},{10,11... | collective-permute-start | bytes 1327112 | tf_op jit(solution)/shard_map/ppermute | solution.py:262
  30.4 0.1 pad_add_fusion.parity_ref
  30.5 0.0 copy-done.1
  30.5 0.0 copy-done
  30.5 10.2 %shard_map.65.mid_ref = bf16[32,32,128]{2,1,0:T(8,128)(2,1)S(1)} custom-call(s32[2]{0:T(128)S(1)} %pad_add_fusion.parity_ref, bf16[144,512]{1,0:T(8,128)(2,1)S(1)} %copy-done, bf16[144,512]{1,0:T(8,128)(2,1)S(1)} %collective-permute-done.first_ref, bf16[144,512]{1,0:T(8,128)(2,1)S(1)} %collective-permute-done.1.second_ref, bf16[32,64,128]{2,1,0:T(8,128)(2,1)S(1)} %bitcast.8), custom_call_target="tpu_custom_call" | custom-call | flops 4294967296 | bytes 1048576 | tf_op jit(solution)/shard_map/pallas_call | solution.py:233
  40.7 0.0 collective-permute-done.3.far_ref
  40.7 0.0 collective-permute-done.2.near_ref
  40.7 11.4 %shard_map.66 = bf16[32,64,128]{2,1,0:T(8,128)(2,1)} custom-call(s32[2]{0:T(128)S(1)} %pad_add_fusion.parity_ref, bf16[144,512]{1,0:T(8,128)(2,1)S(1)} %copy-done, bf16[144,512]{1,0:T(8,128)(2,1)S(1)} %collective-permute-done.first_ref, bf16[144,512]{1,0:T(8,128)(2,1)S(1)} %collective-permute-done.1.second_ref, ...), custom_call_target="tpu_custom_call" | custom-call | tf_op jit(solution)/shard_map/pallas_call | solution.py:245
Async XLA Ops:
  2.4 28.1 %copy-start.1 = (bf16[1,32,64,128]{3,2,1,0:T(8,128)(2,1)S(1)}, bf16[1,32,64,128]{3,2,1,0:T(8,128)(2,1)}, u32[]{:S(2)}) copy-start(bf16[1,32,64,128]{3,2,1,0:T(8,128)(2,1)} %param.6) | copy-start | bytes 1572868
  2.4 16.8 %collective-permute-start.1 = (bf16[144,512]{1,0:T(8,128)(2,1)}, bf16[144,512]{1,0:T(8,128)(2,1)S(1)}, u32[]{:S(2)}, u32[]{:S(2)}) collective-permute-start(bf16[144,512]{1,0:T(8,128)(2,1)} %shard_map.64.own_ref), channel_id=1, source_target_pairs={{32,64},{64,32},{96,128},{128,96},{160,192},{192,160},{224,256},{2... | collective-permute-start | bytes 442376 | tf_op jit(solution)/shard_map/ppermute | solution.py:262
  15.4 6.5 %collective-permute-start = (bf16[144,512]{1,0:T(8,128)(2,1)}, bf16[144,512]{1,0:T(8,128)(2,1)S(1)}, u32[]{:S(2)}, u32[]{:S(2)}) collective-permute-start(bf16[144,512]{1,0:T(8,128)(2,1)} %shard_map.64.own_ref), channel_id=1, source_target_pairs={{0,32},{32,0},{64,96},{96,64},{128,160},{160,128},{192,224},{224,1... | collective-permute-start | bytes 442376 | tf_op jit(solution)/shard_map/ppermute | solution.py:262
  17.4 13.1 %copy-start = (bf16[144,512]{1,0:T(8,128)(2,1)S(1)}, bf16[144,512]{1,0:T(8,128)(2,1)}, u32[]{:S(2)}) copy-start(bf16[144,512]{1,0:T(8,128)(2,1)} %shard_map.64.own_ref) | copy-start | bytes 442372
  22.9 17.9 %collective-permute-start.3 = (bf16[432,512]{1,0:T(8,128)(2,1)S(1)}, bf16[432,512]{1,0:T(8,128)(2,1)S(1)}, u32[]{:S(2)}, u32[]{:S(2)}) collective-permute-start(bf16[432,512]{1,0:T(8,128)(2,1)S(1)} %pad_maximum_fusion), channel_id=1, source_target_pairs={{1,2},{2,1},{3,4},{4,3},{5,6},{6,5},{7,8},{8,7},{9,10},{10,9},{11,... | collective-permute-start | bytes 1327112 | tf_op jit(solution)/shard_map/ppermute | solution.py:262
  27.7 13.0 %collective-permute-start.2 = (bf16[432,512]{1,0:T(8,128)(2,1)S(1)}, bf16[432,512]{1,0:T(8,128)(2,1)S(1)}, u32[]{:S(2)}, u32[]{:S(2)}) collective-permute-start(bf16[432,512]{1,0:T(8,128)(2,1)S(1)} %pad_maximum_fusion), channel_id=1, source_target_pairs={{0,1},{1,0},{2,3},{3,2},{4,5},{5,4},{6,7},{7,6},{8,9},{9,8},{10,11... | collective-permute-start | bytes 1327112 | tf_op jit(solution)/shard_map/ppermute | solution.py:262

commit v2 on v1

--- a/solution.py
+++ b/solution.py
@@ -12,6 +12,7 @@
 RAD = 24
 EXTRA = 16
 WEIGHT, ROW, COL = 2, 5, 6
+UNROLL = 10
 F32, BF16 = jnp.float32, jnp.bfloat16
 
 
@@ -29,7 +30,15 @@
     return jnp.concatenate(halves(x), axis=1)
 
 
-def pack_kernel(count_ref, members_ref, values_ref, precision_ref, cells_ref, out_ref, *, tile_cols):
+def pack_kernel(count_ref, members_in, values_in, precision_in, cells_in, out_ref, *scratch, tile_cols):
+    *held, semaphores = scratch
+    given = (members_in, values_in, precision_in, cells_in)
+    copies = [pltpu.make_async_copy(a, b, semaphores.at[at]) for at, (a, b) in enumerate(zip(given, held))]
+    for copy in copies:
+        copy.start()
+    for copy in copies:
+        copy.wait()
+    members_ref, values_ref, precision_ref, cells_ref = held
     capacity, ensemble = members_ref.shape
     members = members_ref[...].T.astype(F32)
     mean = jnp.sum(members, axis=0, keepdims=True) * (1.0 / ensemble)
@@ -86,50 +95,57 @@
     return both[:, :width] + both[:, width:]
 
 
-def solve(gram_ref, half_ref, z_ref, transform_ref, patches, ensemble):
+def solve(gram_ref, half_ref, z_ref, right_ref, transform_ref, ensemble):
+    patches = range(gram_ref.shape[0])
     row = lax.broadcasted_iota(jnp.int32, (ensemble, ensemble), 0)
     col = lax.broadcasted_iota(jnp.int32, (ensemble, ensemble), 1)
     diagonal = row == col
     traces = []
-    for p in range(patches):
+    for p in patches:
         system = gram_ref[p, :, :ensemble] + jnp.where(diagonal, ensemble - 1.0, 0.0)
         on = jnp.where(diagonal, system, 0.0)
         trace = jnp.sum(jnp.sum(on, axis=0, keepdims=True), axis=1, keepdims=True)
         traces.append(trace)
         half = system * (-0.5 / trace)
         half_ref[p] = half
+        right_ref[p] = side_by_side(half)
         z_ref[p] = jnp.where(diagonal, 1.5, 0.0) + half
 
     def times(matrix, column):
         across = jnp.sum(jnp.where(diagonal, column, 0.0), axis=0, keepdims=True)
         return jnp.sum(matrix * across, axis=1, keepdims=True)
 
-    def advance_half(p, half, right):
-        middle = 1.5 * half + double_dot(right, right)
-        half_ref[p] = 1.5 * middle + double_dot(side_by_side(middle), right)
-
-    for p in range(patches):
-        half = half_ref[p]
-        advance_half(p, half, side_by_side(half))
+    def advance(with_root):
+        for p in patches:
+            right = right_ref[p]
+            if with_root:
+                z = z_ref[p]
+                both = double_dot(jnp.concatenate([right, side_by_side(z)], axis=0), right)
+                z_ref[p] = 1.5 * z + both[ensemble:]
+            else:
+                both = double_dot(right, right)
+            half_ref[p] = 1.5 * half_ref[p] + both[:ensemble]
+        for p in patches:
+            middle = half_ref[p]
+            half = 1.5 * middle + double_dot(side_by_side(middle), right_ref[p])
+            half_ref[p] = half
+            right_ref[p] = side_by_side(half)
 
     def step(_, carry):
-        for p in range(patches):
-            half, z = half_ref[p], z_ref[p]
-            right = side_by_side(half)
-            left = jnp.concatenate([right, side_by_side(z)], axis=0)
-            both = double_dot(left, right)
-            middle = 1.5 * half + both[:ensemble]
-            z_ref[p] = 1.5 * z + both[ensemble:]
-            half_ref[p] = 1.5 * middle + double_dot(side_by_side(middle), right)
+        advance(True)
         return carry
 
-    lax.fori_loop(0, NS_STEPS - 2, step, 0)
-    for p in range(patches):
-        half, z = half_ref[p], z_ref[p]
-        z = 1.5 * z + double_dot(side_by_side(z), side_by_side(half))
-        pull = gram_ref[p, :, ensemble : ensemble + 1] + gram_ref[p, :, ensemble + 1 : ensemble + 2]
-        weights = times(z, times(z, pull)) / traces[p]
-        transform_ref[p] = (z * jnp.sqrt((ensemble - 1.0) / traces[p]) + weights).astype(BF16)
+    advance(False)
+    lax.fori_loop(0, NS_STEPS - 2, step, 0, unroll=UNROLL)
+    for p in patches:
+        z = z_ref[p]
+        z_ref[p] = 1.5 * z + double_dot(side_by_side(z), right_ref[p])
+    pulls = [gram_ref[p, :, ensemble : ensemble + 1] + gram_ref[p, :, ensemble + 1 : ensemble + 2] for p in patches]
+    inner = [times(z_ref[p], pulls[p]) for p in patches]
+    weights = [times(z_ref[p], inner[p]) for p in patches]
+    for p in patches:
+        scale = jnp.sqrt((ensemble - 1.0) / traces[p])
+        transform_ref[p] = (z_ref[p] * scale + weights[p] / traces[p]).astype(BF16)
 
 
 def analyse(cells, transform):
@@ -151,7 +167,7 @@
     return jnp.asarray(2 * PATCH * index + PATCH, F32)
 
 
-def mid_kernel(parity_ref, own_ref, first_ref, second_ref, state_ref, out_ref, gram, half, z, transform):
+def mid_kernel(parity_ref, own_ref, second_ref, first_ref, state_ref, out_ref, gram, half, z, right, transform):
     ensemble = own_ref.shape[0] - EXTRA
     rows, cols = state_ref.shape[0], state_ref.shape[1]
     near, shift = sides(parity_ref[0], float(rows))
@@ -162,7 +178,7 @@
     add_grams(gram, own_ref[...], (0.0, 0.0), (0, 1, 2, 3), centres, ensemble)
     add_grams(gram, first_ref[...], (shift, 0.0), (0, 1), centres, ensemble)
     add_grams(gram, second_ref[...], (-shift, 0.0), (2, 3), centres, ensemble)
-    solve(gram, half, z, transform, 4, ensemble)
+    solve(gram, half, z, right, transform, ensemble)
     for p in range(4):
         r, c = row_index[p // 2], inner[p % 2]
         at = pl.ds(pl.multiple_of(r * PATCH, PATCH), PATCH)
@@ -172,11 +188,13 @@
 
 
 def edge_kernel(
-    parity_ref, own_ref, first_ref, second_ref, near_ref, far_ref, state_ref, mid_ref, out_ref, gram, half, z, transform
+    parity_ref, own_ref, second_ref, first_ref, near_ref, far_ref, state_ref, mid_ref, out_ref, gram, half, z, right, transform, done, semaphores
 ):
     payload = own_ref.shape[0]
     ensemble = payload - EXTRA
     rows, cols = state_ref.shape[0], state_ref.shape[1]
+    inner = pltpu.make_async_copy(mid_ref, out_ref.at[:, PATCH : cols - PATCH, :], semaphores.at[4])
+    inner.start()
     row_near, row_shift = sides(parity_ref[0], float(rows))
     col_near, col_shift = sides(parity_ref[1], float(cols))
     last = cols // PATCH - 1
@@ -191,15 +209,18 @@
         add_grams(gram, ref[:payload], (0.0, shift), (at, 2 + at), centres, ensemble)
         add_grams(gram, ref[payload : 2 * payload], (row_shift, shift), (at,), centres, ensemble)
         add_grams(gram, ref[2 * payload :], (-row_shift, shift), (2 + at,), centres, ensemble)
-    solve(gram, half, z, transform, 4, ensemble)
-    out_ref[:, PATCH : cols - PATCH, :] = mid_ref[...]
+    solve(gram, half, z, right, transform, ensemble)
+    copies = []
     for p in range(4):
         r, c = row_index[p // 2], col_index[p % 2]
         at = pl.ds(pl.multiple_of(r * PATCH, PATCH), PATCH)
         across = pl.ds(pl.multiple_of(c * PATCH, PATCH), PATCH)
         cells = state_ref[at, across, :].reshape(PATCH * PATCH, ensemble)
-        out = analyse(cells, transform[p]).reshape(PATCH, PATCH, ensemble)
-        out_ref[at, across, :] = out
+        done[p] = analyse(cells, transform[p]).reshape(PATCH, PATCH, ensemble)
+        copies.append(pltpu.make_async_copy(done.at[p], out_ref.at[at, across, :], semaphores.at[p]))
+        copies[p].start()
+    for copy in (inner, *copies):
+        copy.wait()
 
 
 def vmem(count):
@@ -214,18 +235,39 @@
         pltpu.VMEM((4, ensemble, ensemble + EXTRA), F32),
         pltpu.VMEM((4, ensemble, ensemble), F32),
         pltpu.VMEM((4, ensemble, ensemble), F32),
+        pltpu.VMEM((4, ensemble, 2 * ensemble), BF16),
         pltpu.VMEM((4, ensemble, ensemble), BF16),
     ]
 
 
 def pack(members, values, precision, cells, counts, tile_cols):
     capacity, ensemble = members.shape
+    given = [pltpu.with_memory_space_constraint(x, pltpu.HBM) for x in (members, values, precision, cells)]
     return pl.pallas_call(
         functools.partial(pack_kernel, tile_cols=tile_cols),
-        out_shape=jax.ShapeDtypeStruct((ensemble + EXTRA, capacity), BF16),
-        in_specs=[SMEM] + vmem(4),
+        out_shape=pltpu.VMEM((ensemble + EXTRA, capacity), BF16),
+        in_specs=[SMEM] + [pl.BlockSpec(memory_space=pltpu.HBM)] * len(given),
         out_specs=pl.BlockSpec(memory_space=pltpu.VMEM),
-    )(counts, members, values, precision, cells)
+        scratch_shapes=[pltpu.VMEM(x.shape, x.dtype) for x in given] + [pltpu.SemaphoreType.DMA((len(given),))],
+        compiler_params=pltpu.CompilerParams(vmem_limit_bytes=4 << 20),
+    )(counts, *given)
+
+
+def stack_kernel(own_ref, second_ref, first_ref, out_ref):
+    rows = own_ref.shape[0]
+    for at, ref in enumerate((own_ref, first_ref, second_ref)):
+        out_ref[at * rows : (at + 1) * rows, :] = ref[...]
+
+
+def stack(own, first, second):
+    rows, capacity = own.shape
+    return pl.pallas_call(
+        stack_kernel,
+        out_shape=jax.ShapeDtypeStruct((3 * rows, capacity), BF16),
+        in_specs=vmem(3),
+        out_specs=pl.BlockSpec(memory_space=pltpu.VMEM),
+        compiler_params=pltpu.CompilerParams(vmem_limit_bytes=4 << 20),
+    )(own, second, first)
 
 
 def middle(parity, own, first, second, state):
@@ -236,20 +278,22 @@
         in_specs=[SMEM] + vmem(4),
         out_specs=pl.BlockSpec(memory_space=pltpu.VMEM),
         scratch_shapes=scratch(ensemble),
-        compiler_params=pltpu.CompilerParams(vmem_limit_bytes=24 << 20),
+        compiler_params=pltpu.CompilerParams(vmem_limit_bytes=12 << 20),
         cost_estimate=pl.CostEstimate(flops=1 << 32, bytes_accessed=1 << 20, transcendentals=0),
-    )(parity, own, first, second, state)
+    )(parity, own, second, first, state)
 
 
 def edges(parity, own, first, second, near, far, state, mid):
+    ensemble = state.shape[-1]
     return pl.pallas_call(
         edge_kernel,
         out_shape=jax.ShapeDtypeStruct(state.shape, BF16),
         in_specs=[SMEM] + vmem(7),
-        out_specs=pl.BlockSpec(memory_space=pltpu.VMEM),
-        scratch_shapes=scratch(state.shape[-1]),
-        compiler_params=pltpu.CompilerParams(vmem_limit_bytes=24 << 20),
-    )(parity, own, first, second, near, far, state, mid)
+        out_specs=pl.BlockSpec(memory_space=pltpu.HBM),
+        scratch_shapes=scratch(ensemble)
+        + [pltpu.VMEM((4, PATCH, PATCH, ensemble), BF16), pltpu.SemaphoreType.DMA((5,))],
+        compiler_params=pltpu.CompilerParams(vmem_limit_bytes=12 << 20),
+    )(parity, own, second, first, near, far, state, mid)
 
 
 def exchange(x, axis, first, wrap):
@@ -274,9 +318,9 @@
         obs_counts,
         tile_cols,
     )
+    first = exchange(own, "lat", 0, False)
     second = exchange(own, "lat", 1, False)
-    first = exchange(own, "lat", 0, False)
-    column = jnp.concatenate([own, first, second], axis=0)
+    column = stack(own, first, second)
     far = exchange(column, "lon", 1, True)
     near = exchange(column, "lon", 0, True)
     cells = state.reshape(tile_rows, tile_cols, ensemble)

time: 52.4 us -> 42.3 us (0.81)
  Pallas kernels: 23.3 us -> 12.8 us
  starting transfers between devices: 22.5 us -> 25.2 us
  waiting for transfers between devices: 4.55 us -> 3.22 us
  other arithmetic: 1.02 us -> 0.08 us
    pallas_call x1, Pallas kernels: 11.4 us -> 6.37 us  [edges(): pl.pallas_call(edge_kernel, out_shape=jax.ShapeDtypeStruct(state.shape, B...]
    pallas_call x1, Pallas kernels: 10.2 us -> 5.3 us  [middle(): pl.pallas_call(mid_kernel, out_shape=jax.ShapeDtypeStruct((rows, cols - 2...]
    ppermute x4, starting transfers between devices: 22.5 us -> 25.2 us  [exchange(): return lax.ppermute(x, axis, pairs)]
    ppermute x4, waiting for transfers between devices: 4.55 us -> 3.22 us  [exchange(): return lax.ppermute(x, axis, pairs)]
    concatenate x1 -> x0, other arithmetic: 0.94 us -> none  [body(): column = jnp.concatenate([own, first, second], axis=0)]
    pallas_call x1, Pallas kernels: 1.72 us -> 1.08 us  [pack(): pl.pallas_call(functools.partial(pack_kernel, tile_cols=tile_cols), out_s...]
  transfers between devices with their start and end apart: 4 -> 4, of which waited for: 2 -> 1; matrix products, arithmetic and copies ran while one was open for 0% -> 0% of each run, Pallas kernels for 20% -> 13%
where the time goes in v2:
time: 42.3 us; the launch traced here: 42.1 us
  starting transfers between devices  25.2 us (60%)
  Pallas kernels  12.8 us (30%)
  waiting for transfers between devices  3.22 us (8%)
  between operations  0.75 us (2%)
    ppermute x4, starting transfers between devices, exchange(): return lax.ppermute(x, axis, pairs)  25.2 us
    pallas_call x1, Pallas kernels, edges(): pl.pallas_call(edge_kernel, out_shape=jax.ShapeDtypeStruct(state.shape, B...  6.37 us
    pallas_call x1, Pallas kernels, middle(): pl.pallas_call(mid_kernel, out_shape=jax.ShapeDtypeStruct((rows, cols - 2...  5.3 us
    ppermute x4, waiting for transfers between devices, exchange(): return lax.ppermute(x, axis, pairs)  3.22 us
    pallas_call x1, Pallas kernels, pack(): pl.pallas_call(functools.partial(pack_kernel, tile_cols=tile_cols), out_s...  1.08 us
  transfers between devices with their start and end apart: 4, of which 1 were waited for; matrix products, arithmetic and copies ran while one was open for 0% of the time, Pallas kernels for 13%

profile of v2, /device:TPU:57, one launch (start us, length us, event | category | flops | bytes accessed | tf_op | source)
XLA Modules:
  0.0 42.1 jit_solution(9882859319848922292)
XLA Ops:
  0.7 1.1 %shard_map.64.own_ref = bf16[144,512]{1,0:T(8,128)(2,1)S(1)} custom-call(s32[1,1]{1,0:T(1,128)S(6)} %copy.7.count_ref, bf16[512,128]{1,0:T(8,128)(2,1)} %bitcast.10, f32[1,512]{1,0:T(1,128)} %bitcast.11, f32[1,512]{1,0:T(1,128)} %bitcast.12, s32[1,512]{1,0:T(1,128)} %bitcast.13), custom_call_target="tpu_custom_call" | custom-call | tf_op jit(solution)/shard_map/pallas_call | solution.py:246
  1.7 0.0 copy-start
  1.8 4.1 %collective-permute-start.1 = (bf16[144,512]{1,0:T(8,128)(2,1)S(1)}, bf16[144,512]{1,0:T(8,128)(2,1)S(1)}, u32[]{:S(2)}, u32[]{:S(2)}) collective-permute-start(bf16[144,512]{1,0:T(8,128)(2,1)S(1)} %shard_map.64.own_ref), channel_id=1, source_target_pairs={{0,32},{32,0},{64,96},{96,64},{128,160},{160,128},{192,224},{224,1... | collective-permute-start | bytes 442376 | tf_op jit(solution)/shard_map/ppermute | solution.py:306
  5.9 11.1 %collective-permute-start = (bf16[144,512]{1,0:T(8,128)(2,1)S(1)}, bf16[144,512]{1,0:T(8,128)(2,1)S(1)}, u32[]{:S(2)}, u32[]{:S(2)}) collective-permute-start(bf16[144,512]{1,0:T(8,128)(2,1)S(1)} %shard_map.64.own_ref), channel_id=1, source_target_pairs={{32,64},{64,32},{96,128},{128,96},{160,192},{192,160},{224,256},{2... | collective-permute-start | bytes 442376 | tf_op jit(solution)/shard_map/ppermute | solution.py:306
  17.0 0.0 collective-permute-done.1.first_ref
  17.0 3.2 %collective-permute-done.second_ref = bf16[144,512]{1,0:T(8,128)(2,1)S(1)} collective-permute-done((bf16[144,512]{1,0:T(8,128)(2,1)S(1)}, bf16[144,512]{1,0:T(8,128)(2,1)S(1)}, u32[]{:S(2)}, u32[]{:S(2)}) %collective-permute-start) | collective-permute-done | bytes 147488 | tf_op jit(solution)/shard_map/ppermute | solution.py:306
  20.3 4.7 %collective-permute-start.3 = (bf16[432,512]{1,0:T(8,128)(2,1)S(1)}, bf16[432,512]{1,0:T(8,128)(2,1)S(1)}, u32[]{:S(2)}, u32[]{:S(2)}) collective-permute-start(bf16[432,512]{1,0:T(8,128)(2,1)S(1)} %shard_map.65), channel_id=1, source_target_pairs={{1,2},{2,1},{3,4},{4,3},{5,6},{6,5},{7,8},{8,7},{9,10},{10,9},{11,... | collective-permute-start | bytes 1327112 | tf_op jit(solution)/shard_map/ppermute | solution.py:306
  24.9 5.4 %collective-permute-start.2 = (bf16[432,512]{1,0:T(8,128)(2,1)S(1)}, bf16[432,512]{1,0:T(8,128)(2,1)S(1)}, u32[]{:S(2)}, u32[]{:S(2)}) collective-permute-start(bf16[432,512]{1,0:T(8,128)(2,1)S(1)} %shard_map.65), channel_id=1, source_target_pairs={{0,1},{1,0},{2,3},{3,2},{4,5},{5,4},{6,7},{7,6},{8,9},{9,8},{10,11... | collective-permute-start | bytes 1327112 | tf_op jit(solution)/shard_map/ppermute | solution.py:306
  30.3 0.1 pad_add_fusion.parity_ref
  30.4 0.0 copy-done
  30.4 5.3 %shard_map.66.mid_ref = bf16[32,32,128]{2,1,0:T(8,128)(2,1)S(1)} custom-call(s32[2]{0:T(128)S(1)} %pad_add_fusion.parity_ref, bf16[144,512]{1,0:T(8,128)(2,1)S(1)} %shard_map.64.own_ref, bf16[144,512]{1,0:T(8,128)(2,1)S(1)} %collective-permute-done.second_ref, bf16[144,512]{1,0:T(8,128)(2,1)S(1)} %collective-permute-done.1.first_ref, ...), custom_call_target="tpu_custom_call" | custom-call | flops 4294967296 | bytes 1048576 | tf_op jit(solution)/shard_map/pallas_call | solution.py:275
  35.7 0.0 collective-permute-done.3.far_ref
  35.7 0.0 collective-permute-done.2.near_ref
  35.7 6.4 %shard_map.67 = bf16[32,64,128]{2,1,0:T(8,128)(2,1)} custom-call(s32[2]{0:T(128)S(1)} %pad_add_fusion.parity_ref, bf16[144,512]{1,0:T(8,128)(2,1)S(1)} %shard_map.64.own_ref, bf16[144,512]{1,0:T(8,128)(2,1)S(1)} %collective-permute-done.second_ref, bf16[144,512]{1,0:T(8,128)(2,1)S(1)} %collective-permute-done.1.first_ref, ...), custom_call_target="tpu_custom_call" | custom-call | tf_op jit(solution)/shard_map/pallas_call | solution.py:288
  (1 shorter events, 0.0 us)
Async XLA Ops:
  1.7 28.6 %copy-start = (bf16[1,32,64,128]{3,2,1,0:T(8,128)(2,1)S(1)}, bf16[1,32,64,128]{3,2,1,0:T(8,128)(2,1)}, u32[]{:S(2)}) copy-start(bf16[1,32,64,128]{3,2,1,0:T(8,128)(2,1)} %param.6) | copy-start | bytes 1572868
  1.8 15.3 %collective-permute-start.1 = (bf16[144,512]{1,0:T(8,128)(2,1)S(1)}, bf16[144,512]{1,0:T(8,128)(2,1)S(1)}, u32[]{:S(2)}, u32[]{:S(2)}) collective-permute-start(bf16[144,512]{1,0:T(8,128)(2,1)S(1)} %shard_map.64.own_ref), channel_id=1, source_target_pairs={{0,32},{32,0},{64,96},{96,64},{128,160},{160,128},{192,224},{224,1... | collective-permute-start | bytes 442376 | tf_op jit(solution)/shard_map/ppermute | solution.py:306
  5.9 14.3 %collective-permute-start = (bf16[144,512]{1,0:T(8,128)(2,1)S(1)}, bf16[144,512]{1,0:T(8,128)(2,1)S(1)}, u32[]{:S(2)}, u32[]{:S(2)}) collective-permute-start(bf16[144,512]{1,0:T(8,128)(2,1)S(1)} %shard_map.64.own_ref), channel_id=1, source_target_pairs={{32,64},{64,32},{96,128},{128,96},{160,192},{192,160},{224,256},{2... | collective-permute-start | bytes 442376 | tf_op jit(solution)/shard_map/ppermute | solution.py:306
  20.3 15.4 %collective-permute-start.3 = (bf16[432,512]{1,0:T(8,128)(2,1)S(1)}, bf16[432,512]{1,0:T(8,128)(2,1)S(1)}, u32[]{:S(2)}, u32[]{:S(2)}) collective-permute-start(bf16[432,512]{1,0:T(8,128)(2,1)S(1)} %shard_map.65), channel_id=1, source_target_pairs={{1,2},{2,1},{3,4},{4,3},{5,6},{6,5},{7,8},{8,7},{9,10},{10,9},{11,... | collective-permute-start | bytes 1327112 | tf_op jit(solution)/shard_map/ppermute | solution.py:306
  24.9 10.8 %collective-permute-start.2 = (bf16[432,512]{1,0:T(8,128)(2,1)S(1)}, bf16[432,512]{1,0:T(8,128)(2,1)S(1)}, u32[]{:S(2)}, u32[]{:S(2)}) collective-permute-start(bf16[432,512]{1,0:T(8,128)(2,1)S(1)} %shard_map.65), channel_id=1, source_target_pairs={{0,1},{1,0},{2,3},{3,2},{4,5},{5,4},{6,7},{7,6},{8,9},{9,8},{10,11... | collective-permute-start | bytes 1327112 | tf_op jit(solution)/shard_map/ppermute | solution.py:306

commit v3 on v2

--- a/solution.py
+++ b/solution.py
@@ -13,6 +13,7 @@
 EXTRA = 16
 WEIGHT, ROW, COL = 2, 5, 6
 UNROLL = 10
+BLOCKS = 4
 F32, BF16 = jnp.float32, jnp.bfloat16
 
 
@@ -79,14 +80,25 @@
     return [local[at : at + 1] for at in range(count)]
 
 
-def add_grams(gram_ref, payload, shifts, patches, centres, ensemble):
-    scalars = payload[ensemble:].astype(F32)
+def add_grams(gram_refs, payload, shifts, centres):
+    ensemble = payload.shape[0] - EXTRA
     spread = payload[:ensemble].astype(F32)
-    local = locals_of(scalars, *shifts, [centres[p] for p in patches])
+    local = locals_of(payload[ensemble:].astype(F32), *shifts, centres)
     weighted = jnp.concatenate([(row * spread).astype(BF16) for row in local], axis=0)
     part = lax.dot_general(weighted, payload, (((1,), (1,)), ((), ())), preferred_element_type=F32)
-    for at, p in enumerate(patches):
-        gram_ref[p] += part[at * ensemble : (at + 1) * ensemble]
+    for at, ref in enumerate(gram_refs):
+        ref[...] += part[at * ensemble : (at + 1) * ensemble]
+
+
+def add_column(gram_refs, column_ref, col_shift, centres, tile_rows):
+    payload = column_ref.shape[0] // BLOCKS
+    half = len(gram_refs) // 2
+    upper, lower = slice(0, half), slice(half, None)
+    blocks = [column_ref[at * payload : (at + 1) * payload, :] for at in range(BLOCKS)]
+    add_grams(gram_refs, blocks[0], (0.0, col_shift), centres)
+    add_grams(gram_refs[upper], blocks[1], (-tile_rows, col_shift), centres[upper])
+    add_grams(gram_refs[lower], blocks[2], (tile_rows, col_shift), centres[lower])
+    add_grams(gram_refs, blocks[3], (0.0, col_shift), centres)
 
 
 def double_dot(left, right):
@@ -156,65 +168,53 @@
     return (mean + jnp.dot(perturbation, transform, preferred_element_type=F32)).astype(BF16)
 
 
-def sides(parity_ref, span):
-    odd = parity_ref
-    near = 1 - odd
-    shift = (2 * near - 1).astype(F32) * span
-    return near, shift
+def sides(odd, cols):
+    last = cols // PATCH - 1
+    shift = (1 - 2 * odd).astype(F32) * cols
+    return (last * (1 - odd), last * odd), shift
 
 
 def centre_of(index):
     return jnp.asarray(2 * PATCH * index + PATCH, F32)
 
 
-def mid_kernel(parity_ref, own_ref, second_ref, first_ref, state_ref, out_ref, gram, half, z, right, transform):
-    ensemble = own_ref.shape[0] - EXTRA
-    rows, cols = state_ref.shape[0], state_ref.shape[1]
-    near, shift = sides(parity_ref[0], float(rows))
-    row_index = (near, 1 - near)
+def patch_at(r, c):
+    return pl.ds(r * PATCH, PATCH), pl.ds(pl.multiple_of(c * PATCH, PATCH), PATCH)
+
+
+def centres_of(columns):
+    return [(centre_of(r), centre_of(c)) for r in range(2) for c in columns]
+
+
+def mid_kernel(odd_ref, column_ref, state_ref, out_ref, part_ref, gram, half, z, right, transform):
+    rows, cols, ensemble = state_ref.shape
+    inner = (1, 2)
+    edge_columns, _ = sides(odd_ref[0], cols)
     gram[...] = jnp.zeros_like(gram)
-    inner = (1, 2)
-    centres = [(centre_of(r), centre_of(c)) for r in row_index for c in inner]
-    add_grams(gram, own_ref[...], (0.0, 0.0), (0, 1, 2, 3), centres, ensemble)
-    add_grams(gram, first_ref[...], (shift, 0.0), (0, 1), centres, ensemble)
-    add_grams(gram, second_ref[...], (-shift, 0.0), (2, 3), centres, ensemble)
+    part_ref[...] = jnp.zeros_like(part_ref)
+    refs = [ref.at[2 * r + at] for r in range(2) for ref in (gram, part_ref) for at in range(2)]
+    add_column(refs, column_ref, 0.0, centres_of(inner + edge_columns), float(rows))
     solve(gram, half, z, right, transform, ensemble)
     for p in range(4):
-        r, c = row_index[p // 2], inner[p % 2]
-        at = pl.ds(pl.multiple_of(r * PATCH, PATCH), PATCH)
-        cells = state_ref[at, c * PATCH : (c + 1) * PATCH, :].reshape(PATCH * PATCH, ensemble)
+        at, across = patch_at(p // 2, inner[p % 2])
+        cells = state_ref[at, across, :].reshape(PATCH * PATCH, ensemble)
         out = analyse(cells, transform[p]).reshape(PATCH, PATCH, ensemble)
-        out_ref[at, (c - 1) * PATCH : c * PATCH, :] = out
-
-
-def edge_kernel(
-    parity_ref, own_ref, second_ref, first_ref, near_ref, far_ref, state_ref, mid_ref, out_ref, gram, half, z, right, transform, done, semaphores
-):
-    payload = own_ref.shape[0]
-    ensemble = payload - EXTRA
-    rows, cols = state_ref.shape[0], state_ref.shape[1]
+        out_ref[at, pl.ds((p % 2) * PATCH, PATCH), :] = out
+
+
+def edge_kernel(odd_ref, near_ref, far_ref, state_ref, mid_ref, part_ref, out_ref, gram, half, z, right, transform, done, semaphores):
+    rows, cols, ensemble = state_ref.shape
     inner = pltpu.make_async_copy(mid_ref, out_ref.at[:, PATCH : cols - PATCH, :], semaphores.at[4])
     inner.start()
-    row_near, row_shift = sides(parity_ref[0], float(rows))
-    col_near, col_shift = sides(parity_ref[1], float(cols))
-    last = cols // PATCH - 1
-    row_index = (row_near, 1 - row_near)
-    col_index = (last * col_near, last * (1 - col_near))
-    gram[...] = jnp.zeros_like(gram)
-    centres = [(centre_of(r), centre_of(c)) for r in row_index for c in col_index]
-    add_grams(gram, own_ref[...], (0.0, 0.0), (0, 1, 2, 3), centres, ensemble)
-    add_grams(gram, first_ref[...], (row_shift, 0.0), (0, 1), centres, ensemble)
-    add_grams(gram, second_ref[...], (-row_shift, 0.0), (2, 3), centres, ensemble)
-    for at, (ref, shift) in enumerate(((near_ref, col_shift), (far_ref, -col_shift))):
-        add_grams(gram, ref[:payload], (0.0, shift), (at, 2 + at), centres, ensemble)
-        add_grams(gram, ref[payload : 2 * payload], (row_shift, shift), (at,), centres, ensemble)
-        add_grams(gram, ref[2 * payload :], (-row_shift, shift), (2 + at,), centres, ensemble)
+    edge_columns, shift = sides(odd_ref[0], cols)
+    gram[...] = part_ref[...]
+    for at, (ref, col_shift) in enumerate(((near_ref, shift), (far_ref, -shift))):
+        refs = [gram.at[at], gram.at[2 + at]]
+        add_column(refs, ref, col_shift, centres_of(edge_columns[at : at + 1]), float(rows))
     solve(gram, half, z, right, transform, ensemble)
     copies = []
     for p in range(4):
-        r, c = row_index[p // 2], col_index[p % 2]
-        at = pl.ds(pl.multiple_of(r * PATCH, PATCH), PATCH)
-        across = pl.ds(pl.multiple_of(c * PATCH, PATCH), PATCH)
+        at, across = patch_at(p // 2, edge_columns[p % 2])
         cells = state_ref[at, across, :].reshape(PATCH * PATCH, ensemble)
         done[p] = analyse(cells, transform[p]).reshape(PATCH, PATCH, ensemble)
         copies.append(pltpu.make_async_copy(done.at[p], out_ref.at[at, across, :], semaphores.at[p]))
@@ -253,63 +253,86 @@
     )(counts, *given)
 
 
-def stack_kernel(own_ref, second_ref, first_ref, out_ref):
-    rows = own_ref.shape[0]
-    for at, ref in enumerate((own_ref, first_ref, second_ref)):
-        out_ref[at * rows : (at + 1) * rows, :] = ref[...]
-
-
-def stack(own, first, second):
+def stack_kernel(own_ref, south_ref, north_ref, out_ref, *, tile_rows):
+    rows, capacity = own_ref.shape
+    kept = capacity // 2
+    ensemble = rows - EXTRA
+    tiles = (own_ref, north_ref, south_ref)
+    for at, ref in enumerate(tiles):
+        out_ref[at * rows : (at + 1) * rows, :] = ref[:, :kept]
+    full = [
+        jnp.max(ref[ensemble:, kept:].astype(F32)[WEIGHT : WEIGHT + 1], axis=1, keepdims=True) > 0.0 for ref in tiles[:2]
+    ]
+
+    def chosen(own, north, south):
+        return jnp.where(full[0], own, jnp.where(full[1], north, south))
+
+    spreads = [ref[:ensemble, kept:].astype(F32) for ref in tiles]
+    scalars = [ref[ensemble:, kept:].astype(F32) for ref in tiles]
+    index = lax.broadcasted_iota(jnp.int32, (EXTRA, kept), 0)
+    shift = chosen(0.0, -float(tile_rows), float(tile_rows))
+    out_ref[3 * rows : 3 * rows + ensemble, :] = chosen(*spreads).astype(BF16)
+    out_ref[3 * rows + ensemble :, :] = (chosen(*scalars) + jnp.where(index == ROW, shift, 0.0)).astype(BF16)
+
+
+def stack(own, north, south, tile_rows):
     rows, capacity = own.shape
     return pl.pallas_call(
-        stack_kernel,
-        out_shape=jax.ShapeDtypeStruct((3 * rows, capacity), BF16),
+        functools.partial(stack_kernel, tile_rows=tile_rows),
+        out_shape=pltpu.VMEM((BLOCKS * rows, capacity // 2), BF16),
         in_specs=vmem(3),
         out_specs=pl.BlockSpec(memory_space=pltpu.VMEM),
         compiler_params=pltpu.CompilerParams(vmem_limit_bytes=4 << 20),
-    )(own, second, first)
-
-
-def middle(parity, own, first, second, state):
+    )(own, south, north)
+
+
+def middle(odd, column, state):
     rows, cols, ensemble = state.shape
     return pl.pallas_call(
         mid_kernel,
-        out_shape=jax.ShapeDtypeStruct((rows, cols - 2 * PATCH, ensemble), BF16),
-        in_specs=[SMEM] + vmem(4),
-        out_specs=pl.BlockSpec(memory_space=pltpu.VMEM),
+        out_shape=(
+            pltpu.VMEM((rows, cols - 2 * PATCH, ensemble), BF16),
+            pltpu.VMEM((4, ensemble, ensemble + EXTRA), F32),
+        ),
+        in_specs=[SMEM] + vmem(2),
+        out_specs=tuple(vmem(2)),
         scratch_shapes=scratch(ensemble),
         compiler_params=pltpu.CompilerParams(vmem_limit_bytes=12 << 20),
         cost_estimate=pl.CostEstimate(flops=1 << 32, bytes_accessed=1 << 20, transcendentals=0),
-    )(parity, own, second, first, state)
-
-
-def edges(parity, own, first, second, near, far, state, mid):
+    )(odd, column, state)
+
+
+def edges(odd, near, far, state, mid, part):
     ensemble = state.shape[-1]
     return pl.pallas_call(
         edge_kernel,
         out_shape=jax.ShapeDtypeStruct(state.shape, BF16),
-        in_specs=[SMEM] + vmem(7),
+        in_specs=[SMEM] + vmem(5),
         out_specs=pl.BlockSpec(memory_space=pltpu.HBM),
         scratch_shapes=scratch(ensemble)
         + [pltpu.VMEM((4, PATCH, PATCH, ensemble), BF16), pltpu.SemaphoreType.DMA((5,))],
         compiler_params=pltpu.CompilerParams(vmem_limit_bytes=12 << 20),
-    )(parity, own, second, first, near, far, state, mid)
-
-
-def exchange(x, axis, first, wrap):
+    )(odd, near, far, state, mid, part)
+
+
+def shifted(x, axis, step):
+    count = lax.axis_size(axis)
+    return lax.ppermute(x, axis, [(i, i + step) for i in range(count) if 0 <= i + step < count])
+
+
+def exchange(x, axis, first):
     count = lax.axis_size(axis)
     pairs = []
     for low in range(first, count, 2):
         high = (low + 1) % count
-        if high > low or wrap:
-            pairs += [(low, high), (high, low)]
+        pairs += [(low, high), (high, low)]
     return lax.ppermute(x, axis, pairs)
 
 
 def body(state, obs_members, obs_values, obs_precision, obs_cells, obs_counts):
     _, tile_rows, tile_cols, ensemble = state.shape
     capacity = obs_members.shape[2]
-    parity = jnp.stack([lax.axis_index("lat") % 2, lax.axis_index("lon") % 2]).astype(jnp.int32)
+    odd = (lax.axis_index("lon") & 1).astype(jnp.int32).reshape(1)
     own = pack(
         obs_members.reshape(capacity, ensemble),
         obs_values.reshape(1, capacity),
@@ -318,14 +341,14 @@
         obs_counts,
         tile_cols,
     )
-    first = exchange(own, "lat", 0, False)
-    second = exchange(own, "lat", 1, False)
-    column = stack(own, first, second)
-    far = exchange(column, "lon", 1, True)
-    near = exchange(column, "lon", 0, True)
+    north = shifted(own, "lat", 1)
+    south = shifted(own, "lat", -1)
+    column = stack(own, north, south, tile_rows)
+    far = exchange(column, "lon", 1)
+    near = exchange(column, "lon", 0)
     cells = state.reshape(tile_rows, tile_cols, ensemble)
-    mid = middle(parity, own, first, second, cells)
-    out = edges(parity, own, first, second, near, far, cells, mid)
+    mid, part = middle(odd, column, cells)
+    out = edges(odd, near, far, cells, mid, part)
     return out.reshape(state.shape)
 
 

time: 42.3 us -> 40.7 us (0.962)
  Pallas kernels: 12.8 us -> 11.8 us
  waiting for transfers between devices: 3.22 us -> 2.49 us
    ppermute x0 -> x2, starting transfers between devices: none -> 14.8 us  [shifted(): lax.ppermute(x, axis, [(i, i + step) for i in range(count) if 0 <= i + st...]
    ppermute x4 -> x2, starting transfers between devices: 25.2 us -> 10.6 us  [exchange(): return lax.ppermute(x, axis, pairs)]
    ppermute x4 -> x2, waiting for transfers between devices: 3.22 us -> 0.01 us  [exchange(): return lax.ppermute(x, axis, pairs)]
    ppermute x0 -> x2, waiting for transfers between devices: none -> 2.49 us  [shifted(): lax.ppermute(x, axis, [(i, i + step) for i in range(count) if 0 <= i + st...]
    pallas_call x1, Pallas kernels: 6.37 us -> 5.46 us  [edges(): pl.pallas_call(edge_kernel, out_shape=jax.ShapeDtypeStruct(state.shape, B...]
  transfers between devices with their start and end apart: 4 -> 4, of which waited for: 1 -> 2; matrix products, arithmetic and copies ran while one was open for 0% -> 0% of each run, Pallas kernels for 13% -> 13%
where the time goes in v3:
time: 40.7 us; the launch traced here: 40.5 us
  starting transfers between devices  25.4 us (62%)
  Pallas kernels  11.8 us (29%)
  waiting for transfers between devices  2.49 us (6%)
  between operations  0.79 us (2%)
    ppermute x2, starting transfers between devices, shifted(): lax.ppermute(x, axis, [(i, i + step) for i in range(count) if 0 <= i + st...  14.8 us
    ppermute x2, starting transfers between devices, exchange(): return lax.ppermute(x, axis, pairs)  10.6 us
    pallas_call x1, Pallas kernels, edges(): pl.pallas_call(edge_kernel, out_shape=jax.ShapeDtypeStruct(state.shape, B...  5.46 us
    pallas_call x1, Pallas kernels, middle(): pl.pallas_call(mid_kernel, out_shape=(pltpu.VMEM((rows, cols - 2 * PATCH,...  5.19 us
    ppermute x2, waiting for transfers between devices, shifted(): lax.ppermute(x, axis, [(i, i + step) for i in range(count) if 0 <= i + st...  2.49 us
    pallas_call x1, Pallas kernels, pack(): pl.pallas_call(functools.partial(pack_kernel, tile_cols=tile_cols), out_s...  1.08 us
  transfers between devices with their start and end apart: 4, of which 2 were waited for; matrix products, arithmetic and copies ran while one was open for 0% of the time, Pallas kernels for 13%

profile of v3, /device:TPU:57, one launch (start us, length us, event | category | flops | bytes accessed | tf_op | source)
XLA Modules:
  0.0 40.5 jit_solution(11391877096619247262)
XLA Ops:
  0.0 0.0 copy-start
  0.7 1.1 %shard_map.64.own_ref = bf16[144,512]{1,0:T(8,128)(2,1)S(1)} custom-call(s32[1,1]{1,0:T(1,128)S(6)} %copy.7.count_ref, bf16[512,128]{1,0:T(8,128)(2,1)} %bitcast.9, f32[1,512]{1,0:T(1,128)} %bitcast.10, f32[1,512]{1,0:T(1,128)} %bitcast.11, s32[1,512]{1,0:T(1,128)} %bitcast.12), custom_call_target="tpu_custom_call" | custom-call | tf_op jit(solution)/shard_map/pallas_call | solution.py:246
  1.8 4.0 %collective-permute-start.1 = (bf16[144,512]{1,0:T(8,128)(2,1)S(1)}, bf16[144,512]{1,0:T(8,128)(2,1)S(1)}, u32[]{:S(2)}, u32[]{:S(2)}) collective-permute-start(bf16[144,512]{1,0:T(8,128)(2,1)S(1)} %shard_map.64.own_ref), channel_id=1, source_target_pairs={{0,32},{32,64},{64,96},{96,128},{128,160},{160,192},{192,224},{224... | collective-permute-start | bytes 442376 | tf_op jit(solution)/shard_map/ppermute | solution.py:320
  5.8 10.8 %collective-permute-start = (bf16[144,512]{1,0:T(8,128)(2,1)S(1)}, bf16[144,512]{1,0:T(8,128)(2,1)S(1)}, u32[]{:S(2)}, u32[]{:S(2)}) collective-permute-start(bf16[144,512]{1,0:T(8,128)(2,1)S(1)} %shard_map.64.own_ref), channel_id=1, source_target_pairs={{32,0},{64,32},{96,64},{128,96},{160,128},{192,160},{224,192},{256... | collective-permute-start | bytes 442376 | tf_op jit(solution)/shard_map/ppermute | solution.py:320
  16.7 1.6 %collective-permute-done.1.north_ref = bf16[144,512]{1,0:T(8,128)(2,1)S(1)} collective-permute-done((bf16[144,512]{1,0:T(8,128)(2,1)S(1)}, bf16[144,512]{1,0:T(8,128)(2,1)S(1)}, u32[]{:S(2)}, u32[]{:S(2)}) %collective-permute-start.1) | collective-permute-done | bytes 147488 | tf_op jit(solution)/shard_map/ppermute | solution.py:320
  18.3 0.9 %collective-permute-done.south_ref = bf16[144,512]{1,0:T(8,128)(2,1)S(1)} collective-permute-done((bf16[144,512]{1,0:T(8,128)(2,1)S(1)}, bf16[144,512]{1,0:T(8,128)(2,1)S(1)}, u32[]{:S(2)}, u32[]{:S(2)}) %collective-permute-start) | collective-permute-done | bytes 147488 | tf_op jit(solution)/shard_map/ppermute | solution.py:320
  19.1 0.1 shard_map.65.column_ref
  19.3 4.6 %collective-permute-start.3 = (bf16[576,256]{1,0:T(8,128)(2,1)S(1)}, bf16[576,256]{1,0:T(8,128)(2,1)S(1)}, u32[]{:S(2)}, u32[]{:S(2)}) collective-permute-start(bf16[576,256]{1,0:T(8,128)(2,1)S(1)} %shard_map.65.column_ref), channel_id=1, source_target_pairs={{1,2},{2,1},{3,4},{4,3},{5,6},{6,5},{7,8},{8,7},{9,10},{10,9},{11,... | collective-permute-start | bytes 884744 | tf_op jit(solution)/shard_map/ppermute | solution.py:329
  23.8 6.0 %collective-permute-start.2 = (bf16[576,256]{1,0:T(8,128)(2,1)S(1)}, bf16[576,256]{1,0:T(8,128)(2,1)S(1)}, u32[]{:S(2)}, u32[]{:S(2)}) collective-permute-start(bf16[576,256]{1,0:T(8,128)(2,1)S(1)} %shard_map.65.column_ref), channel_id=1, source_target_pairs={{0,1},{1,0},{2,3},{3,2},{4,5},{5,4},{6,7},{7,6},{8,9},{9,8},{10,11... | collective-permute-start | bytes 884744 | tf_op jit(solution)/shard_map/ppermute | solution.py:329
  29.8 0.0 copy-done
  29.8 5.2 %shard_map.66 = (bf16[32,32,128]{2,1,0:T(8,128)(2,1)S(1)}, f32[4,128,144]{2,1,0:T(8,128)S(1)}) custom-call(s32[1]{0:T(128)} %bitcast.odd_ref, bf16[576,256]{1,0:T(8,128)(2,1)S(1)} %shard_map.65.column_ref, bf16[32,64,128]{2,1,0:T(8,128)(2,1)S(1)} %bitcast.7), custom_call_target="tpu_custom_call" | custom-call | flops 4294967296 | bytes 1048576 | tf_op jit(solution)/shard_map/pallas_call | solution.py:291
  35.0 0.0 collective-permute-done.3.far_ref
  35.1 0.0 collective-permute-done.2.near_ref
  35.1 5.5 %shard_map.67 = bf16[32,64,128]{2,1,0:T(8,128)(2,1)} custom-call(s32[1]{0:T(128)} %bitcast.odd_ref, bf16[576,256]{1,0:T(8,128)(2,1)S(1)} %collective-permute-done.2.near_ref, bf16[576,256]{1,0:T(8,128)(2,1)S(1)} %collective-permute-done.3.far_ref, bf16[32,64,128]{2,1,0:T(8,128)(2,1)S(1)} %bitcast.8, bf16[32,32,128]{2,1,0:T(8,128)(2,1)S(1)} %get-tuple-element.7.mid_ref, ...), custom_call_target="tpu_custom_call" | custom-call | tf_op jit(solution)/shard_map/pallas_call | solution.py:307
Async XLA Ops:
  0.0 29.8 %copy-start = (bf16[1,32,64,128]{3,2,1,0:T(8,128)(2,1)S(1)}, bf16[1,32,64,128]{3,2,1,0:T(8,128)(2,1)}, u32[]{:S(2)}) copy-start(bf16[1,32,64,128]{3,2,1,0:T(8,128)(2,1)} %param.6) | copy-start | bytes 1572868
  1.8 16.5 %collective-permute-start.1 = (bf16[144,512]{1,0:T(8,128)(2,1)S(1)}, bf16[144,512]{1,0:T(8,128)(2,1)S(1)}, u32[]{:S(2)}, u32[]{:S(2)}) collective-permute-start(bf16[144,512]{1,0:T(8,128)(2,1)S(1)} %shard_map.64.own_ref), channel_id=1, source_target_pairs={{0,32},{32,64},{64,96},{96,128},{128,160},{160,192},{192,224},{224... | collective-permute-start | bytes 442376 | tf_op jit(solution)/shard_map/ppermute | solution.py:320
  5.8 13.3 %collective-permute-start = (bf16[144,512]{1,0:T(8,128)(2,1)S(1)}, bf16[144,512]{1,0:T(8,128)(2,1)S(1)}, u32[]{:S(2)}, u32[]{:S(2)}) collective-permute-start(bf16[144,512]{1,0:T(8,128)(2,1)S(1)} %shard_map.64.own_ref), channel_id=1, source_target_pairs={{32,0},{64,32},{96,64},{128,96},{160,128},{192,160},{224,192},{256... | collective-permute-start | bytes 442376 | tf_op jit(solution)/shard_map/ppermute | solution.py:320
  19.3 15.8 %collective-permute-start.3 = (bf16[576,256]{1,0:T(8,128)(2,1)S(1)}, bf16[576,256]{1,0:T(8,128)(2,1)S(1)}, u32[]{:S(2)}, u32[]{:S(2)}) collective-permute-start(bf16[576,256]{1,0:T(8,128)(2,1)S(1)} %shard_map.65.column_ref), channel_id=1, source_target_pairs={{1,2},{2,1},{3,4},{4,3},{5,6},{6,5},{7,8},{8,7},{9,10},{10,9},{11,... | collective-permute-start | bytes 884744 | tf_op jit(solution)/shard_map/ppermute | solution.py:329
  23.8 11.2 %collective-permute-start.2 = (bf16[576,256]{1,0:T(8,128)(2,1)S(1)}, bf16[576,256]{1,0:T(8,128)(2,1)S(1)}, u32[]{:S(2)}, u32[]{:S(2)}) collective-permute-start(bf16[576,256]{1,0:T(8,128)(2,1)S(1)} %shard_map.65.column_ref), channel_id=1, source_target_pairs={{0,1},{1,0},{2,3},{3,2},{4,5},{5,4},{6,7},{7,6},{8,9},{9,8},{10,11... | collective-permute-start | bytes 884744 | tf_op jit(solution)/shard_map/ppermute | solution.py:329

commit v4 on v3

--- a/solution.py
+++ b/solution.py
@@ -13,6 +13,7 @@
 EXTRA = 16
 WEIGHT, ROW, COL = 2, 5, 6
 UNROLL = 10
+INNER = (1, 2)
 BLOCKS = 4
 F32, BF16 = jnp.float32, jnp.bfloat16
 
@@ -90,12 +91,13 @@
         ref[...] += part[at * ensemble : (at + 1) * ensemble]
 
 
-def add_column(gram_refs, column_ref, col_shift, centres, tile_rows):
+def add_column(gram_refs, column_ref, col_shift, centres, tile_rows, own=True):
     payload = column_ref.shape[0] // BLOCKS
     half = len(gram_refs) // 2
     upper, lower = slice(0, half), slice(half, None)
     blocks = [column_ref[at * payload : (at + 1) * payload, :] for at in range(BLOCKS)]
-    add_grams(gram_refs, blocks[0], (0.0, col_shift), centres)
+    if own:
+        add_grams(gram_refs, blocks[0], (0.0, col_shift), centres)
     add_grams(gram_refs[upper], blocks[1], (-tile_rows, col_shift), centres[upper])
     add_grams(gram_refs[lower], blocks[2], (tile_rows, col_shift), centres[lower])
     add_grams(gram_refs, blocks[3], (0.0, col_shift), centres)
@@ -127,21 +129,31 @@
         across = jnp.sum(jnp.where(diagonal, column, 0.0), axis=0, keepdims=True)
         return jnp.sum(matrix * across, axis=1, keepdims=True)
 
+    def first(p, with_root):
+        right = right_ref[p]
+        if with_root:
+            z = z_ref[p]
+            both = double_dot(jnp.concatenate([right, side_by_side(z)], axis=0), right)
+            z_ref[p] = 1.5 * z + both[ensemble:]
+        else:
+            both = double_dot(right, right)
+        half_ref[p] = 1.5 * half_ref[p] + both[:ensemble]
+
+    def second(p):
+        middle = half_ref[p]
+        half = 1.5 * middle + double_dot(side_by_side(middle), right_ref[p])
+        half_ref[p] = half
+        right_ref[p] = side_by_side(half)
+
     def advance(with_root):
-        for p in patches:
-            right = right_ref[p]
-            if with_root:
-                z = z_ref[p]
-                both = double_dot(jnp.concatenate([right, side_by_side(z)], axis=0), right)
-                z_ref[p] = 1.5 * z + both[ensemble:]
-            else:
-                both = double_dot(right, right)
-            half_ref[p] = 1.5 * half_ref[p] + both[:ensemble]
-        for p in patches:
-            middle = half_ref[p]
-            half = 1.5 * middle + double_dot(side_by_side(middle), right_ref[p])
-            half_ref[p] = half
-            right_ref[p] = side_by_side(half)
+        split = len(patches) // 2
+        for p in patches[:split]:
+            first(p, with_root)
+        for p in patches[split:]:
+            first(p, with_root)
+            second(p - split)
+        for p in patches[split:]:
+            second(p)
 
     def step(_, carry):
         advance(True)
@@ -160,12 +172,11 @@
         transform_ref[p] = (z_ref[p] * scale + weights[p] / traces[p]).astype(BF16)
 
 
-def analyse(cells, transform):
+def centred(cells):
     ensemble = cells.shape[1]
     ones = jnp.full((ensemble, ensemble), 1.0 / ensemble, BF16)
     mean = jnp.dot(cells, ones, preferred_element_type=F32)
-    perturbation = (cells.astype(F32) - mean).astype(BF16)
-    return (mean + jnp.dot(perturbation, transform, preferred_element_type=F32)).astype(BF16)
+    return mean, (cells.astype(F32) - mean).astype(BF16)
 
 
 def sides(odd, cols):
@@ -186,28 +197,51 @@
     return [(centre_of(r), centre_of(c)) for r in range(2) for c in columns]
 
 
-def mid_kernel(odd_ref, column_ref, state_ref, out_ref, part_ref, gram, half, z, right, transform):
+def eight(ref):
+    return [ref.at[4 * edge + 2 * r + at] for r in range(2) for edge in range(2) for at in range(2)]
+
+
+def own_kernel(odd_ref, own_ref, state_ref, part_ref, mean_ref, perturbation_ref):
     rows, cols, ensemble = state_ref.shape
-    inner = (1, 2)
     edge_columns, _ = sides(odd_ref[0], cols)
-    gram[...] = jnp.zeros_like(gram)
     part_ref[...] = jnp.zeros_like(part_ref)
-    refs = [ref.at[2 * r + at] for r in range(2) for ref in (gram, part_ref) for at in range(2)]
-    add_column(refs, column_ref, 0.0, centres_of(inner + edge_columns), float(rows))
+    add_grams(eight(part_ref), own_ref[:, : own_ref.shape[1] // 2], (0.0, 0.0), centres_of(INNER + edge_columns))
+    for r in range(rows // 8):
+        at = slice(r * 8, (r + 1) * 8)
+        mean, perturbation = centred(state_ref[at].reshape(8 * cols, ensemble))
+        mean_ref[at] = mean.reshape(8, cols, ensemble)
+        perturbation_ref[at] = perturbation.reshape(8, cols, ensemble)
+
+
+def analyse(mean_ref, perturbation_ref, at, across, transform):
+    ensemble = transform.shape[0]
+    cells = perturbation_ref[at, across, :].reshape(PATCH * PATCH, ensemble)
+    change = jnp.dot(cells, transform, preferred_element_type=F32)
+    return (mean_ref[at, across, :] + change.reshape(PATCH, PATCH, ensemble)).astype(BF16)
+
+
+def mid_kernel(odd_ref, column_ref, part_ref, mean_ref, perturbation_ref, out_ref, edge_ref, gram, half, z, right, transform):
+    rows, cols, ensemble = mean_ref.shape
+    edge_columns, _ = sides(odd_ref[0], cols)
+    gram[...] = part_ref[:4]
+    edge_ref[...] = part_ref[4:]
+    refs = [ref.at[2 * r + at] for r in range(2) for ref in (gram, edge_ref) for at in range(2)]
+    add_column(refs, column_ref, 0.0, centres_of(INNER + edge_columns), float(rows), own=False)
     solve(gram, half, z, right, transform, ensemble)
     for p in range(4):
-        at, across = patch_at(p // 2, inner[p % 2])
-        cells = state_ref[at, across, :].reshape(PATCH * PATCH, ensemble)
-        out = analyse(cells, transform[p]).reshape(PATCH, PATCH, ensemble)
+        at, across = patch_at(p // 2, INNER[p % 2])
+        out = analyse(mean_ref, perturbation_ref, at, across, transform[p])
         out_ref[at, pl.ds((p % 2) * PATCH, PATCH), :] = out
 
 
-def edge_kernel(odd_ref, near_ref, far_ref, state_ref, mid_ref, part_ref, out_ref, gram, half, z, right, transform, done, semaphores):
-    rows, cols, ensemble = state_ref.shape
+def edge_kernel(
+    odd_ref, far_ref, near_ref, edge_ref, mean_ref, perturbation_ref, mid_ref, out_ref, gram, half, z, right, transform, done, semaphores
+):
+    rows, cols, ensemble = mean_ref.shape
     inner = pltpu.make_async_copy(mid_ref, out_ref.at[:, PATCH : cols - PATCH, :], semaphores.at[4])
     inner.start()
     edge_columns, shift = sides(odd_ref[0], cols)
-    gram[...] = part_ref[...]
+    gram[...] = edge_ref[...]
     for at, (ref, col_shift) in enumerate(((near_ref, shift), (far_ref, -shift))):
         refs = [gram.at[at], gram.at[2 + at]]
         add_column(refs, ref, col_shift, centres_of(edge_columns[at : at + 1]), float(rows))
@@ -215,8 +249,7 @@
     copies = []
     for p in range(4):
         at, across = patch_at(p // 2, edge_columns[p % 2])
-        cells = state_ref[at, across, :].reshape(PATCH * PATCH, ensemble)
-        done[p] = analyse(cells, transform[p]).reshape(PATCH, PATCH, ensemble)
+        done[p] = analyse(mean_ref, perturbation_ref, at, across, transform[p])
         copies.append(pltpu.make_async_copy(done.at[p], out_ref.at[at, across, :], semaphores.at[p]))
         copies[p].start()
     for copy in (inner, *copies):
@@ -253,7 +286,7 @@
     )(counts, *given)
 
 
-def stack_kernel(own_ref, south_ref, north_ref, out_ref, *, tile_rows):
+def stack_kernel(own_ref, north_ref, south_ref, out_ref, *, tile_rows):
     rows, capacity = own_ref.shape
     kept = capacity // 2
     ensemble = rows - EXTRA
@@ -283,36 +316,52 @@
         in_specs=vmem(3),
         out_specs=pl.BlockSpec(memory_space=pltpu.VMEM),
         compiler_params=pltpu.CompilerParams(vmem_limit_bytes=4 << 20),
-    )(own, south, north)
-
-
-def middle(odd, column, state):
+    )(own, north, south)
+
+
+def own_part(odd, own, state):
     rows, cols, ensemble = state.shape
+    return pl.pallas_call(
+        own_kernel,
+        out_shape=(
+            pltpu.VMEM((8, ensemble, ensemble + EXTRA), F32),
+            pltpu.VMEM(state.shape, F32),
+            pltpu.VMEM(state.shape, BF16),
+        ),
+        in_specs=[SMEM] + vmem(2),
+        out_specs=tuple(vmem(3)),
+        compiler_params=pltpu.CompilerParams(vmem_limit_bytes=12 << 20),
+        cost_estimate=pl.CostEstimate(flops=1 << 30, bytes_accessed=1 << 20, transcendentals=0),
+    )(odd, own, state)
+
+
+def middle(odd, column, part, mean, perturbation):
+    rows, cols, ensemble = mean.shape
     return pl.pallas_call(
         mid_kernel,
         out_shape=(
             pltpu.VMEM((rows, cols - 2 * PATCH, ensemble), BF16),
             pltpu.VMEM((4, ensemble, ensemble + EXTRA), F32),
         ),
-        in_specs=[SMEM] + vmem(2),
+        in_specs=[SMEM] + vmem(4),
         out_specs=tuple(vmem(2)),
         scratch_shapes=scratch(ensemble),
         compiler_params=pltpu.CompilerParams(vmem_limit_bytes=12 << 20),
         cost_estimate=pl.CostEstimate(flops=1 << 32, bytes_accessed=1 << 20, transcendentals=0),
-    )(odd, column, state)
-
-
-def edges(odd, near, far, state, mid, part):
-    ensemble = state.shape[-1]
+    )(odd, column, part, mean, perturbation)
+
+
+def edges(odd, near, far, edge, mean, perturbation, mid):
+    ensemble = mean.shape[-1]
     return pl.pallas_call(
         edge_kernel,
-        out_shape=jax.ShapeDtypeStruct(state.shape, BF16),
-        in_specs=[SMEM] + vmem(5),
+        out_shape=jax.ShapeDtypeStruct(mean.shape, BF16),
+        in_specs=[SMEM] + vmem(6),
         out_specs=pl.BlockSpec(memory_space=pltpu.HBM),
         scratch_shapes=scratch(ensemble)
         + [pltpu.VMEM((4, PATCH, PATCH, ensemble), BF16), pltpu.SemaphoreType.DMA((5,))],
         compiler_params=pltpu.CompilerParams(vmem_limit_bytes=12 << 20),
-    )(odd, near, far, state, mid, part)
+    )(odd, far, near, edge, mean, perturbation, mid)
 
 
 def shifted(x, axis, step):
@@ -346,9 +395,9 @@
     column = stack(own, north, south, tile_rows)
     far = exchange(column, "lon", 1)
     near = exchange(column, "lon", 0)
-    cells = state.reshape(tile_rows, tile_cols, ensemble)
-    mid, part = middle(odd, column, cells)
-    out = edges(odd, near, far, cells, mid, part)
+    part, mean, perturbation = own_part(odd, own, state.reshape(tile_rows, tile_cols, ensemble))
+    mid, edge = middle(odd, column, part, mean, perturbation)
+    out = edges(odd, near, far, edge, mean, perturbation, mid)
     return out.reshape(state.shape)
 
 

time: 40.7 us -> 39.9 us (0.980)
  waiting for transfers between devices: 2.49 us -> 1.01 us
  local copies, waits for them, and re-layouts: 0.01 us -> 1.04 us
    ppermute x2, waiting for transfers between devices: 2.49 us -> 1.01 us  [shifted(): lax.ppermute(x, axis, [(i, i + step) for i in range(count) if 0 <= i + st...]
    unnamed x2, local copies, waits for them, and re-layouts: 0.01 us -> 1.04 us
    pallas_call x1, Pallas kernels: 5.19 us -> 4.63 us  [middle(): pl.pallas_call(mid_kernel, out_shape=(pltpu.VMEM((rows, cols - 2 * PATCH,...]
    pallas_call x1 -> x2, Pallas kernels: 5.46 us -> 5.7 us  [the longest x1 5.27 us: edges(): pl.pallas_call(edge_kernel, out_shape=jax.ShapeDtypeStruct(mean.shape, BF...]
where the time goes in v4:
time: 39.9 us; the launch traced here: 39.7 us
  starting transfers between devices  25.4 us (64%)
  Pallas kernels  11.5 us (29%)
  local copies, waits for them, and re-layouts  1.04 us (3%)
  waiting for transfers between devices  1.01 us (3%)
  between operations  0.74 us (2%)
    ppermute x2, starting transfers between devices, shifted(): lax.ppermute(x, axis, [(i, i + step) for i in range(count) if 0 <= i + st...  14.8 us
    ppermute x2, starting transfers between devices, exchange(): return lax.ppermute(x, axis, pairs)  10.6 us
    pallas_call x1, Pallas kernels, edges(): pl.pallas_call(edge_kernel, out_shape=jax.ShapeDtypeStruct(mean.shape, BF...  5.27 us
    pallas_call x1, Pallas kernels, middle(): pl.pallas_call(mid_kernel, out_shape=(pltpu.VMEM((rows, cols - 2 * PATCH,...  4.63 us
    pallas_call x1, Pallas kernels, pack(): pl.pallas_call(functools.partial(pack_kernel, tile_cols=tile_cols), out_s...  1.08 us
    unnamed x2, local copies, waits for them, and re-layouts  1.04 us
    ppermute x2, waiting for transfers between devices, shifted(): lax.ppermute(x, axis, [(i, i + step) for i in range(count) if 0 <= i + st...  1.01 us
  transfers between devices with their start and end apart: 4, of which 2 were waited for; matrix products, arithmetic and copies ran while one was open for 0% of the time, Pallas kernels for 13%

profile of v4, /device:TPU:57, one launch (start us, length us, event | category | flops | bytes accessed | tf_op | source)
XLA Modules:
  0.0 39.7 jit_solution(15417179925662993898)
XLA Ops:
  0.7 1.1 %shard_map.64.own_ref = bf16[144,512]{1,0:T(8,128)(2,1)S(1)} custom-call(s32[1,1]{1,0:T(1,128)S(6)} %copy.7.count_ref, bf16[512,128]{1,0:T(8,128)(2,1)} %bitcast.8, f32[1,512]{1,0:T(1,128)} %bitcast.9, f32[1,512]{1,0:T(1,128)} %bitcast.10, s32[1,512]{1,0:T(1,128)} %bitcast.11), custom_call_target="tpu_custom_call" | custom-call | tf_op jit(solution)/shard_map/pallas_call | solution.py:279
  1.7 4.0 %collective-permute-start = (bf16[144,512]{1,0:T(8,128)(2,1)S(1)}, bf16[144,512]{1,0:T(8,128)(2,1)S(1)}, u32[]{:S(2)}, u32[]{:S(2)}) collective-permute-start(bf16[144,512]{1,0:T(8,128)(2,1)S(1)} %shard_map.64.own_ref), channel_id=1, source_target_pairs={{0,32},{32,64},{64,96},{96,128},{128,160},{160,192},{192,224},{224... | collective-permute-start | bytes 442376 | tf_op jit(solution)/shard_map/ppermute | solution.py:369
  5.7 10.8 %collective-permute-start.1 = (bf16[144,512]{1,0:T(8,128)(2,1)S(1)}, bf16[144,512]{1,0:T(8,128)(2,1)S(1)}, u32[]{:S(2)}, u32[]{:S(2)}) collective-permute-start(bf16[144,512]{1,0:T(8,128)(2,1)S(1)} %shard_map.64.own_ref), channel_id=1, source_target_pairs={{32,0},{64,32},{96,64},{128,96},{160,128},{192,160},{224,192},{256... | collective-permute-start | bytes 442376 | tf_op jit(solution)/shard_map/ppermute | solution.py:369
  16.6 0.0 copy-start
  16.6 1.0 %copy-done = bf16[1,32,64,128]{3,2,1,0:T(8,128)(2,1)S(1)} copy-done((bf16[1,32,64,128]{3,2,1,0:T(8,128)(2,1)S(1)}, bf16[1,32,64,128]{3,2,1,0:T(8,128)(2,1)}, u32[]{:S(2)}) %copy-start) | copy-done | bytes 524312
  17.6 0.4 %shard_map.66 = (f32[8,128,144]{2,1,0:T(8,128)S(1)}, f32[32,64,128]{2,1,0:T(8,128)S(1)}, bf16[32,64,128]{2,1,0:T(8,128)(2,1)S(1)}) custom-call(s32[1]{0:T(128)} %bitcast.odd_ref, bf16[144,512]{1,0:T(8,128)(2,1)S(1)} %shard_map.64.own_ref, bf16[32,64,128]{2,1,0:T(8,128)(2,1)S(1)} %bitcast.7), custom_call_target="tpu_custom_call" | custom-call | flops 1073741824 | bytes 1048576 | tf_op jit(solution)/shard_map/pallas_call | solution.py:324
  18.1 0.1 collective-permute-done.north_ref
  18.2 0.9 %collective-permute-done.1.south_ref = bf16[144,512]{1,0:T(8,128)(2,1)S(1)} collective-permute-done((bf16[144,512]{1,0:T(8,128)(2,1)S(1)}, bf16[144,512]{1,0:T(8,128)(2,1)S(1)}, u32[]{:S(2)}, u32[]{:S(2)}) %collective-permute-start.1) | collective-permute-done | bytes 147488 | tf_op jit(solution)/shard_map/ppermute | solution.py:369
  19.1 0.1 shard_map.65.column_ref
  19.2 4.6 %collective-permute-start.2 = (bf16[576,256]{1,0:T(8,128)(2,1)S(1)}, bf16[576,256]{1,0:T(8,128)(2,1)S(1)}, u32[]{:S(2)}, u32[]{:S(2)}) collective-permute-start(bf16[576,256]{1,0:T(8,128)(2,1)S(1)} %shard_map.65.column_ref), channel_id=1, source_target_pairs={{1,2},{2,1},{3,4},{4,3},{5,6},{6,5},{7,8},{8,7},{9,10},{10,9},{11,... | collective-permute-start | bytes 884744 | tf_op jit(solution)/shard_map/ppermute | solution.py:378
  23.7 6.0 %collective-permute-start.3 = (bf16[576,256]{1,0:T(8,128)(2,1)S(1)}, bf16[576,256]{1,0:T(8,128)(2,1)S(1)}, u32[]{:S(2)}, u32[]{:S(2)}) collective-permute-start(bf16[576,256]{1,0:T(8,128)(2,1)S(1)} %shard_map.65.column_ref), channel_id=1, source_target_pairs={{0,1},{1,0},{2,3},{3,2},{4,5},{5,4},{6,7},{7,6},{8,9},{9,8},{10,11... | collective-permute-start | bytes 884744 | tf_op jit(solution)/shard_map/ppermute | solution.py:378
  29.8 4.6 %shard_map.67 = (bf16[32,32,128]{2,1,0:T(8,128)(2,1)S(1)}, f32[4,128,144]{2,1,0:T(8,128)S(1)}) custom-call(s32[1]{0:T(128)} %bitcast.odd_ref, bf16[576,256]{1,0:T(8,128)(2,1)S(1)} %shard_map.65.column_ref, f32[8,128,144]{2,1,0:T(8,128)S(1)} %get-tuple-element.10.part_ref, f32[32,64,128]{2,1,0:T(8,128)S(1)} %get-tuple-element.11.mean_ref, ...), custom_call_target="tpu_custom_call" | custom-call | flops 4294967296 | bytes 1048576 | tf_op jit(solution)/shard_map/pallas_call | solution.py:340
  34.4 0.0 collective-permute-done.2.far_ref
  34.4 0.0 collective-permute-done.3.near_ref
  34.4 5.3 %shard_map.68 = bf16[32,64,128]{2,1,0:T(8,128)(2,1)} custom-call(s32[1]{0:T(128)} %bitcast.odd_ref, bf16[576,256]{1,0:T(8,128)(2,1)S(1)} %collective-permute-done.2.far_ref, bf16[576,256]{1,0:T(8,128)(2,1)S(1)} %collective-permute-done.3.near_ref, f32[4,128,144]{2,1,0:T(8,128)S(1)} %get-tuple-element.13.edge_ref, ...), custom_call_target="tpu_custom_call" | custom-call | tf_op jit(solution)/shard_map/pallas_call | solution.py:356
Async XLA Ops:
  1.7 16.5 %collective-permute-start = (bf16[144,512]{1,0:T(8,128)(2,1)S(1)}, bf16[144,512]{1,0:T(8,128)(2,1)S(1)}, u32[]{:S(2)}, u32[]{:S(2)}) collective-permute-start(bf16[144,512]{1,0:T(8,128)(2,1)S(1)} %shard_map.64.own_ref), channel_id=1, source_target_pairs={{0,32},{32,64},{64,96},{96,128},{128,160},{160,192},{192,224},{224... | collective-permute-start | bytes 442376 | tf_op jit(solution)/shard_map/ppermute | solution.py:369
  5.7 13.3 %collective-permute-start.1 = (bf16[144,512]{1,0:T(8,128)(2,1)S(1)}, bf16[144,512]{1,0:T(8,128)(2,1)S(1)}, u32[]{:S(2)}, u32[]{:S(2)}) collective-permute-start(bf16[144,512]{1,0:T(8,128)(2,1)S(1)} %shard_map.64.own_ref), channel_id=1, source_target_pairs={{32,0},{64,32},{96,64},{128,96},{160,128},{192,160},{224,192},{256... | collective-permute-start | bytes 442376 | tf_op jit(solution)/shard_map/ppermute | solution.py:369
  16.6 1.0 %copy-start = (bf16[1,32,64,128]{3,2,1,0:T(8,128)(2,1)S(1)}, bf16[1,32,64,128]{3,2,1,0:T(8,128)(2,1)}, u32[]{:S(2)}) copy-start(bf16[1,32,64,128]{3,2,1,0:T(8,128)(2,1)} %param.6) | copy-start | bytes 1572868
  19.2 15.2 %collective-permute-start.2 = (bf16[576,256]{1,0:T(8,128)(2,1)S(1)}, bf16[576,256]{1,0:T(8,128)(2,1)S(1)}, u32[]{:S(2)}, u32[]{:S(2)}) collective-permute-start(bf16[576,256]{1,0:T(8,128)(2,1)S(1)} %shard_map.65.column_ref), channel_id=1, source_target_pairs={{1,2},{2,1},{3,4},{4,3},{5,6},{6,5},{7,8},{8,7},{9,10},{10,9},{11,... | collective-permute-start | bytes 884744 | tf_op jit(solution)/shard_map/ppermute | solution.py:378
  23.7 10.7 %collective-permute-start.3 = (bf16[576,256]{1,0:T(8,128)(2,1)S(1)}, bf16[576,256]{1,0:T(8,128)(2,1)S(1)}, u32[]{:S(2)}, u32[]{:S(2)}) collective-permute-start(bf16[576,256]{1,0:T(8,128)(2,1)S(1)} %shard_map.65.column_ref), channel_id=1, source_target_pairs={{0,1},{1,0},{2,3},{3,2},{4,5},{5,4},{6,7},{7,6},{8,9},{9,8},{10,11... | collective-permute-start | bytes 884744 | tf_op jit(solution)/shard_map/ppermute | solution.py:378

commit v5 on v4

--- a/solution.py
+++ b/solution.py
@@ -286,37 +286,37 @@
     )(counts, *given)
 
 
-def stack_kernel(own_ref, north_ref, south_ref, out_ref, *, tile_rows):
+def stack_kernel(own_ref, north_ref, south_ref, late_ref, out_ref, *, tile_rows):
     rows, capacity = own_ref.shape
     kept = capacity // 2
     ensemble = rows - EXTRA
-    tiles = (own_ref, north_ref, south_ref)
-    for at, ref in enumerate(tiles):
-        out_ref[at * rows : (at + 1) * rows, :] = ref[:, :kept]
+    tiles = (own_ref[...], north_ref[...] + late_ref[...], south_ref[...])
+    for at, tile in enumerate(tiles):
+        out_ref[at * rows : (at + 1) * rows, :] = tile[:, :kept]
     full = [
-        jnp.max(ref[ensemble:, kept:].astype(F32)[WEIGHT : WEIGHT + 1], axis=1, keepdims=True) > 0.0 for ref in tiles[:2]
+        jnp.max(tile[ensemble:, kept:].astype(F32)[WEIGHT : WEIGHT + 1], axis=1, keepdims=True) > 0.0 for tile in tiles[:2]
     ]
 
     def chosen(own, north, south):
         return jnp.where(full[0], own, jnp.where(full[1], north, south))
 
-    spreads = [ref[:ensemble, kept:].astype(F32) for ref in tiles]
-    scalars = [ref[ensemble:, kept:].astype(F32) for ref in tiles]
+    spreads = [tile[:ensemble, kept:].astype(F32) for tile in tiles]
+    scalars = [tile[ensemble:, kept:].astype(F32) for tile in tiles]
     index = lax.broadcasted_iota(jnp.int32, (EXTRA, kept), 0)
     shift = chosen(0.0, -float(tile_rows), float(tile_rows))
     out_ref[3 * rows : 3 * rows + ensemble, :] = chosen(*spreads).astype(BF16)
     out_ref[3 * rows + ensemble :, :] = (chosen(*scalars) + jnp.where(index == ROW, shift, 0.0)).astype(BF16)
 
 
-def stack(own, north, south, tile_rows):
+def stack(own, north, south, late, tile_rows):
     rows, capacity = own.shape
     return pl.pallas_call(
         functools.partial(stack_kernel, tile_rows=tile_rows),
         out_shape=pltpu.VMEM((BLOCKS * rows, capacity // 2), BF16),
-        in_specs=vmem(3),
+        in_specs=vmem(4),
         out_specs=pl.BlockSpec(memory_space=pltpu.VMEM),
         compiler_params=pltpu.CompilerParams(vmem_limit_bytes=4 << 20),
-    )(own, north, south)
+    )(own, north, south, late)
 
 
 def own_part(odd, own, state):
@@ -364,9 +364,12 @@
     )(odd, far, near, edge, mean, perturbation, mid)
 
 
-def shifted(x, axis, step):
-    count = lax.axis_size(axis)
-    return lax.ppermute(x, axis, [(i, i + step) for i in range(count) if 0 <= i + step < count])
+def shifts(x):
+    count = lax.axis_size("lat")
+    upper = count // 2 - 1
+    southward = [(i, i + 1) for i in range(count - 1) if i + 1 != upper]
+    northward = [(i + 1, i) for i in range(count - 1)]
+    return [lax.ppermute(x, "lat", pairs) for pairs in (southward, northward, [(upper - 1, upper)])]
 
 
 def exchange(x, axis, first):
@@ -390,9 +393,7 @@
         obs_counts,
         tile_cols,
     )
-    north = shifted(own, "lat", 1)
-    south = shifted(own, "lat", -1)
-    column = stack(own, north, south, tile_rows)
+    column = stack(own, *shifts(own), tile_rows)
     far = exchange(column, "lon", 1)
     near = exchange(column, "lon", 0)
     part, mean, perturbation = own_part(odd, own, state.reshape(tile_rows, tile_cols, ensemble))

time: 39.9 us -> 39.3 us (0.985)
  waiting for transfers between devices: 1.01 us -> 0.33 us
    ppermute x2 -> x3, waiting for transfers between devices: 1.01 us -> 0.32 us  [shifts(): lax.ppermute(x, 'lat', pairs)]
    ppermute x2 -> x3, starting transfers between devices: 14.8 us -> 14.9 us  [shifts(): lax.ppermute(x, 'lat', pairs)]
  transfers between devices with their start and end apart: 4 -> 5, of which waited for: 2 -> 1; matrix products, arithmetic and copies ran while one was open for 0% -> 0% of each run, Pallas kernels for 13% -> 13%
where the time goes in v5:
time: 39.3 us; the launch traced here: 39.1 us
  starting transfers between devices  25.4 us (65%)
  Pallas kernels  11.5 us (29%)
  local copies, waits for them, and re-layouts  1.04 us (3%)
  between operations  0.75 us (2%)
    ppermute x3, starting transfers between devices, shifts(): lax.ppermute(x, 'lat', pairs)  14.9 us
    ppermute x2, starting transfers between devices, exchange(): return lax.ppermute(x, axis, pairs)  10.6 us
    pallas_call x1, Pallas kernels, edges(): pl.pallas_call(edge_kernel, out_shape=jax.ShapeDtypeStruct(mean.shape, BF...  5.27 us
    pallas_call x1, Pallas kernels, middle(): pl.pallas_call(mid_kernel, out_shape=(pltpu.VMEM((rows, cols - 2 * PATCH,...  4.63 us
    pallas_call x1, Pallas kernels, pack(): pl.pallas_call(functools.partial(pack_kernel, tile_cols=tile_cols), out_s...  1.08 us
    unnamed x2, local copies, waits for them, and re-layouts  1.04 us
  transfers between devices with their start and end apart: 5, of which 1 were waited for; matrix products, arithmetic and copies ran while one was open for 0% of the time, Pallas kernels for 13%

profile of v5, /device:TPU:57, one launch (start us, length us, event | category | flops | bytes accessed | tf_op | source)
XLA Modules:
  0.0 39.1 jit_solution(13374826035411239118)
XLA Ops:
  0.7 1.1 %shard_map.64.own_ref = bf16[144,512]{1,0:T(8,128)(2,1)S(1)} custom-call(s32[1,1]{1,0:T(1,128)S(6)} %copy.7.count_ref, bf16[512,128]{1,0:T(8,128)(2,1)} %bitcast.8, f32[1,512]{1,0:T(1,128)} %bitcast.9, f32[1,512]{1,0:T(1,128)} %bitcast.10, s32[1,512]{1,0:T(1,128)} %bitcast.11), custom_call_target="tpu_custom_call" | custom-call | tf_op jit(solution)/shard_map/pallas_call | solution.py:279
  1.7 4.0 %collective-permute-start = (bf16[144,512]{1,0:T(8,128)(2,1)S(1)}, bf16[144,512]{1,0:T(8,128)(2,1)S(1)}, u32[]{:S(2)}, u32[]{:S(2)}) collective-permute-start(bf16[144,512]{1,0:T(8,128)(2,1)S(1)} %shard_map.64.own_ref), channel_id=1, source_target_pairs={{0,32},{32,64},{64,96},{96,128},{128,160},{160,192},{224,256},{256... | collective-permute-start | bytes 442376 | tf_op jit(solution)/shard_map/ppermute | solution.py:372
  5.7 10.2 %collective-permute-start.1 = (bf16[144,512]{1,0:T(8,128)(2,1)S(1)}, bf16[144,512]{1,0:T(8,128)(2,1)S(1)}, u32[]{:S(2)}, u32[]{:S(2)}) collective-permute-start(bf16[144,512]{1,0:T(8,128)(2,1)S(1)} %shard_map.64.own_ref), channel_id=1, source_target_pairs={{32,0},{64,32},{96,64},{128,96},{160,128},{192,160},{224,192},{256... | collective-permute-start | bytes 442376 | tf_op jit(solution)/shard_map/ppermute | solution.py:372
  16.0 0.7 %collective-permute-start.2 = (bf16[144,512]{1,0:T(8,128)(2,1)S(1)}, bf16[144,512]{1,0:T(8,128)(2,1)S(1)}, u32[]{:S(2)}, u32[]{:S(2)}) collective-permute-start(bf16[144,512]{1,0:T(8,128)(2,1)S(1)} %shard_map.64.own_ref), channel_id=1, source_target_pairs={{192,224},{193,225},{194,226},{195,227},{196,228},{197,229},{198,2... | collective-permute-start | bytes 442376 | tf_op jit(solution)/shard_map/ppermute | solution.py:372
  16.6 0.0 copy-start
  16.7 1.0 %copy-done = bf16[1,32,64,128]{3,2,1,0:T(8,128)(2,1)S(1)} copy-done((bf16[1,32,64,128]{3,2,1,0:T(8,128)(2,1)S(1)}, bf16[1,32,64,128]{3,2,1,0:T(8,128)(2,1)}, u32[]{:S(2)}) %copy-start) | copy-done | bytes 524312
  17.7 0.4 %shard_map.66 = (f32[8,128,144]{2,1,0:T(8,128)S(1)}, f32[32,64,128]{2,1,0:T(8,128)S(1)}, bf16[32,64,128]{2,1,0:T(8,128)(2,1)S(1)}) custom-call(s32[1]{0:T(128)} %bitcast.odd_ref, bf16[144,512]{1,0:T(8,128)(2,1)S(1)} %shard_map.64.own_ref, bf16[32,64,128]{2,1,0:T(8,128)(2,1)S(1)} %bitcast.7), custom_call_target="tpu_custom_call" | custom-call | flops 1073741824 | bytes 1048576 | tf_op jit(solution)/shard_map/pallas_call | solution.py:324
  18.1 0.0 collective-permute-done.north_ref
  18.1 0.3 collective-permute-done.1.south_ref
  18.5 0.0 collective-permute-done.2.late_ref
  18.5 0.1 shard_map.65.column_ref
  18.6 4.6 %collective-permute-start.3 = (bf16[576,256]{1,0:T(8,128)(2,1)S(1)}, bf16[576,256]{1,0:T(8,128)(2,1)S(1)}, u32[]{:S(2)}, u32[]{:S(2)}) collective-permute-start(bf16[576,256]{1,0:T(8,128)(2,1)S(1)} %shard_map.65.column_ref), channel_id=1, source_target_pairs={{1,2},{2,1},{3,4},{4,3},{5,6},{6,5},{7,8},{8,7},{9,10},{10,9},{11,... | collective-permute-start | bytes 884744 | tf_op jit(solution)/shard_map/ppermute | solution.py:381
  23.1 6.0 %collective-permute-start.4 = (bf16[576,256]{1,0:T(8,128)(2,1)S(1)}, bf16[576,256]{1,0:T(8,128)(2,1)S(1)}, u32[]{:S(2)}, u32[]{:S(2)}) collective-permute-start(bf16[576,256]{1,0:T(8,128)(2,1)S(1)} %shard_map.65.column_ref), channel_id=1, source_target_pairs={{0,1},{1,0},{2,3},{3,2},{4,5},{5,4},{6,7},{7,6},{8,9},{9,8},{10,11... | collective-permute-start | bytes 884744 | tf_op jit(solution)/shard_map/ppermute | solution.py:381
  29.2 4.6 %shard_map.67 = (bf16[32,32,128]{2,1,0:T(8,128)(2,1)S(1)}, f32[4,128,144]{2,1,0:T(8,128)S(1)}) custom-call(s32[1]{0:T(128)} %bitcast.odd_ref, bf16[576,256]{1,0:T(8,128)(2,1)S(1)} %shard_map.65.column_ref, f32[8,128,144]{2,1,0:T(8,128)S(1)} %get-tuple-element.10.part_ref, f32[32,64,128]{2,1,0:T(8,128)S(1)} %get-tuple-element.11.mean_ref, ...), custom_call_target="tpu_custom_call" | custom-call | flops 4294967296 | bytes 1048576 | tf_op jit(solution)/shard_map/pallas_call | solution.py:340
  33.8 0.0 collective-permute-done.3.far_ref
  33.8 0.0 collective-permute-done.4.near_ref
  33.8 5.3 %shard_map.68 = bf16[32,64,128]{2,1,0:T(8,128)(2,1)} custom-call(s32[1]{0:T(128)} %bitcast.odd_ref, bf16[576,256]{1,0:T(8,128)(2,1)S(1)} %collective-permute-done.3.far_ref, bf16[576,256]{1,0:T(8,128)(2,1)S(1)} %collective-permute-done.4.near_ref, f32[4,128,144]{2,1,0:T(8,128)S(1)} %get-tuple-element.13.edge_ref, ...), custom_call_target="tpu_custom_call" | custom-call | tf_op jit(solution)/shard_map/pallas_call | solution.py:356
Async XLA Ops:
  1.7 16.4 %collective-permute-start = (bf16[144,512]{1,0:T(8,128)(2,1)S(1)}, bf16[144,512]{1,0:T(8,128)(2,1)S(1)}, u32[]{:S(2)}, u32[]{:S(2)}) collective-permute-start(bf16[144,512]{1,0:T(8,128)(2,1)S(1)} %shard_map.64.own_ref), channel_id=1, source_target_pairs={{0,32},{32,64},{64,96},{96,128},{128,160},{160,192},{224,256},{256... | collective-permute-start | bytes 442376 | tf_op jit(solution)/shard_map/ppermute | solution.py:372
  5.7 12.7 %collective-permute-start.1 = (bf16[144,512]{1,0:T(8,128)(2,1)S(1)}, bf16[144,512]{1,0:T(8,128)(2,1)S(1)}, u32[]{:S(2)}, u32[]{:S(2)}) collective-permute-start(bf16[144,512]{1,0:T(8,128)(2,1)S(1)} %shard_map.64.own_ref), channel_id=1, source_target_pairs={{32,0},{64,32},{96,64},{128,96},{160,128},{192,160},{224,192},{256... | collective-permute-start | bytes 442376 | tf_op jit(solution)/shard_map/ppermute | solution.py:372
  16.0 2.5 %collective-permute-start.2 = (bf16[144,512]{1,0:T(8,128)(2,1)S(1)}, bf16[144,512]{1,0:T(8,128)(2,1)S(1)}, u32[]{:S(2)}, u32[]{:S(2)}) collective-permute-start(bf16[144,512]{1,0:T(8,128)(2,1)S(1)} %shard_map.64.own_ref), channel_id=1, source_target_pairs={{192,224},{193,225},{194,226},{195,227},{196,228},{197,229},{198,2... | collective-permute-start | bytes 442376 | tf_op jit(solution)/shard_map/ppermute | solution.py:372
  16.6 1.0 %copy-start = (bf16[1,32,64,128]{3,2,1,0:T(8,128)(2,1)S(1)}, bf16[1,32,64,128]{3,2,1,0:T(8,128)(2,1)}, u32[]{:S(2)}) copy-start(bf16[1,32,64,128]{3,2,1,0:T(8,128)(2,1)} %param.6) | copy-start | bytes 1572868
  18.6 15.2 %collective-permute-start.3 = (bf16[576,256]{1,0:T(8,128)(2,1)S(1)}, bf16[576,256]{1,0:T(8,128)(2,1)S(1)}, u32[]{:S(2)}, u32[]{:S(2)}) collective-permute-start(bf16[576,256]{1,0:T(8,128)(2,1)S(1)} %shard_map.65.column_ref), channel_id=1, source_target_pairs={{1,2},{2,1},{3,4},{4,3},{5,6},{6,5},{7,8},{8,7},{9,10},{10,9},{11,... | collective-permute-start | bytes 884744 | tf_op jit(solution)/shard_map/ppermute | solution.py:381
  23.1 10.7 %collective-permute-start.4 = (bf16[576,256]{1,0:T(8,128)(2,1)S(1)}, bf16[576,256]{1,0:T(8,128)(2,1)S(1)}, u32[]{:S(2)}, u32[]{:S(2)}) collective-permute-start(bf16[576,256]{1,0:T(8,128)(2,1)S(1)} %shard_map.65.column_ref), channel_id=1, source_target_pairs={{0,1},{1,0},{2,3},{3,2},{4,5},{5,4},{6,7},{7,6},{8,9},{9,8},{10,11... | collective-permute-start | bytes 884744 | tf_op jit(solution)/shard_map/ppermute | solution.py:381

commit v6 on v5

--- a/solution.py
+++ b/solution.py
@@ -1,4 +1,5 @@
 import functools
+from typing import Any, NamedTuple
 
 import jax
 import jax.numpy as jnp
@@ -12,7 +13,7 @@
 RAD = 24
 EXTRA = 16
 WEIGHT, ROW, COL = 2, 5, 6
-UNROLL = 10
+EARLY_STEPS = 7
 INNER = (1, 2)
 BLOCKS = 4
 F32, BF16 = jnp.float32, jnp.bfloat16
@@ -109,67 +110,88 @@
     return both[:, :width] + both[:, width:]
 
 
-def solve(gram_ref, half_ref, z_ref, right_ref, transform_ref, ensemble):
-    patches = range(gram_ref.shape[0])
+class Patch(NamedTuple):
+    gram: Any
+    half: Any
+    z: Any
+    right: Any
+
+
+def patches_of(gram, half, z, right):
+    return [Patch(gram.at[p], half.at[p], z.at[p], right.at[p]) for p in range(half.shape[0])]
+
+
+def diagonal_of(ensemble):
     row = lax.broadcasted_iota(jnp.int32, (ensemble, ensemble), 0)
-    col = lax.broadcasted_iota(jnp.int32, (ensemble, ensemble), 1)
-    diagonal = row == col
-    traces = []
+    return row == lax.broadcasted_iota(jnp.int32, (ensemble, ensemble), 1)
+
+
+def system_of(patch):
+    ensemble = patch.half.shape[0]
+    diagonal = diagonal_of(ensemble)
+    system = patch.gram[:, :ensemble] + jnp.where(diagonal, ensemble - 1.0, 0.0)
+    on = jnp.where(diagonal, system, 0.0)
+    return system, jnp.sum(jnp.sum(on, axis=0, keepdims=True), axis=1, keepdims=True)
+
+
+def begin(patch):
+    system, trace = system_of(patch)
+    half = system * (-0.5 / trace)
+    patch.half[...] = half
+    patch.right[...] = side_by_side(half)
+    patch.z[...] = jnp.where(diagonal_of(half.shape[0]), 1.5, 0.0) + half
+
+
+def first(patch, with_root):
+    right = patch.right[...]
+    ensemble = right.shape[0]
+    if with_root:
+        z = patch.z[...]
+        both = double_dot(jnp.concatenate([right, side_by_side(z)], axis=0), right)
+        patch.z[...] = 1.5 * z + both[ensemble:]
+    else:
+        both = double_dot(right, right)
+    patch.half[...] = 1.5 * patch.half[...] + both[:ensemble]
+
+
+def second(patch):
+    middle = patch.half[...]
+    half = 1.5 * middle + double_dot(side_by_side(middle), patch.right[...])
+    patch.half[...] = half
+    patch.right[...] = side_by_side(half)
+
+
+def advance(some, others, with_root=(True, True)):
+    for p in some:
+        first(p, with_root[0])
+    for at in range(max(len(some), len(others))):
+        if at < len(others):
+            first(others[at], with_root[1])
+        if at < len(some):
+            second(some[at])
+    for p in others:
+        second(p)
+
+
+def finish(patches):
     for p in patches:
-        system = gram_ref[p, :, :ensemble] + jnp.where(diagonal, ensemble - 1.0, 0.0)
-        on = jnp.where(diagonal, system, 0.0)
-        trace = jnp.sum(jnp.sum(on, axis=0, keepdims=True), axis=1, keepdims=True)
-        traces.append(trace)
-        half = system * (-0.5 / trace)
-        half_ref[p] = half
-        right_ref[p] = side_by_side(half)
-        z_ref[p] = jnp.where(diagonal, 1.5, 0.0) + half
+        z = p.z[...]
+        p.z[...] = 1.5 * z + double_dot(side_by_side(z), p.right[...])
+    ensemble = patches[0].half.shape[0]
+    diagonal = diagonal_of(ensemble)
 
     def times(matrix, column):
         across = jnp.sum(jnp.where(diagonal, column, 0.0), axis=0, keepdims=True)
         return jnp.sum(matrix * across, axis=1, keepdims=True)
 
-    def first(p, with_root):
-        right = right_ref[p]
-        if with_root:
-            z = z_ref[p]
-            both = double_dot(jnp.concatenate([right, side_by_side(z)], axis=0), right)
-            z_ref[p] = 1.5 * z + both[ensemble:]
-        else:
-            both = double_dot(right, right)
-        half_ref[p] = 1.5 * half_ref[p] + both[:ensemble]
-
-    def second(p):
-        middle = half_ref[p]
-        half = 1.5 * middle + double_dot(side_by_side(middle), right_ref[p])
-        half_ref[p] = half
-        right_ref[p] = side_by_side(half)
-
-    def advance(with_root):
-        split = len(patches) // 2
-        for p in patches[:split]:
-            first(p, with_root)
-        for p in patches[split:]:
-            first(p, with_root)
-            second(p - split)
-        for p in patches[split:]:
-            second(p)
-
-    def step(_, carry):
-        advance(True)
-        return carry
-
-    advance(False)
-    lax.fori_loop(0, NS_STEPS - 2, step, 0, unroll=UNROLL)
-    for p in patches:
-        z = z_ref[p]
-        z_ref[p] = 1.5 * z + double_dot(side_by_side(z), right_ref[p])
-    pulls = [gram_ref[p, :, ensemble : ensemble + 1] + gram_ref[p, :, ensemble + 1 : ensemble + 2] for p in patches]
-    inner = [times(z_ref[p], pulls[p]) for p in patches]
-    weights = [times(z_ref[p], inner[p]) for p in patches]
-    for p in patches:
-        scale = jnp.sqrt((ensemble - 1.0) / traces[p])
-        transform_ref[p] = (z_ref[p] * scale + weights[p] / traces[p]).astype(BF16)
+    pulls = [p.gram[:, ensemble : ensemble + 1] + p.gram[:, ensemble + 1 : ensemble + 2] for p in patches]
+    inner = [times(p.z[...], pull) for p, pull in zip(patches, pulls)]
+    weights = [times(p.z[...], column) for p, column in zip(patches, inner)]
+    traces = [system_of(p)[1] for p in patches]
+    return [
+        (p.z[...] * jnp.sqrt((ensemble - 1.0) / trace) + weight / trace).astype(BF16)
+        for p, trace, weight in zip(patches, traces, weights)
+    ]
 
 
 def centred(cells):
@@ -220,39 +242,57 @@
     return (mean_ref[at, across, :] + change.reshape(PATCH, PATCH, ensemble)).astype(BF16)
 
 
-def mid_kernel(odd_ref, column_ref, part_ref, mean_ref, perturbation_ref, out_ref, edge_ref, gram, half, z, right, transform):
-    rows, cols, ensemble = mean_ref.shape
-    edge_columns, _ = sides(odd_ref[0], cols)
-    gram[...] = part_ref[:4]
-    edge_ref[...] = part_ref[4:]
-    refs = [ref.at[2 * r + at] for r in range(2) for ref in (gram, edge_ref) for at in range(2)]
-    add_column(refs, column_ref, 0.0, centres_of(INNER + edge_columns), float(rows), own=False)
-    solve(gram, half, z, right, transform, ensemble)
-    for p in range(4):
-        at, across = patch_at(p // 2, INNER[p % 2])
-        out = analyse(mean_ref, perturbation_ref, at, across, transform[p])
-        out_ref[at, pl.ds((p % 2) * PATCH, PATCH), :] = out
+def mid_kernel(odd_ref, column_ref, part_ref, gram, half, z, right, *, tile):
+    edge_columns, _ = sides(odd_ref[0], tile[1])
+    gram[...] = part_ref[...]
+    add_column(eight(gram), column_ref, 0.0, centres_of(INNER + edge_columns), float(tile[0]), own=False)
+    inner = patches_of(gram, half, z, right)
+    for p in inner:
+        begin(p)
+    advance(inner[:2], inner[2:], (False, False))
+    for _ in range(EARLY_STEPS):
+        advance(inner[:2], inner[2:])
 
 
 def edge_kernel(
-    odd_ref, far_ref, near_ref, edge_ref, mean_ref, perturbation_ref, mid_ref, out_ref, gram, half, z, right, transform, done, semaphores
+    odd_ref, far_ref, near_ref, gram_ref, half_ref, z_ref, mean_ref, perturbation_ref, out_ref, gram, half, z, right, done, semaphores
 ):
     rows, cols, ensemble = mean_ref.shape
-    inner = pltpu.make_async_copy(mid_ref, out_ref.at[:, PATCH : cols - PATCH, :], semaphores.at[4])
-    inner.start()
     edge_columns, shift = sides(odd_ref[0], cols)
-    gram[...] = edge_ref[...]
+    gram[...] = gram_ref[...]
+    half[:4] = half_ref[...]
+    z[:4] = z_ref[...]
+    patches = patches_of(gram, half, z, right)
+    inner, edge = patches[:4], patches[4:]
+    for p in inner:
+        p.right[...] = side_by_side(p.half[...])
     for at, (ref, col_shift) in enumerate(((near_ref, shift), (far_ref, -shift))):
-        refs = [gram.at[at], gram.at[2 + at]]
+        refs = [edge[at].gram, edge[2 + at].gram]
         add_column(refs, ref, col_shift, centres_of(edge_columns[at : at + 1]), float(rows))
-    solve(gram, half, z, right, transform, ensemble)
+    for p in edge:
+        begin(p)
+
     copies = []
-    for p in range(4):
-        at, across = patch_at(p // 2, edge_columns[p % 2])
-        done[p] = analyse(mean_ref, perturbation_ref, at, across, transform[p])
-        copies.append(pltpu.make_async_copy(done.at[p], out_ref.at[at, across, :], semaphores.at[p]))
-        copies[p].start()
-    for copy in (inner, *copies):
+
+    def put(transforms, columns):
+        for p, transform in enumerate(transforms):
+            at, across = patch_at(p // 2, columns[p % 2])
+            slot = len(copies)
+            done[slot] = analyse(mean_ref, perturbation_ref, at, across, transform)
+            copies.append(pltpu.make_async_copy(done.at[slot], out_ref.at[at, across, :], semaphores.at[slot]))
+            copies[slot].start()
+
+    left = NS_STEPS - 2 - EARLY_STEPS
+    for step in range(NS_STEPS - 1):
+        with_root = step > 0
+        if step < left:
+            advance(inner, edge, (True, with_root))
+        else:
+            advance(edge[:2], edge[2:], (with_root, with_root))
+        if step == left:
+            put(finish(inner), INNER)
+    put(finish(edge), edge_columns)
+    for copy in copies:
         copy.wait()
 
 
@@ -261,16 +301,6 @@
 
 
 SMEM = pl.BlockSpec(memory_space=pltpu.SMEM)
-
-
-def scratch(ensemble):
-    return [
-        pltpu.VMEM((4, ensemble, ensemble + EXTRA), F32),
-        pltpu.VMEM((4, ensemble, ensemble), F32),
-        pltpu.VMEM((4, ensemble, ensemble), F32),
-        pltpu.VMEM((4, ensemble, 2 * ensemble), BF16),
-        pltpu.VMEM((4, ensemble, ensemble), BF16),
-    ]
 
 
 def pack(members, values, precision, cells, counts, tile_cols):
@@ -335,33 +365,40 @@
     )(odd, own, state)
 
 
-def middle(odd, column, part, mean, perturbation):
-    rows, cols, ensemble = mean.shape
+def middle(odd, column, part, tile):
+    ensemble = part.shape[1]
     return pl.pallas_call(
-        mid_kernel,
+        functools.partial(mid_kernel, tile=tile),
         out_shape=(
-            pltpu.VMEM((rows, cols - 2 * PATCH, ensemble), BF16),
-            pltpu.VMEM((4, ensemble, ensemble + EXTRA), F32),
+            pltpu.VMEM(part.shape, F32),
+            pltpu.VMEM((4, ensemble, ensemble), F32),
+            pltpu.VMEM((4, ensemble, ensemble), F32),
         ),
-        in_specs=[SMEM] + vmem(4),
-        out_specs=tuple(vmem(2)),
-        scratch_shapes=scratch(ensemble),
+        in_specs=[SMEM] + vmem(2),
+        out_specs=tuple(vmem(3)),
+        scratch_shapes=[pltpu.VMEM((4, ensemble, 2 * ensemble), BF16)],
         compiler_params=pltpu.CompilerParams(vmem_limit_bytes=12 << 20),
         cost_estimate=pl.CostEstimate(flops=1 << 32, bytes_accessed=1 << 20, transcendentals=0),
-    )(odd, column, part, mean, perturbation)
-
-
-def edges(odd, near, far, edge, mean, perturbation, mid):
+    )(odd, column, part)
+
+
+def edges(odd, near, far, gram, half, z, mean, perturbation):
     ensemble = mean.shape[-1]
     return pl.pallas_call(
         edge_kernel,
         out_shape=jax.ShapeDtypeStruct(mean.shape, BF16),
-        in_specs=[SMEM] + vmem(6),
+        in_specs=[SMEM] + vmem(7),
         out_specs=pl.BlockSpec(memory_space=pltpu.HBM),
-        scratch_shapes=scratch(ensemble)
-        + [pltpu.VMEM((4, PATCH, PATCH, ensemble), BF16), pltpu.SemaphoreType.DMA((5,))],
+        scratch_shapes=[
+            pltpu.VMEM(gram.shape, F32),
+            pltpu.VMEM((8, ensemble, ensemble), F32),
+            pltpu.VMEM((8, ensemble, ensemble), F32),
+            pltpu.VMEM((8, ensemble, 2 * ensemble), BF16),
+            pltpu.VMEM((8, PATCH, PATCH, ensemble), BF16),
+            pltpu.SemaphoreType.DMA((8,)),
+        ],
         compiler_params=pltpu.CompilerParams(vmem_limit_bytes=12 << 20),
-    )(odd, far, near, edge, mean, perturbation, mid)
+    )(odd, far, near, gram, half, z, mean, perturbation)
 
 
 def shifts(x):
@@ -397,8 +434,8 @@
     far = exchange(column, "lon", 1)
     near = exchange(column, "lon", 0)
     part, mean, perturbation = own_part(odd, own, state.reshape(tile_rows, tile_cols, ensemble))
-    mid, edge = middle(odd, column, part, mean, perturbation)
-    out = edges(odd, near, far, edge, mean, perturbation, mid)
+    gram, half, z = middle(odd, column, part, (tile_rows, tile_cols))
+    out = edges(odd, near, far, gram, half, z, mean, perturbation)
     return out.reshape(state.shape)
 
 

time: 39.3 us -> 38.7 us (0.985)
  Pallas kernels: 11.5 us -> 10.9 us
    pallas_call x1, Pallas kernels: 4.63 us -> 3.21 us  [middle(): pl.pallas_call(functools.partial(mid_kernel, tile=tile), out_shape=(pltpu...]
    pallas_call x1, Pallas kernels: 5.27 us -> 6.06 us  [edges(): pl.pallas_call(edge_kernel, out_shape=jax.ShapeDtypeStruct(mean.shape, BF...]
  transfers between devices with their start and end apart: 5 -> 5, of which waited for: 1 -> 1; matrix products, arithmetic and copies ran while one was open for 0% -> 0% of each run, Pallas kernels for 13% -> 9%
where the time goes in v6:
time: 38.7 us; the launch traced here: 38.5 us
  starting transfers between devices  25.4 us (66%)
  Pallas kernels  10.9 us (28%)
  local copies, waits for them, and re-layouts  1.04 us (3%)
  between operations  0.75 us (2%)
    ppermute x3, starting transfers between devices, shifts(): lax.ppermute(x, 'lat', pairs)  14.9 us
    ppermute x2, starting transfers between devices, exchange(): return lax.ppermute(x, axis, pairs)  10.6 us
    pallas_call x1, Pallas kernels, edges(): pl.pallas_call(edge_kernel, out_shape=jax.ShapeDtypeStruct(mean.shape, BF...  6.06 us
    pallas_call x1, Pallas kernels, middle(): pl.pallas_call(functools.partial(mid_kernel, tile=tile), out_shape=(pltpu...  3.21 us
    pallas_call x1, Pallas kernels, pack(): pl.pallas_call(functools.partial(pack_kernel, tile_cols=tile_cols), out_s...  1.08 us
    unnamed x2, local copies, waits for them, and re-layouts  1.04 us
  transfers between devices with their start and end apart: 5, of which 1 were waited for; matrix products, arithmetic and copies ran while one was open for 0% of the time, Pallas kernels for 9%

profile of v6, /device:TPU:57, one launch (start us, length us, event | category | flops | bytes accessed | tf_op | source)
XLA Modules:
  0.0 38.5 jit_solution(15075187940611222752)
XLA Ops:
  0.7 1.1 %shard_map.64.own_ref = bf16[144,512]{1,0:T(8,128)(2,1)S(1)} custom-call(s32[1,1]{1,0:T(1,128)S(6)} %copy.7.count_ref, bf16[512,128]{1,0:T(8,128)(2,1)} %bitcast.8, f32[1,512]{1,0:T(1,128)} %bitcast.9, f32[1,512]{1,0:T(1,128)} %bitcast.10, s32[1,512]{1,0:T(1,128)} %bitcast.11), custom_call_target="tpu_custom_call" | custom-call | tf_op jit(solution)/shard_map/pallas_call | solution.py:309
  1.7 4.0 %collective-permute-start = (bf16[144,512]{1,0:T(8,128)(2,1)S(1)}, bf16[144,512]{1,0:T(8,128)(2,1)S(1)}, u32[]{:S(2)}, u32[]{:S(2)}) collective-permute-start(bf16[144,512]{1,0:T(8,128)(2,1)S(1)} %shard_map.64.own_ref), channel_id=1, source_target_pairs={{0,32},{32,64},{64,96},{96,128},{128,160},{160,192},{224,256},{256... | collective-permute-start | bytes 442376 | tf_op jit(solution)/shard_map/ppermute | solution.py:409
  5.7 10.2 %collective-permute-start.1 = (bf16[144,512]{1,0:T(8,128)(2,1)S(1)}, bf16[144,512]{1,0:T(8,128)(2,1)S(1)}, u32[]{:S(2)}, u32[]{:S(2)}) collective-permute-start(bf16[144,512]{1,0:T(8,128)(2,1)S(1)} %shard_map.64.own_ref), channel_id=1, source_target_pairs={{32,0},{64,32},{96,64},{128,96},{160,128},{192,160},{224,192},{256... | collective-permute-start | bytes 442376 | tf_op jit(solution)/shard_map/ppermute | solution.py:409
  16.0 0.7 %collective-permute-start.2 = (bf16[144,512]{1,0:T(8,128)(2,1)S(1)}, bf16[144,512]{1,0:T(8,128)(2,1)S(1)}, u32[]{:S(2)}, u32[]{:S(2)}) collective-permute-start(bf16[144,512]{1,0:T(8,128)(2,1)S(1)} %shard_map.64.own_ref), channel_id=1, source_target_pairs={{192,224},{193,225},{194,226},{195,227},{196,228},{197,229},{198,2... | collective-permute-start | bytes 442376 | tf_op jit(solution)/shard_map/ppermute | solution.py:409
  16.6 0.0 copy-start
  16.7 1.0 %copy-done = bf16[1,32,64,128]{3,2,1,0:T(8,128)(2,1)S(1)} copy-done((bf16[1,32,64,128]{3,2,1,0:T(8,128)(2,1)S(1)}, bf16[1,32,64,128]{3,2,1,0:T(8,128)(2,1)}, u32[]{:S(2)}) %copy-start) | copy-done | bytes 524312
  17.7 0.4 %shard_map.66 = (f32[8,128,144]{2,1,0:T(8,128)S(1)}, f32[32,64,128]{2,1,0:T(8,128)S(1)}, bf16[32,64,128]{2,1,0:T(8,128)(2,1)S(1)}) custom-call(s32[1]{0:T(128)} %bitcast.odd_ref, bf16[144,512]{1,0:T(8,128)(2,1)S(1)} %shard_map.64.own_ref, bf16[32,64,128]{2,1,0:T(8,128)(2,1)S(1)} %bitcast.7), custom_call_target="tpu_custom_call" | custom-call | flops 1073741824 | bytes 1048576 | tf_op jit(solution)/shard_map/pallas_call | solution.py:354
  18.1 0.0 collective-permute-done.north_ref
  18.1 0.3 collective-permute-done.1.south_ref
  18.5 0.0 collective-permute-done.2.late_ref
  18.5 0.1 shard_map.65.column_ref
  18.6 4.6 %collective-permute-start.3 = (bf16[576,256]{1,0:T(8,128)(2,1)S(1)}, bf16[576,256]{1,0:T(8,128)(2,1)S(1)}, u32[]{:S(2)}, u32[]{:S(2)}) collective-permute-start(bf16[576,256]{1,0:T(8,128)(2,1)S(1)} %shard_map.65.column_ref), channel_id=1, source_target_pairs={{1,2},{2,1},{3,4},{4,3},{5,6},{6,5},{7,8},{8,7},{9,10},{10,9},{11,... | collective-permute-start | bytes 884744 | tf_op jit(solution)/shard_map/ppermute | solution.py:418
  23.1 6.0 %collective-permute-start.4 = (bf16[576,256]{1,0:T(8,128)(2,1)S(1)}, bf16[576,256]{1,0:T(8,128)(2,1)S(1)}, u32[]{:S(2)}, u32[]{:S(2)}) collective-permute-start(bf16[576,256]{1,0:T(8,128)(2,1)S(1)} %shard_map.65.column_ref), channel_id=1, source_target_pairs={{0,1},{1,0},{2,3},{3,2},{4,5},{5,4},{6,7},{7,6},{8,9},{9,8},{10,11... | collective-permute-start | bytes 884744 | tf_op jit(solution)/shard_map/ppermute | solution.py:418
  29.2 3.2 %shard_map.67 = (f32[8,128,144]{2,1,0:T(8,128)S(1)}, f32[4,128,128]{2,1,0:T(8,128)S(1)}, f32[4,128,128]{2,1,0:T(8,128)S(1)}) custom-call(s32[1]{0:T(128)} %bitcast.odd_ref, bf16[576,256]{1,0:T(8,128)(2,1)S(1)} %shard_map.65.column_ref, f32[8,128,144]{2,1,0:T(8,128)S(1)} %get-tuple-element.11.part_ref), custom_call_target="tpu_custom_call" | custom-call | flops 4294967296 | bytes 1048576 | tf_op jit(solution)/shard_map/pallas_call | solution.py:370
  32.4 0.0 collective-permute-done.3.far_ref
  32.4 0.0 collective-permute-done.4.near_ref
  32.4 6.1 %shard_map.68 = bf16[32,64,128]{2,1,0:T(8,128)(2,1)} custom-call(s32[1]{0:T(128)} %bitcast.odd_ref, bf16[576,256]{1,0:T(8,128)(2,1)S(1)} %collective-permute-done.3.far_ref, bf16[576,256]{1,0:T(8,128)(2,1)S(1)} %collective-permute-done.4.near_ref, f32[8,128,144]{2,1,0:T(8,128)S(1)} %get-tuple-element.12.gram_ref, ...), custom_call_target="tpu_custom_call" | custom-call | tf_op jit(solution)/shard_map/pallas_call | solution.py:387
Async XLA Ops:
  1.7 16.4 %collective-permute-start = (bf16[144,512]{1,0:T(8,128)(2,1)S(1)}, bf16[144,512]{1,0:T(8,128)(2,1)S(1)}, u32[]{:S(2)}, u32[]{:S(2)}) collective-permute-start(bf16[144,512]{1,0:T(8,128)(2,1)S(1)} %shard_map.64.own_ref), channel_id=1, source_target_pairs={{0,32},{32,64},{64,96},{96,128},{128,160},{160,192},{224,256},{256... | collective-permute-start | bytes 442376 | tf_op jit(solution)/shard_map/ppermute | solution.py:409
  5.7 12.7 %collective-permute-start.1 = (bf16[144,512]{1,0:T(8,128)(2,1)S(1)}, bf16[144,512]{1,0:T(8,128)(2,1)S(1)}, u32[]{:S(2)}, u32[]{:S(2)}) collective-permute-start(bf16[144,512]{1,0:T(8,128)(2,1)S(1)} %shard_map.64.own_ref), channel_id=1, source_target_pairs={{32,0},{64,32},{96,64},{128,96},{160,128},{192,160},{224,192},{256... | collective-permute-start | bytes 442376 | tf_op jit(solution)/shard_map/ppermute | solution.py:409
  16.0 2.5 %collective-permute-start.2 = (bf16[144,512]{1,0:T(8,128)(2,1)S(1)}, bf16[144,512]{1,0:T(8,128)(2,1)S(1)}, u32[]{:S(2)}, u32[]{:S(2)}) collective-permute-start(bf16[144,512]{1,0:T(8,128)(2,1)S(1)} %shard_map.64.own_ref), channel_id=1, source_target_pairs={{192,224},{193,225},{194,226},{195,227},{196,228},{197,229},{198,2... | collective-permute-start | bytes 442376 | tf_op jit(solution)/shard_map/ppermute | solution.py:409
  16.6 1.0 %copy-start = (bf16[1,32,64,128]{3,2,1,0:T(8,128)(2,1)S(1)}, bf16[1,32,64,128]{3,2,1,0:T(8,128)(2,1)}, u32[]{:S(2)}) copy-start(bf16[1,32,64,128]{3,2,1,0:T(8,128)(2,1)} %param.6) | copy-start | bytes 1572868
  18.6 13.8 %collective-permute-start.3 = (bf16[576,256]{1,0:T(8,128)(2,1)S(1)}, bf16[576,256]{1,0:T(8,128)(2,1)S(1)}, u32[]{:S(2)}, u32[]{:S(2)}) collective-permute-start(bf16[576,256]{1,0:T(8,128)(2,1)S(1)} %shard_map.65.column_ref), channel_id=1, source_target_pairs={{1,2},{2,1},{3,4},{4,3},{5,6},{6,5},{7,8},{8,7},{9,10},{10,9},{11,... | collective-permute-start | bytes 884744 | tf_op jit(solution)/shard_map/ppermute | solution.py:418
  23.1 9.3 %collective-permute-start.4 = (bf16[576,256]{1,0:T(8,128)(2,1)S(1)}, bf16[576,256]{1,0:T(8,128)(2,1)S(1)}, u32[]{:S(2)}, u32[]{:S(2)}) collective-permute-start(bf16[576,256]{1,0:T(8,128)(2,1)S(1)} %shard_map.65.column_ref), channel_id=1, source_target_pairs={{0,1},{1,0},{2,3},{3,2},{4,5},{5,4},{6,7},{7,6},{8,9},{9,8},{10,11... | collective-permute-start | bytes 884744 | tf_op jit(solution)/shard_map/ppermute | solution.py:418

commit v7 on v6

--- a/solution.py
+++ b/solution.py
@@ -11,7 +11,7 @@
 PATCH = 16
 NS_STEPS = 12
 RAD = 24
-EXTRA = 16
+EXTRA = 8
 WEIGHT, ROW, COL = 2, 5, 6
 EARLY_STEPS = 7
 INNER = (1, 2)
@@ -82,26 +82,28 @@
     return [local[at : at + 1] for at in range(count)]
 
 
-def add_grams(gram_refs, payload, shifts, centres):
-    ensemble = payload.shape[0] - EXTRA
-    spread = payload[:ensemble].astype(F32)
-    local = locals_of(payload[ensemble:].astype(F32), *shifts, centres)
-    weighted = jnp.concatenate([(row * spread).astype(BF16) for row in local], axis=0)
-    part = lax.dot_general(weighted, payload, (((1,), (1,)), ((), ())), preferred_element_type=F32)
-    for at, ref in enumerate(gram_refs):
-        ref[...] += part[at * ensemble : (at + 1) * ensemble]
-
-
-def add_column(gram_refs, column_ref, col_shift, centres, tile_rows, own=True):
-    payload = column_ref.shape[0] // BLOCKS
-    half = len(gram_refs) // 2
-    upper, lower = slice(0, half), slice(half, None)
-    blocks = [column_ref[at * payload : (at + 1) * payload, :] for at in range(BLOCKS)]
-    if own:
-        add_grams(gram_refs, blocks[0], (0.0, col_shift), centres)
-    add_grams(gram_refs[upper], blocks[1], (-tile_rows, col_shift), centres[upper])
-    add_grams(gram_refs[lower], blocks[2], (tile_rows, col_shift), centres[lower])
-    add_grams(gram_refs, blocks[3], (0.0, col_shift), centres)
+def grams_of(blocks, shifts, centres):
+    ensemble = blocks[0].shape[0] - EXTRA
+    weighted = []
+    for payload, shift in zip(blocks, shifts):
+        spread = payload[:ensemble].astype(F32)
+        local = locals_of(payload[ensemble:].astype(F32), *shift, centres)
+        weighted.append(jnp.concatenate([(row * spread).astype(BF16) for row in local], axis=0))
+    left, right = jnp.concatenate(weighted, axis=1), jnp.concatenate(blocks, axis=1)
+    return lax.dot_general(left, right, (((1,), (1,)), ((), ())), preferred_element_type=F32)
+
+
+def add_column(pairs, column_ref, col_shift, centres, tile_rows, own=True):
+    ensemble = column_ref.shape[0] - EXTRA
+    kept = column_ref.shape[1] // BLOCKS
+    half = len(pairs) // 2
+    blocks = [column_ref[:, at * kept : (at + 1) * kept] for at in range(BLOCKS)]
+    for at, row_shift in ((0, -tile_rows), (1, tile_rows)):
+        here = slice(at * half, (at + 1) * half)
+        used = [(blocks[1 + at], row_shift), (blocks[3], 0.0)] + ([(blocks[0], 0.0)] if own else [])
+        part = grams_of([block for block, _ in used], [(shift, col_shift) for _, shift in used], centres[here])
+        for p, (given, out) in enumerate(pairs[here]):
+            out[...] = given[...] + part[p * ensemble : (p + 1) * ensemble]
 
 
 def double_dot(left, right):
@@ -140,6 +142,7 @@
     patch.half[...] = half
     patch.right[...] = side_by_side(half)
     patch.z[...] = jnp.where(diagonal_of(half.shape[0]), 1.5, 0.0) + half
+    return trace
 
 
 def first(patch, with_root):
@@ -173,7 +176,7 @@
         second(p)
 
 
-def finish(patches):
+def finish(patches, traces):
     for p in patches:
         z = p.z[...]
         p.z[...] = 1.5 * z + double_dot(side_by_side(z), p.right[...])
@@ -187,7 +190,6 @@
     pulls = [p.gram[:, ensemble : ensemble + 1] + p.gram[:, ensemble + 1 : ensemble + 2] for p in patches]
     inner = [times(p.z[...], pull) for p, pull in zip(patches, pulls)]
     weights = [times(p.z[...], column) for p, column in zip(patches, inner)]
-    traces = [system_of(p)[1] for p in patches]
     return [
         (p.z[...] * jnp.sqrt((ensemble - 1.0) / trace) + weight / trace).astype(BF16)
         for p, trace, weight in zip(patches, traces, weights)
@@ -226,8 +228,11 @@
 def own_kernel(odd_ref, own_ref, state_ref, part_ref, mean_ref, perturbation_ref):
     rows, cols, ensemble = state_ref.shape
     edge_columns, _ = sides(odd_ref[0], cols)
-    part_ref[...] = jnp.zeros_like(part_ref)
-    add_grams(eight(part_ref), own_ref[:, : own_ref.shape[1] // 2], (0.0, 0.0), centres_of(INNER + edge_columns))
+    ensemble = own_ref.shape[0] - EXTRA
+    block = own_ref[:, : own_ref.shape[1] // 2]
+    part = grams_of([block], [(0.0, 0.0)], centres_of(INNER + edge_columns))
+    for p, ref in enumerate(eight(part_ref)):
+        ref[...] = part[p * ensemble : (p + 1) * ensemble]
     for r in range(rows // 8):
         at = slice(r * 8, (r + 1) * 8)
         mean, perturbation = centred(state_ref[at].reshape(8 * cols, ensemble))
@@ -244,8 +249,7 @@
 
 def mid_kernel(odd_ref, column_ref, part_ref, gram, half, z, right, *, tile):
     edge_columns, _ = sides(odd_ref[0], tile[1])
-    gram[...] = part_ref[...]
-    add_column(eight(gram), column_ref, 0.0, centres_of(INNER + edge_columns), float(tile[0]), own=False)
+    add_column(list(zip(eight(part_ref), eight(gram))), column_ref, 0.0, centres_of(INNER + edge_columns), float(tile[0]), own=False)
     inner = patches_of(gram, half, z, right)
     for p in inner:
         begin(p)
@@ -259,18 +263,16 @@
 ):
     rows, cols, ensemble = mean_ref.shape
     edge_columns, shift = sides(odd_ref[0], cols)
-    gram[...] = gram_ref[...]
     half[:4] = half_ref[...]
     z[:4] = z_ref[...]
-    patches = patches_of(gram, half, z, right)
-    inner, edge = patches[:4], patches[4:]
+    inner = patches_of(gram_ref.at[:4], half.at[:4], z.at[:4], right.at[:4])
+    edge = patches_of(gram, half.at[4:], z.at[4:], right.at[4:])
     for p in inner:
         p.right[...] = side_by_side(p.half[...])
     for at, (ref, col_shift) in enumerate(((near_ref, shift), (far_ref, -shift))):
-        refs = [edge[at].gram, edge[2 + at].gram]
-        add_column(refs, ref, col_shift, centres_of(edge_columns[at : at + 1]), float(rows))
-    for p in edge:
-        begin(p)
+        pairs = [(gram_ref.at[4 + 2 * r + at], gram.at[2 * r + at]) for r in range(2)]
+        add_column(pairs, ref, col_shift, centres_of(edge_columns[at : at + 1]), float(rows))
+    traces = [begin(p) for p in edge]
 
     copies = []
 
@@ -290,8 +292,8 @@
         else:
             advance(edge[:2], edge[2:], (with_root, with_root))
         if step == left:
-            put(finish(inner), INNER)
-    put(finish(edge), edge_columns)
+            put(finish(inner, [system_of(p)[1] for p in inner]), INNER)
+    put(finish(edge, traces), edge_columns)
     for copy in copies:
         copy.wait()
 
@@ -322,7 +324,7 @@
     ensemble = rows - EXTRA
     tiles = (own_ref[...], north_ref[...] + late_ref[...], south_ref[...])
     for at, tile in enumerate(tiles):
-        out_ref[at * rows : (at + 1) * rows, :] = tile[:, :kept]
+        out_ref[:, at * kept : (at + 1) * kept] = tile[:, :kept]
     full = [
         jnp.max(tile[ensemble:, kept:].astype(F32)[WEIGHT : WEIGHT + 1], axis=1, keepdims=True) > 0.0 for tile in tiles[:2]
     ]
@@ -334,15 +336,15 @@
     scalars = [tile[ensemble:, kept:].astype(F32) for tile in tiles]
     index = lax.broadcasted_iota(jnp.int32, (EXTRA, kept), 0)
     shift = chosen(0.0, -float(tile_rows), float(tile_rows))
-    out_ref[3 * rows : 3 * rows + ensemble, :] = chosen(*spreads).astype(BF16)
-    out_ref[3 * rows + ensemble :, :] = (chosen(*scalars) + jnp.where(index == ROW, shift, 0.0)).astype(BF16)
+    out_ref[:ensemble, 3 * kept :] = chosen(*spreads).astype(BF16)
+    out_ref[ensemble:, 3 * kept :] = (chosen(*scalars) + jnp.where(index == ROW, shift, 0.0)).astype(BF16)
 
 
 def stack(own, north, south, late, tile_rows):
     rows, capacity = own.shape
     return pl.pallas_call(
         functools.partial(stack_kernel, tile_rows=tile_rows),
-        out_shape=pltpu.VMEM((BLOCKS * rows, capacity // 2), BF16),
+        out_shape=pltpu.VMEM((rows, BLOCKS * (capacity // 2)), BF16),
         in_specs=vmem(4),
         out_specs=pl.BlockSpec(memory_space=pltpu.VMEM),
         compiler_params=pltpu.CompilerParams(vmem_limit_bytes=4 << 20),
@@ -390,7 +392,7 @@
         in_specs=[SMEM] + vmem(7),
         out_specs=pl.BlockSpec(memory_space=pltpu.HBM),
         scratch_shapes=[
-            pltpu.VMEM(gram.shape, F32),
+            pltpu.VMEM((4, *gram.shape[1:]), F32),
             pltpu.VMEM((8, ensemble, ensemble), F32),
             pltpu.VMEM((8, ensemble, ensemble), F32),
             pltpu.VMEM((8, ensemble, 2 * ensemble), BF16),

time: 38.7 us -> 38.2 us (0.987)
  no operation moved by 1% of the time
where the time goes in v7:
time: 38.2 us; the launch traced here: 38 us
  starting transfers between devices  25.3 us (66%)
  Pallas kernels  10.7 us (28%)
  local copies, waits for them, and re-layouts  1.04 us (3%)
  between operations  0.75 us (2%)
    ppermute x3, starting transfers between devices, shifts(): lax.ppermute(x, 'lat', pairs)  14.9 us
    ppermute x2, starting transfers between devices, exchange(): return lax.ppermute(x, axis, pairs)  10.4 us
    pallas_call x1, Pallas kernels, edges(): pl.pallas_call(edge_kernel, out_shape=jax.ShapeDtypeStruct(mean.shape, BF...  6 us
    pallas_call x1, Pallas kernels, middle(): pl.pallas_call(functools.partial(mid_kernel, tile=tile), out_shape=(pltpu...  3.12 us
    pallas_call x1, Pallas kernels, pack(): pl.pallas_call(functools.partial(pack_kernel, tile_cols=tile_cols), out_s...  1.08 us
    unnamed x2, local copies, waits for them, and re-layouts  1.04 us
  transfers between devices with their start and end apart: 5, of which 1 were waited for; matrix products, arithmetic and copies ran while one was open for 0% of the time, Pallas kernels for 9%

profile of v7, /device:TPU:57, one launch (start us, length us, event | category | flops | bytes accessed | tf_op | source)
XLA Modules:
  0.0 38.0 jit_solution(3385587041282026537)
XLA Ops:
  0.7 1.1 %shard_map.64.own_ref = bf16[136,512]{1,0:T(8,128)(2,1)S(1)} custom-call(s32[1,1]{1,0:T(1,128)S(6)} %copy.7.count_ref, bf16[512,128]{1,0:T(8,128)(2,1)} %bitcast.8, f32[1,512]{1,0:T(1,128)} %bitcast.9, f32[1,512]{1,0:T(1,128)} %bitcast.10, s32[1,512]{1,0:T(1,128)} %bitcast.11), custom_call_target="tpu_custom_call" | custom-call | tf_op jit(solution)/shard_map/pallas_call | solution.py:311
  1.7 4.0 %collective-permute-start = (bf16[136,512]{1,0:T(8,128)(2,1)S(1)}, bf16[136,512]{1,0:T(8,128)(2,1)S(1)}, u32[]{:S(2)}, u32[]{:S(2)}) collective-permute-start(bf16[136,512]{1,0:T(8,128)(2,1)S(1)} %shard_map.64.own_ref), channel_id=1, source_target_pairs={{0,32},{32,64},{64,96},{96,128},{128,160},{160,192},{224,256},{256... | collective-permute-start | bytes 417800 | tf_op jit(solution)/shard_map/ppermute | solution.py:411
  5.7 10.2 %collective-permute-start.1 = (bf16[136,512]{1,0:T(8,128)(2,1)S(1)}, bf16[136,512]{1,0:T(8,128)(2,1)S(1)}, u32[]{:S(2)}, u32[]{:S(2)}) collective-permute-start(bf16[136,512]{1,0:T(8,128)(2,1)S(1)} %shard_map.64.own_ref), channel_id=1, source_target_pairs={{32,0},{64,32},{96,64},{128,96},{160,128},{192,160},{224,192},{256... | collective-permute-start | bytes 417800 | tf_op jit(solution)/shard_map/ppermute | solution.py:411
  16.0 0.7 %collective-permute-start.2 = (bf16[136,512]{1,0:T(8,128)(2,1)S(1)}, bf16[136,512]{1,0:T(8,128)(2,1)S(1)}, u32[]{:S(2)}, u32[]{:S(2)}) collective-permute-start(bf16[136,512]{1,0:T(8,128)(2,1)S(1)} %shard_map.64.own_ref), channel_id=1, source_target_pairs={{192,224},{193,225},{194,226},{195,227},{196,228},{197,229},{198,2... | collective-permute-start | bytes 417800 | tf_op jit(solution)/shard_map/ppermute | solution.py:411
  16.6 0.0 copy-start
  16.7 1.0 %copy-done = bf16[1,32,64,128]{3,2,1,0:T(8,128)(2,1)S(1)} copy-done((bf16[1,32,64,128]{3,2,1,0:T(8,128)(2,1)S(1)}, bf16[1,32,64,128]{3,2,1,0:T(8,128)(2,1)}, u32[]{:S(2)}) %copy-start) | copy-done | bytes 524312
  17.7 0.4 %shard_map.66 = (f32[8,128,136]{2,1,0:T(8,128)S(1)}, f32[32,64,128]{2,1,0:T(8,128)S(1)}, bf16[32,64,128]{2,1,0:T(8,128)(2,1)S(1)}) custom-call(s32[1]{0:T(128)} %bitcast.odd_ref, bf16[136,512]{1,0:T(8,128)(2,1)S(1)} %shard_map.64.own_ref, bf16[32,64,128]{2,1,0:T(8,128)(2,1)S(1)} %bitcast.7), custom_call_target="tpu_custom_call" | custom-call | flops 1073741824 | bytes 1048576 | tf_op jit(solution)/shard_map/pallas_call | solution.py:356
  18.1 0.0 collective-permute-done.north_ref
  18.1 0.1 collective-permute-done.1.south_ref
  18.3 0.0 collective-permute-done.2.late_ref
  18.3 0.1 shard_map.65.column_ref
  18.4 4.6 %collective-permute-start.3 = (bf16[136,1024]{1,0:T(8,128)(2,1)S(1)}, bf16[136,1024]{1,0:T(8,128)(2,1)S(1)}, u32[]{:S(2)}, u32[]{:S(2)}) collective-permute-start(bf16[136,1024]{1,0:T(8,128)(2,1)S(1)} %shard_map.65.column_ref), channel_id=1, source_target_pairs={{1,2},{2,1},{3,4},{4,3},{5,6},{6,5},{7,8},{8,7},{9,10},{10,9},{11,... | collective-permute-start | bytes 835592 | tf_op jit(solution)/shard_map/ppermute | solution.py:420
  23.0 5.8 %collective-permute-start.4 = (bf16[136,1024]{1,0:T(8,128)(2,1)S(1)}, bf16[136,1024]{1,0:T(8,128)(2,1)S(1)}, u32[]{:S(2)}, u32[]{:S(2)}) collective-permute-start(bf16[136,1024]{1,0:T(8,128)(2,1)S(1)} %shard_map.65.column_ref), channel_id=1, source_target_pairs={{0,1},{1,0},{2,3},{3,2},{4,5},{5,4},{6,7},{7,6},{8,9},{9,8},{10,11... | collective-permute-start | bytes 835592 | tf_op jit(solution)/shard_map/ppermute | solution.py:420
  28.8 3.1 %shard_map.67 = (f32[8,128,136]{2,1,0:T(8,128)S(1)}, f32[4,128,128]{2,1,0:T(8,128)S(1)}, f32[4,128,128]{2,1,0:T(8,128)S(1)}) custom-call(s32[1]{0:T(128)} %bitcast.odd_ref, bf16[136,1024]{1,0:T(8,128)(2,1)S(1)} %shard_map.65.column_ref, f32[8,128,136]{2,1,0:T(8,128)S(1)} %get-tuple-element.11.part_ref), custom_call_target="tpu_custom_call" | custom-call | flops 4294967296 | bytes 1048576 | tf_op jit(solution)/shard_map/pallas_call | solution.py:372
  31.9 0.0 collective-permute-done.3.far_ref
  31.9 0.0 collective-permute-done.4.near_ref
  31.9 6.0 %shard_map.68 = bf16[32,64,128]{2,1,0:T(8,128)(2,1)} custom-call(s32[1]{0:T(128)} %bitcast.odd_ref, bf16[136,1024]{1,0:T(8,128)(2,1)S(1)} %collective-permute-done.3.far_ref, bf16[136,1024]{1,0:T(8,128)(2,1)S(1)} %collective-permute-done.4.near_ref, f32[8,128,136]{2,1,0:T(8,128)S(1)} %get-tuple-element.12.gram_ref, ...), custom_call_target="tpu_custom_call" | custom-call | tf_op jit(solution)/shard_map/pallas_call | solution.py:389
Async XLA Ops:
  1.7 16.4 %collective-permute-start = (bf16[136,512]{1,0:T(8,128)(2,1)S(1)}, bf16[136,512]{1,0:T(8,128)(2,1)S(1)}, u32[]{:S(2)}, u32[]{:S(2)}) collective-permute-start(bf16[136,512]{1,0:T(8,128)(2,1)S(1)} %shard_map.64.own_ref), channel_id=1, source_target_pairs={{0,32},{32,64},{64,96},{96,128},{128,160},{160,192},{224,256},{256... | collective-permute-start | bytes 417800 | tf_op jit(solution)/shard_map/ppermute | solution.py:411
  5.7 12.5 %collective-permute-start.1 = (bf16[136,512]{1,0:T(8,128)(2,1)S(1)}, bf16[136,512]{1,0:T(8,128)(2,1)S(1)}, u32[]{:S(2)}, u32[]{:S(2)}) collective-permute-start(bf16[136,512]{1,0:T(8,128)(2,1)S(1)} %shard_map.64.own_ref), channel_id=1, source_target_pairs={{32,0},{64,32},{96,64},{128,96},{160,128},{192,160},{224,192},{256... | collective-permute-start | bytes 417800 | tf_op jit(solution)/shard_map/ppermute | solution.py:411
  16.0 2.3 %collective-permute-start.2 = (bf16[136,512]{1,0:T(8,128)(2,1)S(1)}, bf16[136,512]{1,0:T(8,128)(2,1)S(1)}, u32[]{:S(2)}, u32[]{:S(2)}) collective-permute-start(bf16[136,512]{1,0:T(8,128)(2,1)S(1)} %shard_map.64.own_ref), channel_id=1, source_target_pairs={{192,224},{193,225},{194,226},{195,227},{196,228},{197,229},{198,2... | collective-permute-start | bytes 417800 | tf_op jit(solution)/shard_map/ppermute | solution.py:411
  16.6 1.0 %copy-start = (bf16[1,32,64,128]{3,2,1,0:T(8,128)(2,1)S(1)}, bf16[1,32,64,128]{3,2,1,0:T(8,128)(2,1)}, u32[]{:S(2)}) copy-start(bf16[1,32,64,128]{3,2,1,0:T(8,128)(2,1)} %param.6) | copy-start | bytes 1572868
  18.4 13.5 %collective-permute-start.3 = (bf16[136,1024]{1,0:T(8,128)(2,1)S(1)}, bf16[136,1024]{1,0:T(8,128)(2,1)S(1)}, u32[]{:S(2)}, u32[]{:S(2)}) collective-permute-start(bf16[136,1024]{1,0:T(8,128)(2,1)S(1)} %shard_map.65.column_ref), channel_id=1, source_target_pairs={{1,2},{2,1},{3,4},{4,3},{5,6},{6,5},{7,8},{8,7},{9,10},{10,9},{11,... | collective-permute-start | bytes 835592 | tf_op jit(solution)/shard_map/ppermute | solution.py:420
  23.0 9.0 %collective-permute-start.4 = (bf16[136,1024]{1,0:T(8,128)(2,1)S(1)}, bf16[136,1024]{1,0:T(8,128)(2,1)S(1)}, u32[]{:S(2)}, u32[]{:S(2)}) collective-permute-start(bf16[136,1024]{1,0:T(8,128)(2,1)S(1)} %shard_map.65.column_ref), channel_id=1, source_target_pairs={{0,1},{1,0},{2,3},{3,2},{4,5},{5,4},{6,7},{7,6},{8,9},{9,8},{10,11... | collective-permute-start | bytes 835592 | tf_op jit(solution)/shard_map/ppermute | solution.py:420

commit v8 on v7

--- a/solution.py
+++ b/solution.py
@@ -164,36 +164,48 @@
     patch.right[...] = side_by_side(half)
 
 
-def advance(some, others, with_root=(True, True)):
+def nothing():
+    pass
+
+
+def advance(some, others, with_root=(True, True), fill=iter(())):
     for p in some:
         first(p, with_root[0])
+    next(fill, nothing)()
     for at in range(max(len(some), len(others))):
         if at < len(others):
             first(others[at], with_root[1])
         if at < len(some):
             second(some[at])
+        next(fill, nothing)()
     for p in others:
         second(p)
 
 
-def finish(patches, traces):
-    for p in patches:
+def finish(patches, trace_of, put):
+    ensemble = patches[0].half.shape[0]
+    column = {}
+
+    def last(at):
+        p = patches[at]
         z = p.z[...]
         p.z[...] = 1.5 * z + double_dot(side_by_side(z), p.right[...])
-    ensemble = patches[0].half.shape[0]
-    diagonal = diagonal_of(ensemble)
-
-    def times(matrix, column):
-        across = jnp.sum(jnp.where(diagonal, column, 0.0), axis=0, keepdims=True)
-        return jnp.sum(matrix * across, axis=1, keepdims=True)
-
-    pulls = [p.gram[:, ensemble : ensemble + 1] + p.gram[:, ensemble + 1 : ensemble + 2] for p in patches]
-    inner = [times(p.z[...], pull) for p, pull in zip(patches, pulls)]
-    weights = [times(p.z[...], column) for p, column in zip(patches, inner)]
-    return [
-        (p.z[...] * jnp.sqrt((ensemble - 1.0) / trace) + weight / trace).astype(BF16)
-        for p, trace, weight in zip(patches, traces, weights)
-    ]
+
+    def times(at):
+        across = jnp.sum(jnp.where(diagonal_of(ensemble), column[at], 0.0), axis=0, keepdims=True)
+        column[at] = jnp.sum(patches[at].z[...] * across, axis=1, keepdims=True)
+
+    def once(at):
+        gram = patches[at].gram
+        column[at] = gram[:, ensemble : ensemble + 1] + gram[:, ensemble + 1 : ensemble + 2]
+        times(at)
+
+    def use(at):
+        trace = trace_of(at)
+        scale = jnp.sqrt((ensemble - 1.0) / trace)
+        put(at, (patches[at].z[...] * scale + column[at] / trace).astype(BF16))
+
+    return [functools.partial(piece, at) for piece in (last, once, times, use) for at in range(len(patches))]
 
 
 def centred(cells):
@@ -269,31 +281,35 @@
     edge = patches_of(gram, half.at[4:], z.at[4:], right.at[4:])
     for p in inner:
         p.right[...] = side_by_side(p.half[...])
+    columns = []
     for at, (ref, col_shift) in enumerate(((near_ref, shift), (far_ref, -shift))):
         pairs = [(gram_ref.at[4 + 2 * r + at], gram.at[2 * r + at]) for r in range(2)]
-        add_column(pairs, ref, col_shift, centres_of(edge_columns[at : at + 1]), float(rows))
+        here = centres_of(edge_columns[at : at + 1])
+        columns.append(functools.partial(add_column, pairs, ref, col_shift, here, float(rows)))
+    advance(inner[:2], inner[2:], fill=iter(columns))
     traces = [begin(p) for p in edge]
 
     copies = []
 
-    def put(transforms, columns):
-        for p, transform in enumerate(transforms):
-            at, across = patch_at(p // 2, columns[p % 2])
-            slot = len(copies)
-            done[slot] = analyse(mean_ref, perturbation_ref, at, across, transform)
-            copies.append(pltpu.make_async_copy(done.at[slot], out_ref.at[at, across, :], semaphores.at[slot]))
-            copies[slot].start()
-
-    left = NS_STEPS - 2 - EARLY_STEPS
+    def put(place, at, transform):
+        band, across = patch_at(at // 2, place[at % 2])
+        slot = len(copies)
+        done[slot] = analyse(mean_ref, perturbation_ref, band, across, transform)
+        copies.append(pltpu.make_async_copy(done.at[slot], out_ref.at[band, across, :], semaphores.at[slot]))
+        copies[slot].start()
+
+    left = NS_STEPS - 3 - EARLY_STEPS
+    pieces = iter(finish(inner, lambda at: system_of(inner[at])[1], functools.partial(put, INNER)))
     for step in range(NS_STEPS - 1):
         with_root = step > 0
         if step < left:
             advance(inner, edge, (True, with_root))
         else:
-            advance(edge[:2], edge[2:], (with_root, with_root))
-        if step == left:
-            put(finish(inner, [system_of(p)[1] for p in inner]), INNER)
-    put(finish(edge, traces), edge_columns)
+            advance(edge[:2], edge[2:], (with_root, with_root), pieces)
+    for piece in pieces:
+        piece()
+    for piece in finish(edge, lambda at: traces[at], functools.partial(put, edge_columns)):
+        piece()
     for copy in copies:
         copy.wait()
 

time: 38.2 us -> 38 us (level)
  no operation moved by 1% of the time
where the time goes in v8:
time: 38 us; the launch traced here: 37.7 us
  starting transfers between devices  25.3 us (67%)
  Pallas kernels  10.5 us (28%)
  local copies, waits for them, and re-layouts  1.04 us (3%)
  between operations  0.75 us (2%)
    ppermute x3, starting transfers between devices, shifts(): lax.ppermute(x, 'lat', pairs)  14.9 us
    ppermute x2, starting transfers between devices, exchange(): return lax.ppermute(x, axis, pairs)  10.4 us
    pallas_call x1, Pallas kernels, edges(): pl.pallas_call(edge_kernel, out_shape=jax.ShapeDtypeStruct(mean.shape, BF...  5.77 us
    pallas_call x1, Pallas kernels, middle(): pl.pallas_call(functools.partial(mid_kernel, tile=tile), out_shape=(pltpu...  3.12 us
    pallas_call x1, Pallas kernels, pack(): pl.pallas_call(functools.partial(pack_kernel, tile_cols=tile_cols), out_s...  1.08 us
    unnamed x2, local copies, waits for them, and re-layouts  1.04 us
  transfers between devices with their start and end apart: 5, of which 1 were waited for; matrix products, arithmetic and copies ran while one was open for 0% of the time, Pallas kernels for 9%

profile of v8, /device:TPU:57, one launch (start us, length us, event | category | flops | bytes accessed | tf_op | source)
XLA Modules:
  0.0 37.7 jit_solution(6825635531652326210)
XLA Ops:
  0.7 1.1 %shard_map.64.own_ref = bf16[136,512]{1,0:T(8,128)(2,1)S(1)} custom-call(s32[1,1]{1,0:T(1,128)S(6)} %copy.7.count_ref, bf16[512,128]{1,0:T(8,128)(2,1)} %bitcast.8, f32[1,512]{1,0:T(1,128)} %bitcast.9, f32[1,512]{1,0:T(1,128)} %bitcast.10, s32[1,512]{1,0:T(1,128)} %bitcast.11), custom_call_target="tpu_custom_call" | custom-call | tf_op jit(solution)/shard_map/pallas_call | solution.py:327
  1.7 4.0 %collective-permute-start = (bf16[136,512]{1,0:T(8,128)(2,1)S(1)}, bf16[136,512]{1,0:T(8,128)(2,1)S(1)}, u32[]{:S(2)}, u32[]{:S(2)}) collective-permute-start(bf16[136,512]{1,0:T(8,128)(2,1)S(1)} %shard_map.64.own_ref), channel_id=1, source_target_pairs={{0,32},{32,64},{64,96},{96,128},{128,160},{160,192},{224,256},{256... | collective-permute-start | bytes 417800 | tf_op jit(solution)/shard_map/ppermute | solution.py:427
  5.7 10.2 %collective-permute-start.1 = (bf16[136,512]{1,0:T(8,128)(2,1)S(1)}, bf16[136,512]{1,0:T(8,128)(2,1)S(1)}, u32[]{:S(2)}, u32[]{:S(2)}) collective-permute-start(bf16[136,512]{1,0:T(8,128)(2,1)S(1)} %shard_map.64.own_ref), channel_id=1, source_target_pairs={{32,0},{64,32},{96,64},{128,96},{160,128},{192,160},{224,192},{256... | collective-permute-start | bytes 417800 | tf_op jit(solution)/shard_map/ppermute | solution.py:427
  16.0 0.7 %collective-permute-start.2 = (bf16[136,512]{1,0:T(8,128)(2,1)S(1)}, bf16[136,512]{1,0:T(8,128)(2,1)S(1)}, u32[]{:S(2)}, u32[]{:S(2)}) collective-permute-start(bf16[136,512]{1,0:T(8,128)(2,1)S(1)} %shard_map.64.own_ref), channel_id=1, source_target_pairs={{192,224},{193,225},{194,226},{195,227},{196,228},{197,229},{198,2... | collective-permute-start | bytes 417800 | tf_op jit(solution)/shard_map/ppermute | solution.py:427
  16.6 0.0 copy-start
  16.7 1.0 %copy-done = bf16[1,32,64,128]{3,2,1,0:T(8,128)(2,1)S(1)} copy-done((bf16[1,32,64,128]{3,2,1,0:T(8,128)(2,1)S(1)}, bf16[1,32,64,128]{3,2,1,0:T(8,128)(2,1)}, u32[]{:S(2)}) %copy-start) | copy-done | bytes 524312
  17.7 0.4 %shard_map.66 = (f32[8,128,136]{2,1,0:T(8,128)S(1)}, f32[32,64,128]{2,1,0:T(8,128)S(1)}, bf16[32,64,128]{2,1,0:T(8,128)(2,1)S(1)}) custom-call(s32[1]{0:T(128)} %bitcast.odd_ref, bf16[136,512]{1,0:T(8,128)(2,1)S(1)} %shard_map.64.own_ref, bf16[32,64,128]{2,1,0:T(8,128)(2,1)S(1)} %bitcast.7), custom_call_target="tpu_custom_call" | custom-call | flops 1073741824 | bytes 1048576 | tf_op jit(solution)/shard_map/pallas_call | solution.py:372
  18.1 0.0 collective-permute-done.north_ref
  18.1 0.1 collective-permute-done.1.south_ref
  18.3 0.0 collective-permute-done.2.late_ref
  18.3 0.1 shard_map.65.column_ref
  18.4 4.6 %collective-permute-start.3 = (bf16[136,1024]{1,0:T(8,128)(2,1)S(1)}, bf16[136,1024]{1,0:T(8,128)(2,1)S(1)}, u32[]{:S(2)}, u32[]{:S(2)}) collective-permute-start(bf16[136,1024]{1,0:T(8,128)(2,1)S(1)} %shard_map.65.column_ref), channel_id=1, source_target_pairs={{1,2},{2,1},{3,4},{4,3},{5,6},{6,5},{7,8},{8,7},{9,10},{10,9},{11,... | collective-permute-start | bytes 835592 | tf_op jit(solution)/shard_map/ppermute | solution.py:436
  23.0 5.8 %collective-permute-start.4 = (bf16[136,1024]{1,0:T(8,128)(2,1)S(1)}, bf16[136,1024]{1,0:T(8,128)(2,1)S(1)}, u32[]{:S(2)}, u32[]{:S(2)}) collective-permute-start(bf16[136,1024]{1,0:T(8,128)(2,1)S(1)} %shard_map.65.column_ref), channel_id=1, source_target_pairs={{0,1},{1,0},{2,3},{3,2},{4,5},{5,4},{6,7},{7,6},{8,9},{9,8},{10,11... | collective-permute-start | bytes 835592 | tf_op jit(solution)/shard_map/ppermute | solution.py:436
  28.8 3.1 %shard_map.67 = (f32[8,128,136]{2,1,0:T(8,128)S(1)}, f32[4,128,128]{2,1,0:T(8,128)S(1)}, f32[4,128,128]{2,1,0:T(8,128)S(1)}) custom-call(s32[1]{0:T(128)} %bitcast.odd_ref, bf16[136,1024]{1,0:T(8,128)(2,1)S(1)} %shard_map.65.column_ref, f32[8,128,136]{2,1,0:T(8,128)S(1)} %get-tuple-element.11.part_ref), custom_call_target="tpu_custom_call" | custom-call | flops 4294967296 | bytes 1048576 | tf_op jit(solution)/shard_map/pallas_call | solution.py:388
  31.9 0.0 collective-permute-done.3.far_ref
  31.9 0.0 collective-permute-done.4.near_ref
  31.9 5.8 %shard_map.68 = bf16[32,64,128]{2,1,0:T(8,128)(2,1)} custom-call(s32[1]{0:T(128)} %bitcast.odd_ref, bf16[136,1024]{1,0:T(8,128)(2,1)S(1)} %collective-permute-done.3.far_ref, bf16[136,1024]{1,0:T(8,128)(2,1)S(1)} %collective-permute-done.4.near_ref, f32[8,128,136]{2,1,0:T(8,128)S(1)} %get-tuple-element.12.gram_ref, ...), custom_call_target="tpu_custom_call" | custom-call | tf_op jit(solution)/shard_map/pallas_call | solution.py:405
Async XLA Ops:
  1.7 16.4 %collective-permute-start = (bf16[136,512]{1,0:T(8,128)(2,1)S(1)}, bf16[136,512]{1,0:T(8,128)(2,1)S(1)}, u32[]{:S(2)}, u32[]{:S(2)}) collective-permute-start(bf16[136,512]{1,0:T(8,128)(2,1)S(1)} %shard_map.64.own_ref), channel_id=1, source_target_pairs={{0,32},{32,64},{64,96},{96,128},{128,160},{160,192},{224,256},{256... | collective-permute-start | bytes 417800 | tf_op jit(solution)/shard_map/ppermute | solution.py:427
  5.7 12.5 %collective-permute-start.1 = (bf16[136,512]{1,0:T(8,128)(2,1)S(1)}, bf16[136,512]{1,0:T(8,128)(2,1)S(1)}, u32[]{:S(2)}, u32[]{:S(2)}) collective-permute-start(bf16[136,512]{1,0:T(8,128)(2,1)S(1)} %shard_map.64.own_ref), channel_id=1, source_target_pairs={{32,0},{64,32},{96,64},{128,96},{160,128},{192,160},{224,192},{256... | collective-permute-start | bytes 417800 | tf_op jit(solution)/shard_map/ppermute | solution.py:427
  16.0 2.3 %collective-permute-start.2 = (bf16[136,512]{1,0:T(8,128)(2,1)S(1)}, bf16[136,512]{1,0:T(8,128)(2,1)S(1)}, u32[]{:S(2)}, u32[]{:S(2)}) collective-permute-start(bf16[136,512]{1,0:T(8,128)(2,1)S(1)} %shard_map.64.own_ref), channel_id=1, source_target_pairs={{192,224},{193,225},{194,226},{195,227},{196,228},{197,229},{198,2... | collective-permute-start | bytes 417800 | tf_op jit(solution)/shard_map/ppermute | solution.py:427
  16.6 1.0 %copy-start = (bf16[1,32,64,128]{3,2,1,0:T(8,128)(2,1)S(1)}, bf16[1,32,64,128]{3,2,1,0:T(8,128)(2,1)}, u32[]{:S(2)}) copy-start(bf16[1,32,64,128]{3,2,1,0:T(8,128)(2,1)} %param.6) | copy-start | bytes 1572868
  18.4 13.5 %collective-permute-start.3 = (bf16[136,1024]{1,0:T(8,128)(2,1)S(1)}, bf16[136,1024]{1,0:T(8,128)(2,1)S(1)}, u32[]{:S(2)}, u32[]{:S(2)}) collective-permute-start(bf16[136,1024]{1,0:T(8,128)(2,1)S(1)} %shard_map.65.column_ref), channel_id=1, source_target_pairs={{1,2},{2,1},{3,4},{4,3},{5,6},{6,5},{7,8},{8,7},{9,10},{10,9},{11,... | collective-permute-start | bytes 835592 | tf_op jit(solution)/shard_map/ppermute | solution.py:436
  23.0 9.0 %collective-permute-start.4 = (bf16[136,1024]{1,0:T(8,128)(2,1)S(1)}, bf16[136,1024]{1,0:T(8,128)(2,1)S(1)}, u32[]{:S(2)}, u32[]{:S(2)}) collective-permute-start(bf16[136,1024]{1,0:T(8,128)(2,1)S(1)} %shard_map.65.column_ref), channel_id=1, source_target_pairs={{0,1},{1,0},{2,3},{3,2},{4,5},{5,4},{6,7},{7,6},{8,9},{9,8},{10,11... | collective-permute-start | bytes 835592 | tf_op jit(solution)/shard_map/ppermute | solution.py:436

commit v9 on v8

--- a/solution.py
+++ b/solution.py
@@ -13,7 +13,7 @@
 RAD = 24
 EXTRA = 8
 WEIGHT, ROW, COL = 2, 5, 6
-EARLY_STEPS = 7
+EARLY_STEPS = 6
 INNER = (1, 2)
 BLOCKS = 4
 F32, BF16 = jnp.float32, jnp.bfloat16

time: 38 us -> 37.7 us (level)
  no operation moved by 1% of the time
where the time goes in v9:
time: 37.7 us; the launch traced here: 37.5 us
  starting transfers between devices  25.3 us (67%)
  Pallas kernels  10.3 us (27%)
  local copies, waits for them, and re-layouts  1.04 us (3%)
  between operations  0.75 us (2%)
    ppermute x3, starting transfers between devices, shifts(): lax.ppermute(x, 'lat', pairs)  14.9 us
    ppermute x2, starting transfers between devices, exchange(): return lax.ppermute(x, axis, pairs)  10.4 us
    pallas_call x1, Pallas kernels, edges(): pl.pallas_call(edge_kernel, out_shape=jax.ShapeDtypeStruct(mean.shape, BF...  5.85 us
    pallas_call x1, Pallas kernels, middle(): pl.pallas_call(functools.partial(mid_kernel, tile=tile), out_shape=(pltpu...  2.8 us
    pallas_call x1, Pallas kernels, pack(): pl.pallas_call(functools.partial(pack_kernel, tile_cols=tile_cols), out_s...  1.08 us
    unnamed x2, local copies, waits for them, and re-layouts  1.04 us
  transfers between devices with their start and end apart: 5, of which 1 were waited for; matrix products, arithmetic and copies ran while one was open for 0% of the time, Pallas kernels for 9%

profile of v9, /device:TPU:57, one launch (start us, length us, event | category | flops | bytes accessed | tf_op | source)
XLA Modules:
  0.0 37.5 jit_solution(9124754736079149186)
XLA Ops:
  0.7 1.1 %shard_map.64.own_ref = bf16[136,512]{1,0:T(8,128)(2,1)S(1)} custom-call(s32[1,1]{1,0:T(1,128)S(6)} %copy.7.count_ref, bf16[512,128]{1,0:T(8,128)(2,1)} %bitcast.8, f32[1,512]{1,0:T(1,128)} %bitcast.9, f32[1,512]{1,0:T(1,128)} %bitcast.10, s32[1,512]{1,0:T(1,128)} %bitcast.11), custom_call_target="tpu_custom_call" | custom-call | tf_op jit(solution)/shard_map/pallas_call | solution.py:327
  1.7 4.0 %collective-permute-start = (bf16[136,512]{1,0:T(8,128)(2,1)S(1)}, bf16[136,512]{1,0:T(8,128)(2,1)S(1)}, u32[]{:S(2)}, u32[]{:S(2)}) collective-permute-start(bf16[136,512]{1,0:T(8,128)(2,1)S(1)} %shard_map.64.own_ref), channel_id=1, source_target_pairs={{0,32},{32,64},{64,96},{96,128},{128,160},{160,192},{224,256},{256... | collective-permute-start | bytes 417800 | tf_op jit(solution)/shard_map/ppermute | solution.py:427
  5.7 10.2 %collective-permute-start.1 = (bf16[136,512]{1,0:T(8,128)(2,1)S(1)}, bf16[136,512]{1,0:T(8,128)(2,1)S(1)}, u32[]{:S(2)}, u32[]{:S(2)}) collective-permute-start(bf16[136,512]{1,0:T(8,128)(2,1)S(1)} %shard_map.64.own_ref), channel_id=1, source_target_pairs={{32,0},{64,32},{96,64},{128,96},{160,128},{192,160},{224,192},{256... | collective-permute-start | bytes 417800 | tf_op jit(solution)/shard_map/ppermute | solution.py:427
  16.0 0.7 %collective-permute-start.2 = (bf16[136,512]{1,0:T(8,128)(2,1)S(1)}, bf16[136,512]{1,0:T(8,128)(2,1)S(1)}, u32[]{:S(2)}, u32[]{:S(2)}) collective-permute-start(bf16[136,512]{1,0:T(8,128)(2,1)S(1)} %shard_map.64.own_ref), channel_id=1, source_target_pairs={{192,224},{193,225},{194,226},{195,227},{196,228},{197,229},{198,2... | collective-permute-start | bytes 417800 | tf_op jit(solution)/shard_map/ppermute | solution.py:427
  16.6 0.0 copy-start
  16.7 1.0 %copy-done = bf16[1,32,64,128]{3,2,1,0:T(8,128)(2,1)S(1)} copy-done((bf16[1,32,64,128]{3,2,1,0:T(8,128)(2,1)S(1)}, bf16[1,32,64,128]{3,2,1,0:T(8,128)(2,1)}, u32[]{:S(2)}) %copy-start) | copy-done | bytes 524312
  17.7 0.4 %shard_map.66 = (f32[8,128,136]{2,1,0:T(8,128)S(1)}, f32[32,64,128]{2,1,0:T(8,128)S(1)}, bf16[32,64,128]{2,1,0:T(8,128)(2,1)S(1)}) custom-call(s32[1]{0:T(128)} %bitcast.odd_ref, bf16[136,512]{1,0:T(8,128)(2,1)S(1)} %shard_map.64.own_ref, bf16[32,64,128]{2,1,0:T(8,128)(2,1)S(1)} %bitcast.7), custom_call_target="tpu_custom_call" | custom-call | flops 1073741824 | bytes 1048576 | tf_op jit(solution)/shard_map/pallas_call | solution.py:372
  18.1 0.0 collective-permute-done.north_ref
  18.1 0.1 collective-permute-done.1.south_ref
  18.3 0.0 collective-permute-done.2.late_ref
  18.3 0.1 shard_map.65.column_ref
  18.4 4.6 %collective-permute-start.3 = (bf16[136,1024]{1,0:T(8,128)(2,1)S(1)}, bf16[136,1024]{1,0:T(8,128)(2,1)S(1)}, u32[]{:S(2)}, u32[]{:S(2)}) collective-permute-start(bf16[136,1024]{1,0:T(8,128)(2,1)S(1)} %shard_map.65.column_ref), channel_id=1, source_target_pairs={{1,2},{2,1},{3,4},{4,3},{5,6},{6,5},{7,8},{8,7},{9,10},{10,9},{11,... | collective-permute-start | bytes 835592 | tf_op jit(solution)/shard_map/ppermute | solution.py:436
  23.0 5.8 %collective-permute-start.4 = (bf16[136,1024]{1,0:T(8,128)(2,1)S(1)}, bf16[136,1024]{1,0:T(8,128)(2,1)S(1)}, u32[]{:S(2)}, u32[]{:S(2)}) collective-permute-start(bf16[136,1024]{1,0:T(8,128)(2,1)S(1)} %shard_map.65.column_ref), channel_id=1, source_target_pairs={{0,1},{1,0},{2,3},{3,2},{4,5},{5,4},{6,7},{7,6},{8,9},{9,8},{10,11... | collective-permute-start | bytes 835592 | tf_op jit(solution)/shard_map/ppermute | solution.py:436
  28.8 2.8 %shard_map.67 = (f32[8,128,136]{2,1,0:T(8,128)S(1)}, f32[4,128,128]{2,1,0:T(8,128)S(1)}, f32[4,128,128]{2,1,0:T(8,128)S(1)}) custom-call(s32[1]{0:T(128)} %bitcast.odd_ref, bf16[136,1024]{1,0:T(8,128)(2,1)S(1)} %shard_map.65.column_ref, f32[8,128,136]{2,1,0:T(8,128)S(1)} %get-tuple-element.11.part_ref), custom_call_target="tpu_custom_call" | custom-call | flops 4294967296 | bytes 1048576 | tf_op jit(solution)/shard_map/pallas_call | solution.py:388
  31.6 0.0 collective-permute-done.3.far_ref
  31.6 0.0 collective-permute-done.4.near_ref
  31.6 5.9 %shard_map.68 = bf16[32,64,128]{2,1,0:T(8,128)(2,1)} custom-call(s32[1]{0:T(128)} %bitcast.odd_ref, bf16[136,1024]{1,0:T(8,128)(2,1)S(1)} %collective-permute-done.3.far_ref, bf16[136,1024]{1,0:T(8,128)(2,1)S(1)} %collective-permute-done.4.near_ref, f32[8,128,136]{2,1,0:T(8,128)S(1)} %get-tuple-element.12.gram_ref, ...), custom_call_target="tpu_custom_call" | custom-call | tf_op jit(solution)/shard_map/pallas_call | solution.py:405
Async XLA Ops:
  1.7 16.4 %collective-permute-start = (bf16[136,512]{1,0:T(8,128)(2,1)S(1)}, bf16[136,512]{1,0:T(8,128)(2,1)S(1)}, u32[]{:S(2)}, u32[]{:S(2)}) collective-permute-start(bf16[136,512]{1,0:T(8,128)(2,1)S(1)} %shard_map.64.own_ref), channel_id=1, source_target_pairs={{0,32},{32,64},{64,96},{96,128},{128,160},{160,192},{224,256},{256... | collective-permute-start | bytes 417800 | tf_op jit(solution)/shard_map/ppermute | solution.py:427
  5.7 12.5 %collective-permute-start.1 = (bf16[136,512]{1,0:T(8,128)(2,1)S(1)}, bf16[136,512]{1,0:T(8,128)(2,1)S(1)}, u32[]{:S(2)}, u32[]{:S(2)}) collective-permute-start(bf16[136,512]{1,0:T(8,128)(2,1)S(1)} %shard_map.64.own_ref), channel_id=1, source_target_pairs={{32,0},{64,32},{96,64},{128,96},{160,128},{192,160},{224,192},{256... | collective-permute-start | bytes 417800 | tf_op jit(solution)/shard_map/ppermute | solution.py:427
  16.0 2.3 %collective-permute-start.2 = (bf16[136,512]{1,0:T(8,128)(2,1)S(1)}, bf16[136,512]{1,0:T(8,128)(2,1)S(1)}, u32[]{:S(2)}, u32[]{:S(2)}) collective-permute-start(bf16[136,512]{1,0:T(8,128)(2,1)S(1)} %shard_map.64.own_ref), channel_id=1, source_target_pairs={{192,224},{193,225},{194,226},{195,227},{196,228},{197,229},{198,2... | collective-permute-start | bytes 417800 | tf_op jit(solution)/shard_map/ppermute | solution.py:427
  16.6 1.0 %copy-start = (bf16[1,32,64,128]{3,2,1,0:T(8,128)(2,1)S(1)}, bf16[1,32,64,128]{3,2,1,0:T(8,128)(2,1)}, u32[]{:S(2)}) copy-start(bf16[1,32,64,128]{3,2,1,0:T(8,128)(2,1)} %param.6) | copy-start | bytes 1572868
  18.4 13.2 %collective-permute-start.3 = (bf16[136,1024]{1,0:T(8,128)(2,1)S(1)}, bf16[136,1024]{1,0:T(8,128)(2,1)S(1)}, u32[]{:S(2)}, u32[]{:S(2)}) collective-permute-start(bf16[136,1024]{1,0:T(8,128)(2,1)S(1)} %shard_map.65.column_ref), channel_id=1, source_target_pairs={{1,2},{2,1},{3,4},{4,3},{5,6},{6,5},{7,8},{8,7},{9,10},{10,9},{11,... | collective-permute-start | bytes 835592 | tf_op jit(solution)/shard_map/ppermute | solution.py:436
  23.0 8.7 %collective-permute-start.4 = (bf16[136,1024]{1,0:T(8,128)(2,1)S(1)}, bf16[136,1024]{1,0:T(8,128)(2,1)S(1)}, u32[]{:S(2)}, u32[]{:S(2)}) collective-permute-start(bf16[136,1024]{1,0:T(8,128)(2,1)S(1)} %shard_map.65.column_ref), channel_id=1, source_target_pairs={{0,1},{1,0},{2,3},{3,2},{4,5},{5,4},{6,7},{7,6},{8,9},{9,8},{10,11... | collective-permute-start | bytes 835592 | tf_op jit(solution)/shard_map/ppermute | solution.py:436

commit v10 on v9

--- a/solution.py
+++ b/solution.py
@@ -13,7 +13,7 @@
 RAD = 24
 EXTRA = 8
 WEIGHT, ROW, COL = 2, 5, 6
-EARLY_STEPS = 6
+EARLY_STEPS = 4
 INNER = (1, 2)
 BLOCKS = 4
 F32, BF16 = jnp.float32, jnp.bfloat16

time: 37.7 us -> 37.7 us (level)
  Pallas kernels: 10.3 us -> 9.9 us
    pallas_call x1, Pallas kernels: 2.8 us -> 2.17 us  [middle(): pl.pallas_call(functools.partial(mid_kernel, tile=tile), out_shape=(pltpu...]
  transfers between devices with their start and end apart: 5 -> 5, of which waited for: 1 -> 1; matrix products, arithmetic and copies ran while one was open for 0% -> 0% of each run, Pallas kernels for 9% -> 7%
where the time goes in v10:
time: 37.7 us; the launch traced here: 37.1 us
  starting transfers between devices  25.3 us (67%)
  Pallas kernels  9.9 us (26%)
  local copies, waits for them, and re-layouts  1.04 us (3%)
  between operations  0.75 us (2%)
    ppermute x3, starting transfers between devices, shifts(): lax.ppermute(x, 'lat', pairs)  14.9 us
    ppermute x2, starting transfers between devices, exchange(): return lax.ppermute(x, axis, pairs)  10.4 us
    pallas_call x1, Pallas kernels, edges(): pl.pallas_call(edge_kernel, out_shape=jax.ShapeDtypeStruct(mean.shape, BF...  6.11 us
    pallas_call x1, Pallas kernels, middle(): pl.pallas_call(functools.partial(mid_kernel, tile=tile), out_shape=(pltpu...  2.17 us
    pallas_call x1, Pallas kernels, pack(): pl.pallas_call(functools.partial(pack_kernel, tile_cols=tile_cols), out_s...  1.08 us
    unnamed x2, local copies, waits for them, and re-layouts  1.04 us
  transfers between devices with their start and end apart: 5, of which 1 were waited for; matrix products, arithmetic and copies ran while one was open for 0% of the time, Pallas kernels for 7%

profile of v10, /device:TPU:57, one launch (start us, length us, event | category | flops | bytes accessed | tf_op | source)
XLA Modules:
  0.0 37.1 jit_solution(6338380440133164922)
XLA Ops:
  0.7 1.1 %shard_map.64.own_ref = bf16[136,512]{1,0:T(8,128)(2,1)S(1)} custom-call(s32[1,1]{1,0:T(1,128)S(6)} %copy.7.count_ref, bf16[512,128]{1,0:T(8,128)(2,1)} %bitcast.8, f32[1,512]{1,0:T(1,128)} %bitcast.9, f32[1,512]{1,0:T(1,128)} %bitcast.10, s32[1,512]{1,0:T(1,128)} %bitcast.11), custom_call_target="tpu_custom_call" | custom-call | tf_op jit(solution)/shard_map/pallas_call | solution.py:327
  1.7 4.0 %collective-permute-start = (bf16[136,512]{1,0:T(8,128)(2,1)S(1)}, bf16[136,512]{1,0:T(8,128)(2,1)S(1)}, u32[]{:S(2)}, u32[]{:S(2)}) collective-permute-start(bf16[136,512]{1,0:T(8,128)(2,1)S(1)} %shard_map.64.own_ref), channel_id=1, source_target_pairs={{0,32},{32,64},{64,96},{96,128},{128,160},{160,192},{224,256},{256... | collective-permute-start | bytes 417800 | tf_op jit(solution)/shard_map/ppermute | solution.py:427
  5.7 10.2 %collective-permute-start.1 = (bf16[136,512]{1,0:T(8,128)(2,1)S(1)}, bf16[136,512]{1,0:T(8,128)(2,1)S(1)}, u32[]{:S(2)}, u32[]{:S(2)}) collective-permute-start(bf16[136,512]{1,0:T(8,128)(2,1)S(1)} %shard_map.64.own_ref), channel_id=1, source_target_pairs={{32,0},{64,32},{96,64},{128,96},{160,128},{192,160},{224,192},{256... | collective-permute-start | bytes 417800 | tf_op jit(solution)/shard_map/ppermute | solution.py:427
  16.0 0.7 %collective-permute-start.2 = (bf16[136,512]{1,0:T(8,128)(2,1)S(1)}, bf16[136,512]{1,0:T(8,128)(2,1)S(1)}, u32[]{:S(2)}, u32[]{:S(2)}) collective-permute-start(bf16[136,512]{1,0:T(8,128)(2,1)S(1)} %shard_map.64.own_ref), channel_id=1, source_target_pairs={{192,224},{193,225},{194,226},{195,227},{196,228},{197,229},{198,2... | collective-permute-start | bytes 417800 | tf_op jit(solution)/shard_map/ppermute | solution.py:427
  16.6 0.0 copy-start
  16.7 1.0 %copy-done = bf16[1,32,64,128]{3,2,1,0:T(8,128)(2,1)S(1)} copy-done((bf16[1,32,64,128]{3,2,1,0:T(8,128)(2,1)S(1)}, bf16[1,32,64,128]{3,2,1,0:T(8,128)(2,1)}, u32[]{:S(2)}) %copy-start) | copy-done | bytes 524312
  17.7 0.4 %shard_map.66 = (f32[8,128,136]{2,1,0:T(8,128)S(1)}, f32[32,64,128]{2,1,0:T(8,128)S(1)}, bf16[32,64,128]{2,1,0:T(8,128)(2,1)S(1)}) custom-call(s32[1]{0:T(128)} %bitcast.odd_ref, bf16[136,512]{1,0:T(8,128)(2,1)S(1)} %shard_map.64.own_ref, bf16[32,64,128]{2,1,0:T(8,128)(2,1)S(1)} %bitcast.7), custom_call_target="tpu_custom_call" | custom-call | flops 1073741824 | bytes 1048576 | tf_op jit(solution)/shard_map/pallas_call | solution.py:372
  18.1 0.0 collective-permute-done.north_ref
  18.1 0.1 collective-permute-done.1.south_ref
  18.3 0.0 collective-permute-done.2.late_ref
  18.3 0.1 shard_map.65.column_ref
  18.4 4.6 %collective-permute-start.3 = (bf16[136,1024]{1,0:T(8,128)(2,1)S(1)}, bf16[136,1024]{1,0:T(8,128)(2,1)S(1)}, u32[]{:S(2)}, u32[]{:S(2)}) collective-permute-start(bf16[136,1024]{1,0:T(8,128)(2,1)S(1)} %shard_map.65.column_ref), channel_id=1, source_target_pairs={{1,2},{2,1},{3,4},{4,3},{5,6},{6,5},{7,8},{8,7},{9,10},{10,9},{11,... | collective-permute-start | bytes 835592 | tf_op jit(solution)/shard_map/ppermute | solution.py:436
  23.0 5.8 %collective-permute-start.4 = (bf16[136,1024]{1,0:T(8,128)(2,1)S(1)}, bf16[136,1024]{1,0:T(8,128)(2,1)S(1)}, u32[]{:S(2)}, u32[]{:S(2)}) collective-permute-start(bf16[136,1024]{1,0:T(8,128)(2,1)S(1)} %shard_map.65.column_ref), channel_id=1, source_target_pairs={{0,1},{1,0},{2,3},{3,2},{4,5},{5,4},{6,7},{7,6},{8,9},{9,8},{10,11... | collective-permute-start | bytes 835592 | tf_op jit(solution)/shard_map/ppermute | solution.py:436
  28.8 2.2 %shard_map.67 = (f32[8,128,136]{2,1,0:T(8,128)S(1)}, f32[4,128,128]{2,1,0:T(8,128)S(1)}, f32[4,128,128]{2,1,0:T(8,128)S(1)}) custom-call(s32[1]{0:T(128)} %bitcast.odd_ref, bf16[136,1024]{1,0:T(8,128)(2,1)S(1)} %shard_map.65.column_ref, f32[8,128,136]{2,1,0:T(8,128)S(1)} %get-tuple-element.11.part_ref), custom_call_target="tpu_custom_call" | custom-call | flops 4294967296 | bytes 1048576 | tf_op jit(solution)/shard_map/pallas_call | solution.py:388
  31.0 0.0 collective-permute-done.3.far_ref
  31.0 0.0 collective-permute-done.4.near_ref
  31.0 6.1 %shard_map.68 = bf16[32,64,128]{2,1,0:T(8,128)(2,1)} custom-call(s32[1]{0:T(128)} %bitcast.odd_ref, bf16[136,1024]{1,0:T(8,128)(2,1)S(1)} %collective-permute-done.3.far_ref, bf16[136,1024]{1,0:T(8,128)(2,1)S(1)} %collective-permute-done.4.near_ref, f32[8,128,136]{2,1,0:T(8,128)S(1)} %get-tuple-element.12.gram_ref, ...), custom_call_target="tpu_custom_call" | custom-call | tf_op jit(solution)/shard_map/pallas_call | solution.py:405
Async XLA Ops:
  1.7 16.4 %collective-permute-start = (bf16[136,512]{1,0:T(8,128)(2,1)S(1)}, bf16[136,512]{1,0:T(8,128)(2,1)S(1)}, u32[]{:S(2)}, u32[]{:S(2)}) collective-permute-start(bf16[136,512]{1,0:T(8,128)(2,1)S(1)} %shard_map.64.own_ref), channel_id=1, source_target_pairs={{0,32},{32,64},{64,96},{96,128},{128,160},{160,192},{224,256},{256... | collective-permute-start | bytes 417800 | tf_op jit(solution)/shard_map/ppermute | solution.py:427
  5.7 12.5 %collective-permute-start.1 = (bf16[136,512]{1,0:T(8,128)(2,1)S(1)}, bf16[136,512]{1,0:T(8,128)(2,1)S(1)}, u32[]{:S(2)}, u32[]{:S(2)}) collective-permute-start(bf16[136,512]{1,0:T(8,128)(2,1)S(1)} %shard_map.64.own_ref), channel_id=1, source_target_pairs={{32,0},{64,32},{96,64},{128,96},{160,128},{192,160},{224,192},{256... | collective-permute-start | bytes 417800 | tf_op jit(solution)/shard_map/ppermute | solution.py:427
  16.0 2.3 %collective-permute-start.2 = (bf16[136,512]{1,0:T(8,128)(2,1)S(1)}, bf16[136,512]{1,0:T(8,128)(2,1)S(1)}, u32[]{:S(2)}, u32[]{:S(2)}) collective-permute-start(bf16[136,512]{1,0:T(8,128)(2,1)S(1)} %shard_map.64.own_ref), channel_id=1, source_target_pairs={{192,224},{193,225},{194,226},{195,227},{196,228},{197,229},{198,2... | collective-permute-start | bytes 417800 | tf_op jit(solution)/shard_map/ppermute | solution.py:427
  16.6 1.0 %copy-start = (bf16[1,32,64,128]{3,2,1,0:T(8,128)(2,1)S(1)}, bf16[1,32,64,128]{3,2,1,0:T(8,128)(2,1)}, u32[]{:S(2)}) copy-start(bf16[1,32,64,128]{3,2,1,0:T(8,128)(2,1)} %param.6) | copy-start | bytes 1572868
  18.4 12.6 %collective-permute-start.3 = (bf16[136,1024]{1,0:T(8,128)(2,1)S(1)}, bf16[136,1024]{1,0:T(8,128)(2,1)S(1)}, u32[]{:S(2)}, u32[]{:S(2)}) collective-permute-start(bf16[136,1024]{1,0:T(8,128)(2,1)S(1)} %shard_map.65.column_ref), channel_id=1, source_target_pairs={{1,2},{2,1},{3,4},{4,3},{5,6},{6,5},{7,8},{8,7},{9,10},{10,9},{11,... | collective-permute-start | bytes 835592 | tf_op jit(solution)/shard_map/ppermute | solution.py:436
  23.0 8.0 %collective-permute-start.4 = (bf16[136,1024]{1,0:T(8,128)(2,1)S(1)}, bf16[136,1024]{1,0:T(8,128)(2,1)S(1)}, u32[]{:S(2)}, u32[]{:S(2)}) collective-permute-start(bf16[136,1024]{1,0:T(8,128)(2,1)S(1)} %shard_map.65.column_ref), channel_id=1, source_target_pairs={{0,1},{1,0},{2,3},{3,2},{4,5},{5,4},{6,7},{7,6},{8,9},{9,8},{10,11... | collective-permute-start | bytes 835592 | tf_op jit(solution)/shard_map/ppermute | solution.py:436
